TPU v7x, 256 devices: a whole 4x4x8 slice. The times are simulated.
256 devices in a mesh: row: 8 (over z_hi, core), col: 32 (over x, y, z_lo).
Axes of the slice: x: 4, y: 4, z: 8 (z_hi: 4, z_lo: 2; z = z_hi * 2 + z_lo), core: 2. Of those that a mesh axis runs over, the one named last changes fastest.
Arguments:
- features: bfloat16 [32768, 128], P(('row', 'col')), may hold values from -6 to 6
- weight: bfloat16 [128, 512], replicated, may hold values from -0.5 to 0.5
- bias: float32 [512], replicated, may hold values from -4 to 4
- tile_values: bfloat16 [8, 32, 128, 128, 128], P('row', 'col'), may hold values from 0 to 0.019897461
- tile_index: int32 [8, 32, 128], P('row', 'col'), may hold values from 0 to 255, as said below
- tile_count: int32 [8, 32], P('row', 'col'), may hold values from 16 to 128, as said below
- cotangent: bfloat16 [32768, 512], P(('col', 'row')), may hold values from -20 to 20
Outputs:
- hidden_out: bfloat16 [32768, 512], P(('col', 'row'))
- grad_features: bfloat16 [32768, 128], P(('row', 'col'))
- grad_weight: float32 [128, 512], replicated
- grad_bias: float32 [512], replicated
Inputs may be any that keep to these rules, and one draw needn't show every extreme that they name: `tile_index`: within a cell the slots name distinct tiles; slots at or beyond the cell's count hold arbitrary tiles and values. `tile_count`: counts differ from cell to cell; some cell holds exactly 128 live slots.
All inputs are finite; a program needn't handle non-finite values.
Results may differ from a plain program's by a relative error of at most 0.0065.
Values may be sent and summed in bfloat16 or wider, within the bound.
No kernel may reach another device: no remote copies, remote signals or barrier semaphores. Data moves between devices by JAX's collectives and lax.ppermute only.
A program may use at most 128 MiB of HBM per device.

v0:
```python
import jax
import jax.numpy as jnp
from jax import lax
from jax.experimental import pallas as pl
from jax.experimental.pallas import tpu as pltpu
from jax.sharding import PartitionSpec as P

BF, F32 = jnp.bfloat16, jnp.float32
VMEM = pltpu.VMEM


def ring(count, inner, size, step):
    pairs = []
    for i in range(size):
        digit = (i // inner) % count
        pairs.append((i, i + (((digit + step) % count) - digit) * inner))
    return pairs


def mirror(count, inner, size, mask):
    pairs = []
    for i in range(size):
        digit = (i // inner) % count
        pairs.append((i, i + ((digit ^ mask) - digit) * inner))
    return pairs


def move_x(v, step):
    return lax.ppermute(v, "col", ring(4, 8, 32, step))


def move_y(v, step):
    return lax.ppermute(v, "col", ring(4, 2, 32, step))


def move_h(v, step):
    return lax.ppermute(v, "row", ring(4, 2, 8, step))


def swap_x(v, mask):
    return lax.ppermute(v, "col", mirror(4, 8, 32, mask))


def swap_y(v, mask):
    return lax.ppermute(v, "col", mirror(4, 2, 32, mask))


def swap_z(v):
    return lax.ppermute(v, "col", mirror(2, 1, 32, 1))


def swap_k(v):
    return lax.ppermute(v, "row", mirror(2, 1, 8, 1))


def pair(v):
    high = v.astype(BF)
    return jnp.concatenate([high, (v - high.astype(F32)).astype(BF)])


def unpair(v):
    rows = v.shape[0] // 2
    return v[:rows].astype(F32) + v[rows:].astype(F32)


def spread_kernel(count_ref, put_row, put_col, tiles_ref, dense_ref, sems):
    size = tiles_ref.shape[1]
    dense_ref[...] = jnp.zeros_like(dense_ref)

    def copy(slot):
        rows = pl.ds(pl.multiple_of(put_row[slot] * size, size), size)
        cols = pl.ds(pl.multiple_of(put_col[slot] * size, size), size)
        return pltpu.make_async_copy(tiles_ref.at[slot], dense_ref.at[rows, cols], sems.at[slot])

    def begin(slot, carry):
        copy(slot).start()
        return carry

    def end(slot, carry):
        copy(slot).wait()
        return carry

    lax.fori_loop(0, count_ref[0], begin, 0)
    lax.fori_loop(0, count_ref[0], end, 0)


def spread(tiles, count, put_row, put_col, rows, cols):
    slots, size, _ = tiles.shape
    smem = pl.BlockSpec(memory_space=pltpu.SMEM)
    return pl.pallas_call(
        spread_kernel,
        out_shape=jax.ShapeDtypeStruct((rows * size, cols * size), BF),
        in_specs=[smem, smem, smem, pl.BlockSpec(memory_space=pl.ANY)],
        out_specs=pl.BlockSpec(memory_space=VMEM),
        scratch_shapes=[pltpu.SemaphoreType.DMA((slots,))],
        compiler_params=pltpu.CompilerParams(vmem_limit_bytes=32 * 2**20),
        cost_estimate=pl.CostEstimate(
            flops=0, bytes_accessed=2 * size * size * (slots + rows * cols), transcendentals=0
        ),
        name="spread",
    )(count, put_row, put_col, tiles)


def middle_kernel(place, own, in1, in2, in3, weight, bias, cot, hidden_ref, sent_ref, gw_ref, whole):
    agg = own[...] + in1[...].astype(F32) + in2[...].astype(F32) + in3[...].astype(F32)
    high = agg.astype(BF)
    low = (agg - high.astype(F32)).astype(BF)
    w = weight[...]
    pre = (
        jnp.dot(high, w, preferred_element_type=F32)
        + jnp.dot(low, w, preferred_element_type=F32)
        + bias[...]
    )
    sig = jax.nn.sigmoid(pre)
    hidden_ref[...] = (pre * sig).astype(BF)
    dpre = (cot[...].astype(F32) * (sig + pre * sig * (1.0 - sig))).astype(BF)
    back = lax.dot_general(
        dpre, w, (((1,), (1,)), ((), ())), preferred_element_type=F32
    ).astype(BF)
    over_nodes = (((0,), (0,)), ((), ()))
    whole[...] = lax.dot_general(
        high, dpre, over_nodes, preferred_element_type=F32
    ) + lax.dot_general(low, dpre, over_nodes, preferred_element_type=F32)
    sums = jnp.sum(dpre.astype(F32), axis=0, keepdims=True)
    size, lanes = back.shape
    blocks = cot.shape[1] // lanes
    rows = whole.shape[0] // 8
    tail = jnp.concatenate(
        [sums[:, j * lanes : (j + 1) * lanes] for j in range(blocks)]
        + [jnp.zeros((rows - blocks, lanes), F32)]
    )
    for h in range(4):
        sent_ref[h, :size, :] = back
        for k in range(2):
            at = (lax.rem(place[0] + h, 4) * 2 + lax.rem(place[1] + k, 2)) * rows
            for j in range(blocks + 1):
                if j < blocks:
                    piece = whole[pl.ds(pl.multiple_of(at, rows), rows), j * lanes : (j + 1) * lanes]
                else:
                    piece = tail
                to = (k * (blocks + 1) + j) * rows
                sent_ref[h, size + to : size + to + rows, :] = piece.astype(BF)
                if h == 0:
                    gw_ref[to : to + rows, :] = piece


def middle(place, own, arrived, weight, bias, cotangent):
    size, width = cotangent.shape
    feats = weight.shape[0]
    share = 2 * (feats // 8) * (width // feats + 1)
    vmem = pl.BlockSpec(memory_space=VMEM)
    return pl.pallas_call(
        middle_kernel,
        out_shape=(
            jax.ShapeDtypeStruct((size, width), BF),
            jax.ShapeDtypeStruct((4, size + share, feats), BF),
            jax.ShapeDtypeStruct((share, feats), F32),
        ),
        in_specs=[pl.BlockSpec(memory_space=pltpu.SMEM)] + [vmem] * 7,
        out_specs=(vmem, vmem, vmem),
        scratch_shapes=[VMEM((feats, width), F32)],
        compiler_params=pltpu.CompilerParams(vmem_limit_bytes=16 * 2**20),
        cost_estimate=pl.CostEstimate(
            flops=10 * size * feats * width, bytes_accessed=10 * size * width, transcendentals=size * width
        ),
        name="middle",
    )(place, own, *arrived, weight, bias[None, :], cotangent)


def settle_kernel(place, near, far, out_ref, bias_ref):
    lanes = near.shape[1]
    blocks = out_ref.shape[1] // lanes
    rows = near.shape[0] // 4 // (blocks + 1)
    for k in range(2):
        part = far if k else near
        for h in range(4):
            at = (lax.rem(place[0] - h + 4, 4) * 2 + lax.rem(place[1] + k, 2)) * rows
            for j in range(blocks):
                first = (h * (blocks + 1) + j) * rows
                out_ref[pl.ds(pl.multiple_of(at, rows), rows), j * lanes : (j + 1) * lanes] = part[
                    first : first + rows, :
                ]
    for j in range(blocks):
        bias_ref[:, j * lanes : (j + 1) * lanes] = near[blocks * rows + j : blocks * rows + j + 1, :]


def settle(place, near, far, feats, width):
    vmem = pl.BlockSpec(memory_space=VMEM)
    return pl.pallas_call(
        settle_kernel,
        out_shape=(
            jax.ShapeDtypeStruct((feats, width), F32),
            jax.ShapeDtypeStruct((1, width), F32),
        ),
        in_specs=[pl.BlockSpec(memory_space=pltpu.SMEM), vmem, vmem],
        out_specs=(vmem, vmem),
        name="settle",
    )(place, near, far)


def local(features, weight, bias, tile_values, tile_index, tile_count, cotangent):
    size = features.shape[0]
    feats, width = weight.shape
    places = tile_index[0, 0]
    row, col = lax.axis_index("row"), lax.axis_index("col")
    h, k = row // 2, row % 2
    x, y, z = col // 8, (col // 2) % 4, col % 2
    here = jnp.stack([h, k]).astype(jnp.int32)

    tile_row, tile_col = places // 32, places % 32
    from_x, from_y = tile_col // 8, (tile_col // 2) % 4
    far_h, far_k = (h - tile_row // 2) % 4, (k - tile_row) % 2
    bits_x, bits_y = x ^ from_x, y ^ from_y
    put_row = (far_k * 4 + far_h).astype(jnp.int32)
    put_col = jnp.where(
        (z - tile_col) % 2 == 0,
        ((x - from_x) % 4) * 4 + (bits_y ^ (bits_y >> 1)),
        16 + ((y - from_y) % 4) * 4 + (bits_x ^ (bits_x >> 1)),
    ).astype(jnp.int32)
    dense = spread(tile_values[0, 0], tile_count[0], put_row, put_col, 8, 32)

    near, other = features, swap_z(features)
    near = jnp.concatenate([near, swap_y(near, 1)])
    other = jnp.concatenate([other, swap_x(other, 1)])
    near = jnp.concatenate([near, swap_y(near, 3)])
    other = jnp.concatenate([other, swap_x(other, 3)])
    near = [near] + [move_x(near, s) for s in (1, 2, 3)]
    other = [other] + [move_y(other, s) for s in (1, 2, 3)]
    source = jnp.concatenate(near + other)

    part = jnp.dot(dense, source, preferred_element_type=F32).reshape(2, 4, size, feats)
    half = part[0] + swap_k(part[1].astype(BF)).astype(F32)
    sent = half.astype(BF)
    arrived = [move_h(sent[s], -s) for s in (1, 2, 3)]
    hidden_out, sent, gw = middle(here, half[0], arrived, weight, bias, cotangent)

    arrived = [move_h(sent[s], s) for s in (1, 2, 3)]
    target = jnp.concatenate([sent[0][:size]] + [v[:size] for v in arrived])
    gw = gw + sum(v[size:].astype(F32) for v in arrived)
    share = gw.shape[0] // 2
    arrived = swap_k(jnp.concatenate([target, pair(gw[share:])]))
    gw = pair(gw[:share] + unpair(arrived[4 * size :]))
    target = jnp.concatenate([target, arrived[: 4 * size]])
    grad = lax.dot_general(dense, target, (((0,), (0,)), ((), ())), preferred_element_type=F32)
    grad = grad.reshape(2, 4, 4 * size, feats)
    near, other = grad[0], grad[1]

    rows = 4 * size
    arrived = [move_x(jnp.concatenate([near[s].astype(BF), gw]), -s) for s in (1, 2, 3)]
    near = near[0] + sum(v[:rows].astype(F32) for v in arrived)
    one, two, three = [unpair(v[rows:]) for v in arrived]
    gw = pair((unpair(gw) + two) + (one + three))
    other = other[0] + sum(move_y(other[s].astype(BF), -s).astype(F32) for s in (1, 2, 3))
    for mask in (3, 1):
        rows = rows // 2
        arrived = swap_y(jnp.concatenate([near[rows:].astype(BF), gw]), mask)
        near = near[:rows] + arrived[:rows].astype(F32)
        gw = pair(unpair(gw) + unpair(arrived[rows:]))
        other = other[:rows] + swap_x(other[rows:].astype(BF), mask).astype(F32)
    arrived = swap_z(jnp.concatenate([other.astype(BF), gw]))
    grad_features = (near + arrived[:rows].astype(F32)).astype(BF)
    gw = unpair(gw) + unpair(arrived[rows:])

    gw = jnp.concatenate([gw] + [move_h(gw, s) for s in (1, 2, 3)])
    grad_weight, grad_bias = settle(here, gw, swap_k(gw), feats, width)
    return (hidden_out, grad_features, grad_weight, grad_bias.reshape(width))


def solution(mesh):
    in_specs = (
        P(("row", "col"), None),
        P(),
        P(),
        P("row", "col", None, None, None),
        P("row", "col", None),
        P("row", "col"),
        P(("col", "row"), None),
    )
    out_specs = (P(("col", "row"), None), P(("row", "col"), None), P(), P())
    return jax.shard_map(local, mesh=mesh, in_specs=in_specs, out_specs=out_specs, check_vma=False)
```

profile of v0, /device:TPU:1, one launch (start us, length us, event | category | flops | bytes accessed | tf_op | source)
XLA Modules:
  0.0 125.0 jit_solution(17266653369990487524)
XLA Ops:
  0.6 2.2 %collective-permute-start = (bf16[128,128]{1,0:T(8,128)(2,1)}, bf16[128,128]{1,0:T(8,128)(2,1)S(1)}, u32[]{:S(2)}, u32[]{:S(2)}) collective-permute-start(bf16[128,128]{1,0:T(8,128)(2,1)} %param.7), channel_id=1, source_target_pairs={{0,2},{1,3},{2,0},{3,1},{4,6},{5,7},{6,4},{7,5},{8,10},{9,11},{10,... | collective-permute-start | bytes 98312 | tf_op jit(solution)/shard_map/ppermute | solution.py:45
  2.8 1.6 %collective-permute-start.5 = (bf16[128,128]{1,0:T(8,128)(2,1)}, bf16[128,128]{1,0:T(8,128)(2,1)S(1)}, u32[]{:S(2)}, u32[]{:S(2)}) collective-permute-start(bf16[128,128]{1,0:T(8,128)(2,1)} %param.7), channel_id=1, source_target_pairs={{0,1},{1,0},{2,3},{3,2},{4,5},{5,4},{6,7},{7,6},{8,9},{9,8},{10,11... | collective-permute-start | bytes 98312 | tf_op jit(solution)/shard_map/ppermute | solution.py:49
  6.1 2.0 %collective-permute-start.1 = (bf16[256,128]{1,0:T(8,128)(2,1)S(1)}, bf16[256,128]{1,0:T(8,128)(2,1)S(1)}, u32[]{:S(2)}, u32[]{:S(2)}) collective-permute-start(bf16[256,128]{1,0:T(8,128)(2,1)S(1)} %pad_maximum_fusion.10), channel_id=1, source_target_pairs={{0,6},{1,7},{2,4},{3,5},{4,2},{5,3},{6,0},{7,1},{8,14},{9,15},{10,... | collective-permute-start | bytes 196616 | tf_op jit(solution)/shard_map/ppermute | solution.py:45
  11.7 2.5 %collective-permute-start.3 = (bf16[512,128]{1,0:T(8,128)(2,1)S(1)}, bf16[512,128]{1,0:T(8,128)(2,1)S(1)}, u32[]{:S(2)}, u32[]{:S(2)}) collective-permute-start(bf16[512,128]{1,0:T(8,128)(2,1)S(1)} %get-tuple-element.48), channel_id=1, source_target_pairs={{0,16},{1,17},{2,18},{3,19},{4,20},{5,21},{6,22},{7,23},{8,24},{9,... | collective-permute-start | bytes 393224 | tf_op jit(solution)/shard_map/ppermute | solution.py:29
  19.7 2.7 %collective-permute-start.9 = (bf16[512,128]{1,0:T(8,128)(2,1)S(1)}, bf16[512,128]{1,0:T(8,128)(2,1)S(1)}, u32[]{:S(2)}, u32[]{:S(2)}) collective-permute-start(bf16[512,128]{1,0:T(8,128)(2,1)S(1)} %get-tuple-element.46), channel_id=1, source_target_pairs={{0,4},{1,5},{2,6},{3,7},{4,0},{5,1},{6,2},{7,3},{8,12},{9,13},{10,... | collective-permute-start | bytes 393224 | tf_op jit(solution)/shard_map/ppermute | solution.py:33
  24.5 2.2 %copy-done = bf16[1,1,128,128,128]{4,3,2,1,0:T(8,128)(2,1)S(1)} copy-done((bf16[1,1,128,128,128]{4,3,2,1,0:T(8,128)(2,1)S(1)}, bf16[1,1,128,128,128]{4,3,2,1,0:T(8,128)(2,1)}, u32[]{:S(2)}) %copy-start) | copy-done | bytes 4194328
  26.6 3.5 %spread.1 = bf16[1024,4096]{1,0:T(8,128)(2,1)S(1)} custom-call(s32[1]{0:T(128)} %bitcast.46.count_ref, s32[128]{0:T(128)S(1)} %get-tuple-element.62.put_row, s32[128]{0:T(128)S(1)} %get-tuple-element.61.put_col, bf16[128,128,128]{2,1,0:T(8,128)(2,1)S(1)} %bitcast.47), custom_call_target="tpu_custom_call" | custom-call | bytes 12582912 | tf_op jit(solution)/shard_map/spread/pallas_call | solution.py:90
  30.2 2.0 %collective-permute-start.10 = (bf16[512,128]{1,0:T(8,128)(2,1)S(1)}, bf16[512,128]{1,0:T(8,128)(2,1)S(1)}, u32[]{:S(2)}, u32[]{:S(2)}) collective-permute-start(bf16[512,128]{1,0:T(8,128)(2,1)S(1)} %get-tuple-element.46), channel_id=1, source_target_pairs={{0,6},{1,7},{2,0},{3,1},{4,2},{5,3},{6,4},{7,5},{8,14},{9,15},{10,... | collective-permute-start | bytes 393224 | tf_op jit(solution)/shard_map/ppermute | solution.py:33
  32.3 1.9 %collective-permute-done.10 = bf16[512,128]{1,0:T(8,128)(2,1)S(1)} collective-permute-done((bf16[512,128]{1,0:T(8,128)(2,1)S(1)}, bf16[512,128]{1,0:T(8,128)(2,1)S(1)}, u32[]{:S(2)}, u32[]{:S(2)}) %collective-permute-start.10) | collective-permute-done | bytes 131104 | tf_op jit(solution)/shard_map/ppermute | solution.py:33
  34.2 2.3 %fusion.34 = f32[1024,128]{1,0:T(8,128)S(1)} fusion(bf16[1024,4096]{1,0:T(8,128)(2,1)S(1)} %spread.1, bf16[4096,128]{1,0:T(8,128)(2,1)S(1)} %constant_dynamic-update-slice_fusion.6), kind=kOutput, calls=%fused_computation.142 | convolution fusion | flops 1073741824 | bytes 9961472 | tf_op jit(solution)/shard_map/dot_general | solution.py:231
  36.6 5.4 %collective-permute-start.11 = (bf16[4,128,128]{2,1,0:T(8,128)(2,1)S(1)}, bf16[4,128,128]{2,1,0:T(8,128)(2,1)S(1)}, u32[]{:S(2)}, u32[]{:S(2)}) collective-permute-start(bf16[4,128,128]{2,1,0:T(8,128)(2,1)S(1)} %bitcast.50), channel_id=1, source_target_pairs={{0,32},{32,0},{64,96},{96,64},{128,160},{160,128},{192,224},{224,1... | collective-permute-start | bytes 393224 | tf_op jit(solution)/shard_map/ppermute | solution.py:53
  43.0 2.8 %collective-permute-start.14 = (bf16[128,128]{1,0:T(8,128)(2,1)S(1)}, bf16[128,128]{1,0:T(8,128)(2,1)S(1)}, u32[]{:S(2)}, u32[]{:S(2)}) collective-permute-start(bf16[128,128]{1,0:T(8,128)(2,1)S(1)} %get-tuple-element.37), channel_id=1, source_target_pairs={{0,64},{32,96},{64,128},{96,160},{128,192},{160,224},{192,0},{224,... | collective-permute-start | bytes 98312 | tf_op jit(solution)/shard_map/ppermute | solution.py:37
  45.8 4.9 %collective-permute-start.13 = (bf16[128,128]{1,0:T(8,128)(2,1)S(1)}, bf16[128,128]{1,0:T(8,128)(2,1)S(1)}, u32[]{:S(2)}, u32[]{:S(2)}) collective-permute-start(bf16[128,128]{1,0:T(8,128)(2,1)S(1)} %get-tuple-element.38), channel_id=1, source_target_pairs={{0,128},{32,160},{64,192},{96,224},{128,0},{160,32},{192,64},{224,... | collective-permute-start | bytes 98312 | tf_op jit(solution)/shard_map/ppermute | solution.py:37
  50.6 3.4 %collective-permute-start.12 = (bf16[128,128]{1,0:T(8,128)(2,1)S(1)}, bf16[128,128]{1,0:T(8,128)(2,1)S(1)}, u32[]{:S(2)}, u32[]{:S(2)}) collective-permute-start(bf16[128,128]{1,0:T(8,128)(2,1)S(1)} %get-tuple-element.39), channel_id=1, source_target_pairs={{0,192},{32,224},{64,0},{96,32},{128,64},{160,96},{192,128},{224,1... | collective-permute-start | bytes 98312 | tf_op jit(solution)/shard_map/ppermute | solution.py:37
  56.6 2.4 %collective-permute-start.15 = (bf16[288,128]{1,0:T(8,128)(2,1)S(1)}, bf16[288,128]{1,0:T(8,128)(2,1)S(1)}, u32[]{:S(2)}, u32[]{:S(2)}) collective-permute-start(bf16[288,128]{1,0:T(8,128)(2,1)S(1)} %get-tuple-element.36), channel_id=1, source_target_pairs={{0,64},{32,96},{64,128},{96,160},{128,192},{160,224},{192,0},{224,... | collective-permute-start | bytes 221192 | tf_op jit(solution)/shard_map/ppermute | solution.py:37
  59.0 1.8 %collective-permute-start.17 = (bf16[288,128]{1,0:T(8,128)(2,1)S(1)}, bf16[288,128]{1,0:T(8,128)(2,1)S(1)}, u32[]{:S(2)}, u32[]{:S(2)}) collective-permute-start(bf16[288,128]{1,0:T(8,128)(2,1)S(1)} %get-tuple-element.34), channel_id=1, source_target_pairs={{0,192},{32,224},{64,0},{96,32},{128,64},{160,96},{192,128},{224,1... | collective-permute-start | bytes 221192 | tf_op jit(solution)/shard_map/ppermute | solution.py:37
  60.8 4.4 %collective-permute-start.16 = (bf16[288,128]{1,0:T(8,128)(2,1)S(1)}, bf16[288,128]{1,0:T(8,128)(2,1)S(1)}, u32[]{:S(2)}, u32[]{:S(2)}) collective-permute-start(bf16[288,128]{1,0:T(8,128)(2,1)S(1)} %get-tuple-element.35), channel_id=1, source_target_pairs={{0,128},{32,160},{64,192},{96,224},{128,0},{160,32},{192,64},{224,... | collective-permute-start | bytes 221192 | tf_op jit(solution)/shard_map/ppermute | solution.py:37
  65.2 2.9 %collective-permute-done.16 = bf16[288,128]{1,0:T(8,128)(2,1)S(1)} collective-permute-done((bf16[288,128]{1,0:T(8,128)(2,1)S(1)}, bf16[288,128]{1,0:T(8,128)(2,1)S(1)}, u32[]{:S(2)}, u32[]{:S(2)}) %collective-permute-start.16) | collective-permute-done | bytes 73760 | tf_op jit(solution)/shard_map/ppermute | solution.py:37
  68.1 3.5 %collective-permute-start.18 = (bf16[672,128]{1,0:T(8,128)(2,1)S(1)}, bf16[672,128]{1,0:T(8,128)(2,1)S(1)}, u32[]{:S(2)}, u32[]{:S(2)}) collective-permute-start(bf16[672,128]{1,0:T(8,128)(2,1)S(1)} %constant_dynamic-update-slice_fusion.18), channel_id=1, source_target_pairs={{0,32},{32,0},{64,96},{96,64},{128,160},{160,128},{192,224},{224,1... | collective-permute-start | bytes 516104 | tf_op jit(solution)/shard_map/ppermute | solution.py:53
  72.7 2.5 %fusion.33 = (bf16[4096,128]{1,0:T(8,128)(2,1)S(1)}, f32[4096,128]{1,0:T(8,128)S(1)}) fusion(bf16[1024,4096]{1,0:T(8,128)(2,1)S(1)} %spread.1, bf16[1024,128]{1,0:T(8,128)(2,1)S(1)} %slice_dynamic-update-slice_fusion), kind=kOutput, calls=%fused_computation.141 | convolution fusion | flops 1074266112 | bytes 11796480 | tf_op jit(solution)/shard_map/dot_general | solution.py:244
  75.2 2.4 %collective-permute-start.24 = (bf16[512,128]{1,0:T(8,128)(2,1)S(1)}, bf16[512,128]{1,0:T(8,128)(2,1)S(1)}, u32[]{:S(2)}, u32[]{:S(2)}) collective-permute-start(bf16[512,128]{1,0:T(8,128)(2,1)S(1)} %get-tuple-element.26), channel_id=1, source_target_pairs={{0,6},{1,7},{2,0},{3,1},{4,2},{5,3},{6,4},{7,5},{8,14},{9,15},{10,... | collective-permute-start | bytes 393224 | tf_op jit(solution)/shard_map/ppermute | solution.py:33
  77.7 3.8 %collective-permute-start.19 = (bf16[672,128]{1,0:T(8,128)(2,1)S(1)}, bf16[672,128]{1,0:T(8,128)(2,1)S(1)}, u32[]{:S(2)}, u32[]{:S(2)}) collective-permute-start(bf16[672,128]{1,0:T(8,128)(2,1)S(1)} %get-tuple-element.50), channel_id=1, source_target_pairs={{0,24},{1,25},{2,26},{3,27},{4,28},{5,29},{6,30},{7,31},{8,0},{9,1... | collective-permute-start | bytes 516104 | tf_op jit(solution)/shard_map/ppermute | solution.py:29
  83.3 7.3 %collective-permute-done.26 = bf16[512,128]{1,0:T(8,128)(2,1)S(1)} collective-permute-done((bf16[512,128]{1,0:T(8,128)(2,1)S(1)}, bf16[512,128]{1,0:T(8,128)(2,1)S(1)}, u32[]{:S(2)}, u32[]{:S(2)}) %collective-permute-start.26) | collective-permute-done | bytes 131104 | tf_op jit(solution)/shard_map/ppermute | solution.py:33
  90.7 1.6 %collective-permute-done.21 = bf16[672,128]{1,0:T(8,128)(2,1)S(1)} collective-permute-done((bf16[672,128]{1,0:T(8,128)(2,1)S(1)}, bf16[672,128]{1,0:T(8,128)(2,1)S(1)}, u32[]{:S(2)}, u32[]{:S(2)}) %collective-permute-start.21) | collective-permute-done | bytes 172064 | tf_op jit(solution)/shard_map/ppermute | solution.py:29
  93.1 3.8 %collective-permute-done.27 = bf16[256,128]{1,0:T(8,128)(2,1)S(1)} collective-permute-done((bf16[256,128]{1,0:T(8,128)(2,1)S(1)}, bf16[256,128]{1,0:T(8,128)(2,1)S(1)}, u32[]{:S(2)}, u32[]{:S(2)}) %collective-permute-start.27) | collective-permute-done | bytes 65568 | tf_op jit(solution)/shard_map/ppermute | solution.py:41
  100.1 1.6 %collective-permute-done.23 = bf16[288,128]{1,0:T(8,128)(2,1)S(1)} collective-permute-done((bf16[288,128]{1,0:T(8,128)(2,1)S(1)}, bf16[288,128]{1,0:T(8,128)(2,1)S(1)}, u32[]{:S(2)}, u32[]{:S(2)}) %collective-permute-start.23) | collective-permute-done | bytes 73760 | tf_op jit(solution)/shard_map/ppermute | solution.py:45
  102.8 2.3 %collective-permute-done.29 = bf16[288,128]{1,0:T(8,128)(2,1)S(1)} collective-permute-done((bf16[288,128]{1,0:T(8,128)(2,1)S(1)}, bf16[288,128]{1,0:T(8,128)(2,1)S(1)}, u32[]{:S(2)}, u32[]{:S(2)}) %collective-permute-start.29) | collective-permute-done | bytes 73760 | tf_op jit(solution)/shard_map/ppermute | solution.py:49
  105.1 3.3 %collective-permute-start.32 = (f32[80,128]{1,0:T(8,128)S(1)}, f32[80,128]{1,0:T(8,128)S(1)}, u32[]{:S(2)}, u32[]{:S(2)}) collective-permute-start(f32[80,128]{1,0:T(8,128)S(1)} %fusion.11), channel_id=1, source_target_pairs={{0,192},{32,224},{64,0},{96,32},{128,64},{160,96},{192,128},{224,1... | collective-permute-start | bytes 122888 | tf_op jit(solution)/shard_map/ppermute | solution.py:37
  109.0 2.3 %collective-permute-start.30 = (f32[80,128]{1,0:T(8,128)S(1)}, f32[80,128]{1,0:T(8,128)S(1)}, u32[]{:S(2)}, u32[]{:S(2)}) collective-permute-start(f32[80,128]{1,0:T(8,128)S(1)} %fusion.11), channel_id=1, source_target_pairs={{0,64},{32,96},{64,128},{96,160},{128,192},{160,224},{192,0},{224,... | collective-permute-start | bytes 122888 | tf_op jit(solution)/shard_map/ppermute | solution.py:37
  111.3 4.0 %collective-permute-done.31 = f32[80,128]{1,0:T(8,128)S(1)} collective-permute-done((f32[80,128]{1,0:T(8,128)S(1)}, f32[80,128]{1,0:T(8,128)S(1)}, u32[]{:S(2)}, u32[]{:S(2)}) %collective-permute-start.31) | collective-permute-done | bytes 40992 | tf_op jit(solution)/shard_map/ppermute | solution.py:37
  115.3 6.3 %collective-permute-start.33 = (f32[320,128]{1,0:T(8,128)S(1)}, f32[320,128]{1,0:T(8,128)S(1)}, u32[]{:S(2)}, u32[]{:S(2)}) collective-permute-start(f32[320,128]{1,0:T(8,128)S(1)} %pad_maximum_fusion.6.near), channel_id=1, source_target_pairs={{0,32},{32,0},{64,96},{96,64},{128,160},{160,128},{192,224},{224,1... | collective-permute-start | bytes 491528 | tf_op jit(solution)/shard_map/ppermute | solution.py:53
  123.3 1.7 %settle.1 = (f32[128,512]{1,0:T(8,128)}, f32[1,512]{1,0:T(1,128)}) custom-call(s32[2]{0:T(128)} %copy-done.4, f32[320,128]{1,0:T(8,128)} %copy-done.5, f32[320,128]{1,0:T(8,128)} %copy-done.6), custom_call_target="tpu_custom_call" | custom-call | tf_op jit(solution)/shard_map/settle/pallas_call | solution.py:189
  (105 shorter events, 26.3 us)
Async XLA Ops:
  0.6 4.7 %collective-permute-start = (bf16[128,128]{1,0:T(8,128)(2,1)}, bf16[128,128]{1,0:T(8,128)(2,1)S(1)}, u32[]{:S(2)}, u32[]{:S(2)}) collective-permute-start(bf16[128,128]{1,0:T(8,128)(2,1)} %param.7), channel_id=1, source_target_pairs={{0,2},{1,3},{2,0},{3,1},{4,6},{5,7},{6,4},{7,5},{8,10},{9,11},{10,... | collective-permute-start | bytes 98312 | tf_op jit(solution)/shard_map/ppermute | solution.py:45
  2.8 5.2 %collective-permute-start.5 = (bf16[128,128]{1,0:T(8,128)(2,1)}, bf16[128,128]{1,0:T(8,128)(2,1)S(1)}, u32[]{:S(2)}, u32[]{:S(2)}) collective-permute-start(bf16[128,128]{1,0:T(8,128)(2,1)} %param.7), channel_id=1, source_target_pairs={{0,1},{1,0},{2,3},{3,2},{4,5},{5,4},{6,7},{7,6},{8,9},{9,8},{10,11... | collective-permute-start | bytes 98312 | tf_op jit(solution)/shard_map/ppermute | solution.py:49
  6.1 4.3 %collective-permute-start.1 = (bf16[256,128]{1,0:T(8,128)(2,1)S(1)}, bf16[256,128]{1,0:T(8,128)(2,1)S(1)}, u32[]{:S(2)}, u32[]{:S(2)}) collective-permute-start(bf16[256,128]{1,0:T(8,128)(2,1)S(1)} %pad_maximum_fusion.10), channel_id=1, source_target_pairs={{0,6},{1,7},{2,4},{3,5},{4,2},{5,3},{6,0},{7,1},{8,14},{9,15},{10,... | collective-permute-start | bytes 196616 | tf_op jit(solution)/shard_map/ppermute | solution.py:45
  8.0 6.1 %collective-permute-start.6 = (bf16[128,128]{1,0:T(8,128)(2,1)S(1)}, bf16[128,128]{1,0:T(8,128)(2,1)S(1)}, u32[]{:S(2)}, u32[]{:S(2)}) collective-permute-start(bf16[128,128]{1,0:T(8,128)(2,1)S(1)} %collective-permute-done.5), channel_id=1, source_target_pairs={{0,8},{1,9},{2,10},{3,11},{4,12},{5,13},{6,14},{7,15},{8,0},{9,1},... | collective-permute-start | bytes 98312 | tf_op jit(solution)/shard_map/ppermute | solution.py:41
  10.4 6.5 %collective-permute-start.2 = (bf16[512,128]{1,0:T(8,128)(2,1)S(1)}, bf16[512,128]{1,0:T(8,128)(2,1)S(1)}, u32[]{:S(2)}, u32[]{:S(2)}) collective-permute-start(bf16[512,128]{1,0:T(8,128)(2,1)S(1)} %get-tuple-element.48), channel_id=1, source_target_pairs={{0,8},{1,9},{2,10},{3,11},{4,12},{5,13},{6,14},{7,15},{8,16},{9,17... | collective-permute-start | bytes 393224 | tf_op jit(solution)/shard_map/ppermute | solution.py:29
  11.7 6.8 %collective-permute-start.3 = (bf16[512,128]{1,0:T(8,128)(2,1)S(1)}, bf16[512,128]{1,0:T(8,128)(2,1)S(1)}, u32[]{:S(2)}, u32[]{:S(2)}) collective-permute-start(bf16[512,128]{1,0:T(8,128)(2,1)S(1)} %get-tuple-element.48), channel_id=1, source_target_pairs={{0,16},{1,17},{2,18},{3,19},{4,20},{5,21},{6,22},{7,23},{8,24},{9,... | collective-permute-start | bytes 393224 | tf_op jit(solution)/shard_map/ppermute | solution.py:29
  14.2 5.5 %collective-permute-start.7 = (bf16[256,128]{1,0:T(8,128)(2,1)S(1)}, bf16[256,128]{1,0:T(8,128)(2,1)S(1)}, u32[]{:S(2)}, u32[]{:S(2)}) collective-permute-start(bf16[256,128]{1,0:T(8,128)(2,1)S(1)} %pad_maximum_fusion.11), channel_id=1, source_target_pairs={{0,24},{1,25},{2,26},{3,27},{4,28},{5,29},{6,30},{7,31},{8,16},{9,... | collective-permute-start | bytes 196616 | tf_op jit(solution)/shard_map/ppermute | solution.py:41
  15.4 4.1 %collective-permute-start.4 = (bf16[512,128]{1,0:T(8,128)(2,1)S(1)}, bf16[512,128]{1,0:T(8,128)(2,1)S(1)}, u32[]{:S(2)}, u32[]{:S(2)}) collective-permute-start(bf16[512,128]{1,0:T(8,128)(2,1)S(1)} %get-tuple-element.48), channel_id=1, source_target_pairs={{0,24},{1,25},{2,26},{3,27},{4,28},{5,29},{6,30},{7,31},{8,0},{9,1... | collective-permute-start | bytes 393224 | tf_op jit(solution)/shard_map/ppermute | solution.py:29
  19.7 12.6 %collective-permute-start.9 = (bf16[512,128]{1,0:T(8,128)(2,1)S(1)}, bf16[512,128]{1,0:T(8,128)(2,1)S(1)}, u32[]{:S(2)}, u32[]{:S(2)}) collective-permute-start(bf16[512,128]{1,0:T(8,128)(2,1)S(1)} %get-tuple-element.46), channel_id=1, source_target_pairs={{0,4},{1,5},{2,6},{3,7},{4,0},{5,1},{6,2},{7,3},{8,12},{9,13},{10,... | collective-permute-start | bytes 393224 | tf_op jit(solution)/shard_map/ppermute | solution.py:33
  22.4 9.8 %collective-permute-start.8 = (bf16[512,128]{1,0:T(8,128)(2,1)S(1)}, bf16[512,128]{1,0:T(8,128)(2,1)S(1)}, u32[]{:S(2)}, u32[]{:S(2)}) collective-permute-start(bf16[512,128]{1,0:T(8,128)(2,1)S(1)} %get-tuple-element.46), channel_id=1, source_target_pairs={{0,2},{1,3},{2,4},{3,5},{4,6},{5,7},{6,0},{7,1},{8,10},{9,11},{10,... | collective-permute-start | bytes 393224 | tf_op jit(solution)/shard_map/ppermute | solution.py:33
  30.2 4.0 %collective-permute-start.10 = (bf16[512,128]{1,0:T(8,128)(2,1)S(1)}, bf16[512,128]{1,0:T(8,128)(2,1)S(1)}, u32[]{:S(2)}, u32[]{:S(2)}) collective-permute-start(bf16[512,128]{1,0:T(8,128)(2,1)S(1)} %get-tuple-element.46), channel_id=1, source_target_pairs={{0,6},{1,7},{2,0},{3,1},{4,2},{5,3},{6,4},{7,5},{8,14},{9,15},{10,... | collective-permute-start | bytes 393224 | tf_op jit(solution)/shard_map/ppermute | solution.py:33
  36.6 6.3 %collective-permute-start.11 = (bf16[4,128,128]{2,1,0:T(8,128)(2,1)S(1)}, bf16[4,128,128]{2,1,0:T(8,128)(2,1)S(1)}, u32[]{:S(2)}, u32[]{:S(2)}) collective-permute-start(bf16[4,128,128]{2,1,0:T(8,128)(2,1)S(1)} %bitcast.50), channel_id=1, source_target_pairs={{0,32},{32,0},{64,96},{96,64},{128,160},{160,128},{192,224},{224,1... | collective-permute-start | bytes 393224 | tf_op jit(solution)/shard_map/ppermute | solution.py:53
  43.0 11.0 %collective-permute-start.14 = (bf16[128,128]{1,0:T(8,128)(2,1)S(1)}, bf16[128,128]{1,0:T(8,128)(2,1)S(1)}, u32[]{:S(2)}, u32[]{:S(2)}) collective-permute-start(bf16[128,128]{1,0:T(8,128)(2,1)S(1)} %get-tuple-element.37), channel_id=1, source_target_pairs={{0,64},{32,96},{64,128},{96,160},{128,192},{160,224},{192,0},{224,... | collective-permute-start | bytes 98312 | tf_op jit(solution)/shard_map/ppermute | solution.py:37
  45.8 8.2 %collective-permute-start.13 = (bf16[128,128]{1,0:T(8,128)(2,1)S(1)}, bf16[128,128]{1,0:T(8,128)(2,1)S(1)}, u32[]{:S(2)}, u32[]{:S(2)}) collective-permute-start(bf16[128,128]{1,0:T(8,128)(2,1)S(1)} %get-tuple-element.38), channel_id=1, source_target_pairs={{0,128},{32,160},{64,192},{96,224},{128,0},{160,32},{192,64},{224,... | collective-permute-start | bytes 98312 | tf_op jit(solution)/shard_map/ppermute | solution.py:37
  50.6 4.4 %collective-permute-start.12 = (bf16[128,128]{1,0:T(8,128)(2,1)S(1)}, bf16[128,128]{1,0:T(8,128)(2,1)S(1)}, u32[]{:S(2)}, u32[]{:S(2)}) collective-permute-start(bf16[128,128]{1,0:T(8,128)(2,1)S(1)} %get-tuple-element.39), channel_id=1, source_target_pairs={{0,192},{32,224},{64,0},{96,32},{128,64},{160,96},{192,128},{224,1... | collective-permute-start | bytes 98312 | tf_op jit(solution)/shard_map/ppermute | solution.py:37
  56.6 8.6 %collective-permute-start.15 = (bf16[288,128]{1,0:T(8,128)(2,1)S(1)}, bf16[288,128]{1,0:T(8,128)(2,1)S(1)}, u32[]{:S(2)}, u32[]{:S(2)}) collective-permute-start(bf16[288,128]{1,0:T(8,128)(2,1)S(1)} %get-tuple-element.36), channel_id=1, source_target_pairs={{0,64},{32,96},{64,128},{96,160},{128,192},{160,224},{192,0},{224,... | collective-permute-start | bytes 221192 | tf_op jit(solution)/shard_map/ppermute | solution.py:37
  59.0 6.2 %collective-permute-start.17 = (bf16[288,128]{1,0:T(8,128)(2,1)S(1)}, bf16[288,128]{1,0:T(8,128)(2,1)S(1)}, u32[]{:S(2)}, u32[]{:S(2)}) collective-permute-start(bf16[288,128]{1,0:T(8,128)(2,1)S(1)} %get-tuple-element.34), channel_id=1, source_target_pairs={{0,192},{32,224},{64,0},{96,32},{128,64},{160,96},{192,128},{224,1... | collective-permute-start | bytes 221192 | tf_op jit(solution)/shard_map/ppermute | solution.py:37
  60.8 7.3 %collective-permute-start.16 = (bf16[288,128]{1,0:T(8,128)(2,1)S(1)}, bf16[288,128]{1,0:T(8,128)(2,1)S(1)}, u32[]{:S(2)}, u32[]{:S(2)}) collective-permute-start(bf16[288,128]{1,0:T(8,128)(2,1)S(1)} %get-tuple-element.35), channel_id=1, source_target_pairs={{0,128},{32,160},{64,192},{96,224},{128,0},{160,32},{192,64},{224,... | collective-permute-start | bytes 221192 | tf_op jit(solution)/shard_map/ppermute | solution.py:37
  68.1 4.6 %collective-permute-start.18 = (bf16[672,128]{1,0:T(8,128)(2,1)S(1)}, bf16[672,128]{1,0:T(8,128)(2,1)S(1)}, u32[]{:S(2)}, u32[]{:S(2)}) collective-permute-start(bf16[672,128]{1,0:T(8,128)(2,1)S(1)} %constant_dynamic-update-slice_fusion.18), channel_id=1, source_target_pairs={{0,32},{32,0},{64,96},{96,64},{128,160},{160,128},{192,224},{224,1... | collective-permute-start | bytes 516104 | tf_op jit(solution)/shard_map/ppermute | solution.py:53
  75.2 6.9 %collective-permute-start.24 = (bf16[512,128]{1,0:T(8,128)(2,1)S(1)}, bf16[512,128]{1,0:T(8,128)(2,1)S(1)}, u32[]{:S(2)}, u32[]{:S(2)}) collective-permute-start(bf16[512,128]{1,0:T(8,128)(2,1)S(1)} %get-tuple-element.26), channel_id=1, source_target_pairs={{0,6},{1,7},{2,0},{3,1},{4,2},{5,3},{6,4},{7,5},{8,14},{9,15},{10,... | collective-permute-start | bytes 393224 | tf_op jit(solution)/shard_map/ppermute | solution.py:33
  77.7 13.0 %collective-permute-start.19 = (bf16[672,128]{1,0:T(8,128)(2,1)S(1)}, bf16[672,128]{1,0:T(8,128)(2,1)S(1)}, u32[]{:S(2)}, u32[]{:S(2)}) collective-permute-start(bf16[672,128]{1,0:T(8,128)(2,1)S(1)} %get-tuple-element.50), channel_id=1, source_target_pairs={{0,24},{1,25},{2,26},{3,27},{4,28},{5,29},{6,30},{7,31},{8,0},{9,1... | collective-permute-start | bytes 516104 | tf_op jit(solution)/shard_map/ppermute | solution.py:29
  81.5 9.2 %collective-permute-start.20 = (bf16[672,128]{1,0:T(8,128)(2,1)S(1)}, bf16[672,128]{1,0:T(8,128)(2,1)S(1)}, u32[]{:S(2)}, u32[]{:S(2)}) collective-permute-start(bf16[672,128]{1,0:T(8,128)(2,1)S(1)} %get-tuple-element.51), channel_id=1, source_target_pairs={{0,16},{1,17},{2,18},{3,19},{4,20},{5,21},{6,22},{7,23},{8,24},{9,... | collective-permute-start | bytes 516104 | tf_op jit(solution)/shard_map/ppermute | solution.py:29
  81.5 10.8 %collective-permute-start.21 = (bf16[672,128]{1,0:T(8,128)(2,1)S(1)}, bf16[672,128]{1,0:T(8,128)(2,1)S(1)}, u32[]{:S(2)}, u32[]{:S(2)}) collective-permute-start(bf16[672,128]{1,0:T(8,128)(2,1)S(1)} %get-tuple-element.52), channel_id=1, source_target_pairs={{0,8},{1,9},{2,10},{3,11},{4,12},{5,13},{6,14},{7,15},{8,16},{9,17... | collective-permute-start | bytes 516104 | tf_op jit(solution)/shard_map/ppermute | solution.py:29
  82.1 8.5 %collective-permute-start.26 = (bf16[512,128]{1,0:T(8,128)(2,1)S(1)}, bf16[512,128]{1,0:T(8,128)(2,1)S(1)}, u32[]{:S(2)}, u32[]{:S(2)}) collective-permute-start(bf16[512,128]{1,0:T(8,128)(2,1)S(1)} %get-tuple-element.27), channel_id=1, source_target_pairs={{0,2},{1,3},{2,4},{3,5},{4,6},{5,7},{6,0},{7,1},{8,10},{9,11},{10,... | collective-permute-start | bytes 393224 | tf_op jit(solution)/shard_map/ppermute | solution.py:33
  82.2 8.5 %collective-permute-start.25 = (bf16[512,128]{1,0:T(8,128)(2,1)S(1)}, bf16[512,128]{1,0:T(8,128)(2,1)S(1)}, u32[]{:S(2)}, u32[]{:S(2)}) collective-permute-start(bf16[512,128]{1,0:T(8,128)(2,1)S(1)} %get-tuple-element.28), channel_id=1, source_target_pairs={{0,4},{1,5},{2,6},{3,7},{4,0},{5,1},{6,2},{7,3},{8,12},{9,13},{10,... | collective-permute-start | bytes 393224 | tf_op jit(solution)/shard_map/ppermute | solution.py:33
  92.5 4.4 %collective-permute-start.27 = (bf16[256,128]{1,0:T(8,128)(2,1)S(1)}, bf16[256,128]{1,0:T(8,128)(2,1)S(1)}, u32[]{:S(2)}, u32[]{:S(2)}) collective-permute-start(bf16[256,128]{1,0:T(8,128)(2,1)S(1)} %slice.425), channel_id=1, source_target_pairs={{0,24},{1,25},{2,26},{3,27},{4,28},{5,29},{6,30},{7,31},{8,16},{9,... | collective-permute-start | bytes 196616 | tf_op jit(solution)/shard_map/ppermute | solution.py:41
  93.0 5.1 %collective-permute-start.22 = (bf16[416,128]{1,0:T(8,128)(2,1)S(1)}, bf16[416,128]{1,0:T(8,128)(2,1)S(1)}, u32[]{:S(2)}, u32[]{:S(2)}) collective-permute-start(bf16[416,128]{1,0:T(8,128)(2,1)S(1)} %pad_maximum_fusion.7), channel_id=1, source_target_pairs={{0,6},{1,7},{2,4},{3,5},{4,2},{5,3},{6,0},{7,1},{8,14},{9,15},{10,... | collective-permute-start | bytes 319496 | tf_op jit(solution)/shard_map/ppermute | solution.py:45
  98.2 3.5 %collective-permute-start.23 = (bf16[288,128]{1,0:T(8,128)(2,1)S(1)}, bf16[288,128]{1,0:T(8,128)(2,1)S(1)}, u32[]{:S(2)}, u32[]{:S(2)}) collective-permute-start(bf16[288,128]{1,0:T(8,128)(2,1)S(1)} %pad_maximum_fusion.8), channel_id=1, source_target_pairs={{0,2},{1,3},{2,0},{3,1},{4,6},{5,7},{6,4},{7,5},{8,10},{9,11},{10,... | collective-permute-start | bytes 221192 | tf_op jit(solution)/shard_map/ppermute | solution.py:45
  105.1 6.2 %collective-permute-start.32 = (f32[80,128]{1,0:T(8,128)S(1)}, f32[80,128]{1,0:T(8,128)S(1)}, u32[]{:S(2)}, u32[]{:S(2)}) collective-permute-start(f32[80,128]{1,0:T(8,128)S(1)} %fusion.11), channel_id=1, source_target_pairs={{0,192},{32,224},{64,0},{96,32},{128,64},{160,96},{192,128},{224,1... | collective-permute-start | bytes 122888 | tf_op jit(solution)/shard_map/ppermute | solution.py:37
  108.4 6.9 %collective-permute-start.31 = (f32[80,128]{1,0:T(8,128)S(1)}, f32[80,128]{1,0:T(8,128)S(1)}, u32[]{:S(2)}, u32[]{:S(2)}) collective-permute-start(f32[80,128]{1,0:T(8,128)S(1)} %fusion.11), channel_id=1, source_target_pairs={{0,128},{32,160},{64,192},{96,224},{128,0},{160,32},{192,64},{224,... | collective-permute-start | bytes 122888 | tf_op jit(solution)/shard_map/ppermute | solution.py:37
  109.0 6.2 %collective-permute-start.30 = (f32[80,128]{1,0:T(8,128)S(1)}, f32[80,128]{1,0:T(8,128)S(1)}, u32[]{:S(2)}, u32[]{:S(2)}) collective-permute-start(f32[80,128]{1,0:T(8,128)S(1)} %fusion.11), channel_id=1, source_target_pairs={{0,64},{32,96},{64,128},{96,160},{128,192},{160,224},{192,0},{224,... | collective-permute-start | bytes 122888 | tf_op jit(solution)/shard_map/ppermute | solution.py:37
  115.3 7.3 %collective-permute-start.33 = (f32[320,128]{1,0:T(8,128)S(1)}, f32[320,128]{1,0:T(8,128)S(1)}, u32[]{:S(2)}, u32[]{:S(2)}) collective-permute-start(f32[320,128]{1,0:T(8,128)S(1)} %pad_maximum_fusion.6.near), channel_id=1, source_target_pairs={{0,32},{32,0},{64,96},{96,64},{128,160},{160,128},{192,224},{224,1... | collective-permute-start | bytes 491528 | tf_op jit(solution)/shard_map/ppermute | solution.py:53
  (9 other events, 124.4 us)
where the time goes:
time: 125 us
  starting transfers between devices  69.9 us (56%)
  waiting for transfers between devices  35.2 us (28%)
  Pallas kernels  6.74 us (5%)
  matrix products  4.8 us (4%)
  local copies, waits for them, and re-layouts  4.11 us (3%)
  other arithmetic  2.57 us (2%)
  between operations  1.65 us (1%)
    ppermute x9, starting transfers between devices, move_h(): return lax.ppermute(v, 'row', ring(4, 2, 8, step))  25.8 us
    ppermute x3, starting transfers between devices, swap_k(): return lax.ppermute(v, 'row', mirror(2, 1, 8, 1))  15.1 us
    ppermute x6, starting transfers between devices, move_x(): return lax.ppermute(v, 'col', ring(4, 8, 32, step))  9.69 us
    ppermute x6, waiting for transfers between devices, move_y(): return lax.ppermute(v, 'col', ring(4, 2, 32, step))  9.22 us
    ppermute x6, starting transfers between devices, move_y(): return lax.ppermute(v, 'col', ring(4, 2, 32, step))  9.03 us
    ppermute x9, waiting for transfers between devices, move_h(): return lax.ppermute(v, 'row', ring(4, 2, 8, step))  7.89 us
    ppermute x4, waiting for transfers between devices, swap_x(): return lax.ppermute(v, 'col', mirror(4, 8, 32, mask))  5.45 us
    ppermute x4, starting transfers between devices, swap_y(): return lax.ppermute(v, 'col', mirror(4, 2, 32, mask))  4.58 us
  transfers between devices with their start and end apart: 34, of which 18 were waited for; matrix products, arithmetic and copies ran while one was open for 3% of the time, Pallas kernels for 3%

commit v1 on v0

v1 whole, which is shorter than its diff:
```python
import jax
import jax.numpy as jnp
from jax import lax
from jax.experimental import pallas as pl
from jax.experimental.pallas import tpu as pltpu
from jax.sharding import PartitionSpec as P

BF, F32 = jnp.bfloat16, jnp.float32
VMEM = pltpu.VMEM


def ring(i, count, inner, step):
    digit = (i // inner) % count
    return i + ((digit + step) % count - digit) * inner


def mirror(i, count, inner, mask):
    digit = (i // inner) % count
    return i + ((digit ^ mask) - digit) * inner


def move_xy(v, step, turn):
    pairs = []
    for i in range(256):
        row, col = i // 32, i % 32
        pairs.append((i, row * 32 + ring(col, 4, 2 if row % 2 == turn else 8, step)))
    return lax.ppermute(v, ("row", "col"), pairs)


def move_h(v, step):
    return lax.ppermute(v, "row", [(i, ring(i, 4, 2, step)) for i in range(8)])


def swap_h(v, mask):
    return lax.ppermute(v, "row", [(i, mirror(i, 4, 2, mask)) for i in range(8)])


def swap_k(v):
    return lax.ppermute(v, "row", [(i, i ^ 1) for i in range(8)])


def swap_z(v):
    return lax.ppermute(v, "col", [(i, i ^ 1) for i in range(32)])


def pair(v):
    high = v.astype(BF)
    return jnp.concatenate([high, (v - high.astype(F32)).astype(BF)])


def unpair(v):
    rows = v.shape[0] // 2
    return v[:rows].astype(F32) + v[rows:].astype(F32)


def spread_kernel(count_ref, put_row, put_col, tiles_ref, dense_ref):
    size = tiles_ref.shape[1]
    dense_ref[...] = jnp.zeros_like(dense_ref)

    def place(slot, carry):
        rows = pl.ds(pl.multiple_of(put_row[slot] * size, size), size)
        cols = pl.ds(pl.multiple_of(put_col[slot] * size, size), size)
        dense_ref[rows, cols] = tiles_ref[slot]
        return carry

    lax.fori_loop(0, count_ref[0], place, 0)


def spread(tiles, count, put_row, put_col, rows, cols):
    slots, size, _ = tiles.shape
    smem = pl.BlockSpec(memory_space=pltpu.SMEM)
    return pl.pallas_call(
        spread_kernel,
        out_shape=jax.ShapeDtypeStruct((rows * size, cols * size), BF),
        in_specs=[smem, smem, smem, pl.BlockSpec(memory_space=VMEM)],
        out_specs=pl.BlockSpec(memory_space=VMEM),
        compiler_params=pltpu.CompilerParams(vmem_limit_bytes=32 * 2**20),
        cost_estimate=pl.CostEstimate(
            flops=0, bytes_accessed=2 * size * size * (slots + rows * cols), transcendentals=0
        ),
        name="spread",
    )(count, put_row, put_col, tiles)


def middle_kernel(place, own, in1, in2, in3, weight, bias, cot, hidden_ref, sent_ref, gw_ref, whole):
    agg = own[...] + in1[...].astype(F32) + in2[...].astype(F32) + in3[...].astype(F32)
    high = agg.astype(BF)
    low = (agg - high.astype(F32)).astype(BF)
    w = weight[...]
    pre = (
        jnp.dot(high, w, preferred_element_type=F32)
        + jnp.dot(low, w, preferred_element_type=F32)
        + bias[...]
    )
    sig = jax.nn.sigmoid(pre)
    hidden_ref[...] = (pre * sig).astype(BF)
    dpre = (cot[...].astype(F32) * (sig + pre * sig * (1.0 - sig))).astype(BF)
    back = lax.dot_general(
        dpre, w, (((1,), (1,)), ((), ())), preferred_element_type=F32
    ).astype(BF)
    over_nodes = (((0,), (0,)), ((), ()))
    whole[...] = lax.dot_general(
        high, dpre, over_nodes, preferred_element_type=F32
    ) + lax.dot_general(low, dpre, over_nodes, preferred_element_type=F32)
    sums = jnp.sum(dpre.astype(F32), axis=0, keepdims=True)
    size, lanes = back.shape
    blocks = cot.shape[1] // lanes
    rows = whole.shape[0] // 8
    tail = jnp.concatenate(
        [sums[:, j * lanes : (j + 1) * lanes] for j in range(blocks)]
        + [jnp.zeros((rows - blocks, lanes), F32)]
    )
    for h in range(4):
        sent_ref[h, :size, :] = back
        for k in range(2):
            at = (lax.rem(place[0] + h, 4) * 2 + (place[1] ^ k)) * rows
            at = pl.ds(pl.multiple_of(at, rows), rows)
            for j in range(blocks + 1):
                piece = whole[at, j * lanes : (j + 1) * lanes] if j < blocks else tail
                to = (k * (blocks + 1) + j) * rows
                sent_ref[h, size + to : size + to + rows, :] = piece.astype(BF)
                if h == 0:
                    gw_ref[to : to + rows, :] = piece


def middle(place, own, arrived, weight, bias, cotangent):
    size, width = cotangent.shape
    feats = weight.shape[0]
    share = (feats // 4) * (width // feats + 1)
    vmem = pl.BlockSpec(memory_space=VMEM)
    return pl.pallas_call(
        middle_kernel,
        out_shape=(
            jax.ShapeDtypeStruct((size, width), BF),
            jax.ShapeDtypeStruct((4, size + share, feats), BF),
            jax.ShapeDtypeStruct((share, feats), F32),
        ),
        in_specs=[pl.BlockSpec(memory_space=pltpu.SMEM)] + [vmem] * 7,
        out_specs=(vmem, vmem, vmem),
        scratch_shapes=[VMEM((feats, width), F32)],
        compiler_params=pltpu.CompilerParams(vmem_limit_bytes=16 * 2**20),
        cost_estimate=pl.CostEstimate(
            flops=10 * size * feats * width, bytes_accessed=10 * size * width, transcendentals=size * width
        ),
        name="middle",
    )(place, own, *arrived, weight, bias[None, :], cotangent)


def settle_kernel(place, near, far, out_ref):
    lanes = near.shape[1]
    blocks = out_ref.shape[1] // lanes
    rows = near.shape[0] // 4 // blocks
    for k, part in ((0, near), (1, far)):
        for first, bits in enumerate((0, 1, 3, 2)):
            at = ((place[0] ^ bits) * 2 + (place[1] ^ k)) * rows
            at = pl.ds(pl.multiple_of(at, rows), rows)
            for j in range(blocks):
                start = (first * blocks + j) * rows
                out_ref[at, j * lanes : (j + 1) * lanes] = part[start : start + rows, :].astype(F32)


def settle(place, near, far, feats, width):
    vmem = pl.BlockSpec(memory_space=VMEM)
    return pl.pallas_call(
        settle_kernel,
        out_shape=jax.ShapeDtypeStruct((feats, width), F32),
        in_specs=[pl.BlockSpec(memory_space=pltpu.SMEM), vmem, vmem],
        out_specs=vmem,
        compiler_params=pltpu.CompilerParams(vmem_limit_bytes=16 * 2**20),
        name="settle",
    )(place, near, far)


def local(features, weight, bias, tile_values, tile_index, tile_count, cotangent):
    size = features.shape[0]
    feats, width = weight.shape
    places = tile_index[0, 0]
    row, col = lax.axis_index("row"), lax.axis_index("col")
    h, k = row // 2, row % 2
    x, y, z = col // 8, (col // 2) % 4, col % 2
    here = jnp.stack([h, k]).astype(jnp.int32)

    tile_row, tile_col = places // 32, places % 32
    far_h, far_k = (h - tile_row // 2) % 4, (k - tile_row) % 2
    far_x, far_y, far_z = (x - tile_col // 8) % 4, (y - tile_col // 2) % 4, (z - tile_col) % 2
    put_row = (far_k * 4 + far_h).astype(jnp.int32)
    put_col = (jnp.where(k == 0, far_x * 4 + far_y, far_y * 4 + far_x) * 2 + far_z).astype(jnp.int32)
    dense = spread(tile_values[0, 0], tile_count[0], put_row, put_col, 8, 32)

    source = jnp.stack([features, swap_z(features)])
    for turn in (0, 1):
        source = jnp.stack([source] + [move_xy(source, s, turn) for s in (1, 2, 3)])
    source = source.reshape(-1, feats)

    part = jnp.dot(dense, source, preferred_element_type=F32).reshape(2, 4, size, feats)
    half = part[0] + swap_k(part[1].astype(BF)).astype(F32)
    sent = half.astype(BF)
    arrived = [move_h(sent[s], -s) for s in (1, 2, 3)]
    hidden_out, sent, gw = middle(here, half[0], arrived, weight, bias, cotangent)

    arrived = [move_h(sent[s], s) for s in (1, 2, 3)]
    target = jnp.concatenate([sent[0][:size]] + [v[:size] for v in arrived])
    gw = gw + sum(v[size:].astype(F32) for v in arrived)
    share = gw.shape[0] // 2
    arrived = swap_k(jnp.concatenate([target, pair(gw[share:])]))
    gw = gw[:share] + unpair(arrived[4 * size :])
    target = jnp.concatenate([target, arrived[: 4 * size]])
    gw = gw + swap_z(gw)

    grad = lax.dot_general(dense, target, (((0,), (0,)), ((), ())), preferred_element_type=F32)
    for turn in (1, 0):
        grad = grad.reshape(4, -1, feats)
        rows = grad.shape[1]
        low, extra = grad.astype(BF), gw.astype(BF)
        arrived = [move_xy(jnp.concatenate([low[s], extra]), -s, turn) for s in (1, 2, 3)]
        grad = grad[0] + sum(v[:rows].astype(F32) for v in arrived)
        one, two, three = [v[rows:].astype(F32) for v in arrived]
        gw = (extra.astype(F32) + two) + (one + three)
    grad_features = (grad[:size] + swap_z(grad[size:].astype(BF)).astype(F32)).astype(BF)

    share = share * width // (width + feats)
    grad_bias = gw[share : share + width // feats].reshape(width)
    gw = gw[:share].astype(BF)
    gw = jnp.concatenate([gw, swap_h(gw, 1)])
    gw = jnp.concatenate([gw, swap_h(gw, 3)])
    grad_weight = settle(here, gw, swap_k(gw), feats, width)
    return (hidden_out, grad_features, grad_weight, grad_bias)


def solution(mesh):
    in_specs = (
        P(("row", "col"), None),
        P(),
        P(),
        P("row", "col", None, None, None),
        P("row", "col", None),
        P("row", "col"),
        P(("col", "row"), None),
    )
    out_specs = (P(("col", "row"), None), P(("row", "col"), None), P(), P())
    return jax.shard_map(local, mesh=mesh, in_specs=in_specs, out_specs=out_specs, check_vma=False)
```

time: 125 us -> 102 us (0.82)
  starting transfers between devices: 69.9 us -> 50.7 us
  Pallas kernels: 6.74 us -> 4.2 us
    ppermute x34 -> x26, starting transfers between devices: 69.9 us -> 50.7 us  [the longest x6 16.6 us: move_h(): return lax.ppermute(v, 'row', [(i, ring(i, 4, 2, step)) for i in range(8)])]
    pallas_call x1, Pallas kernels: 3.51 us -> 1.45 us  [spread(): pl.pallas_call(spread_kernel, out_shape=jax.ShapeDtypeStruct((rows * size...]
    unnamed x28 -> x13, local copies, waits for them, and re-layouts: 3.88 us -> 2.26 us
    ppermute x34 -> x26, waiting for transfers between devices: 35.2 us -> 34.6 us  [the longest x12 18.8 us: move_xy(): return lax.ppermute(v, ('row', 'col'), pairs)]
  transfers between devices with their start and end apart: 34 -> 26, of which waited for: 18 -> 17; matrix products, arithmetic and copies ran while one was open for 3% -> 4% of each run, Pallas kernels for 3% -> 1%
where the time goes in v1:
time: 102 us
  starting transfers between devices  50.7 us (50%)
  waiting for transfers between devices  34.6 us (34%)
  matrix products  4.76 us (5%)
  Pallas kernels  4.2 us (4%)
  local copies, waits for them, and re-layouts  3 us (3%)
  other arithmetic  2.72 us (3%)
  between operations  1.56 us (2%)
    ppermute x12, waiting for transfers between devices, move_xy(): return lax.ppermute(v, ('row', 'col'), pairs)  18.8 us
    ppermute x6, starting transfers between devices, move_h(): return lax.ppermute(v, 'row', [(i, ring(i, 4, 2, step)) for i in range(8)])  16.6 us
    ppermute x3, starting transfers between devices, swap_k(): return lax.ppermute(v, 'row', [(i, i ^ 1) for i in range(8)])  13.8 us
    ppermute x12, starting transfers between devices, move_xy(): return lax.ppermute(v, ('row', 'col'), pairs)  13.5 us
    ppermute x6, waiting for transfers between devices, move_h(): return lax.ppermute(v, 'row', [(i, ring(i, 4, 2, step)) for i in range(8)])  7.95 us
    ppermute x3, starting transfers between devices, swap_z(): return lax.ppermute(v, 'col', [(i, i ^ 1) for i in range(32)])  4.62 us
    ppermute x2, waiting for transfers between devices, swap_h(): lax.ppermute(v, 'row', [(i, mirror(i, 4, 2, mask)) for i in range(8)])  4.15 us
    dot_general x1, matrix products, local(): lax.dot_general(dense, target, (((0,), (0,)), ((), ())), preferred_elemen...  2.42 us
  transfers between devices with their start and end apart: 26, of which 17 were waited for; matrix products, arithmetic and copies ran while one was open for 4% of the time, Pallas kernels for 1%

profile of v1, /device:TPU:1, one launch (start us, length us, event | category | flops | bytes accessed | tf_op | source)
XLA Modules:
  0.0 101.6 jit_solution(10705354810070523196)
XLA Ops:
  0.6 2.6 %collective-permute-start = (bf16[128,128]{1,0:T(8,128)(2,1)}, bf16[128,128]{1,0:T(8,128)(2,1)S(1)}, u32[]{:S(2)}, u32[]{:S(2)}) collective-permute-start(bf16[128,128]{1,0:T(8,128)(2,1)} %param.7), channel_id=1, source_target_pairs={{0,1},{1,0},{2,3},{3,2},{4,5},{5,4},{6,7},{7,6},{8,9},{9,8},{10,11... | collective-permute-start | bytes 98312 | tf_op jit(solution)/shard_map/ppermute | solution.py:43
  3.2 1.5 %collective-permute-done = bf16[128,128]{1,0:T(8,128)(2,1)S(1)} collective-permute-done((bf16[128,128]{1,0:T(8,128)(2,1)}, bf16[128,128]{1,0:T(8,128)(2,1)S(1)}, u32[]{:S(2)}, u32[]{:S(2)}) %collective-permute-start) | collective-permute-done | bytes 32800 | tf_op jit(solution)/shard_map/ppermute | solution.py:43
  5.5 2.6 %collective-permute-start.3 = (bf16[2,128,128]{2,1,0:T(8,128)(2,1)S(1)}, bf16[2,128,128]{2,1,0:T(8,128)(2,1)S(1)}, u32[]{:S(2)}, u32[]{:S(2)}) collective-permute-start(bf16[2,128,128]{2,1,0:T(8,128)(2,1)S(1)} %get-tuple-element.37), channel_id=1, source_target_pairs={{0,6},{1,7},{2,0},{3,1},{4,2},{5,3},{6,4},{7,5},{8,14},{9,15},{10,... | collective-permute-start | bytes 196616 | tf_op jit(solution)/shard_map/ppermute | solution.py:27
  9.4 3.3 %collective-permute-done.2 = bf16[2,128,128]{2,1,0:T(8,128)(2,1)S(1)} collective-permute-done((bf16[2,128,128]{2,1,0:T(8,128)(2,1)S(1)}, bf16[2,128,128]{2,1,0:T(8,128)(2,1)S(1)}, u32[]{:S(2)}, u32[]{:S(2)}) %collective-permute-start.2) | collective-permute-done | bytes 65568 | tf_op jit(solution)/shard_map/ppermute | solution.py:27
  13.4 2.8 %collective-permute-start.6 = (bf16[4,2,128,128]{3,2,1,0:T(8,128)(2,1)S(1)}, bf16[4,2,128,128]{3,2,1,0:T(8,128)(2,1)S(1)}, u32[]{:S(2)}, u32[]{:S(2)}) collective-permute-start(bf16[4,2,128,128]{3,2,1,0:T(8,128)(2,1)S(1)} %get-tuple-element.26), channel_id=1, source_target_pairs={{0,24},{1,25},{2,26},{3,27},{4,28},{5,29},{6,30},{7,31},{8,0},{9,1... | collective-permute-start | bytes 786440 | tf_op jit(solution)/shard_map/ppermute | solution.py:27
  18.6 2.2 %copy-done = bf16[1,1,128,128,128]{4,3,2,1,0:T(8,128)(2,1)S(1)} copy-done((bf16[1,1,128,128,128]{4,3,2,1,0:T(8,128)(2,1)S(1)}, bf16[1,1,128,128,128]{4,3,2,1,0:T(8,128)(2,1)}, u32[]{:S(2)}) %copy-start) | copy-done | bytes 4194328
  20.8 1.5 %spread.1 = bf16[1024,4096]{1,0:T(8,128)(2,1)S(1)} custom-call(s32[1]{0:T(128)} %bitcast.60.count_ref, s32[128]{0:T(128)S(1)} %get-tuple-element.45.put_row, s32[128]{0:T(128)S(1)} %get-tuple-element.44.put_col, bf16[128,128,128]{2,1,0:T(8,128)(2,1)S(1)} %bitcast.61), custom_call_target="tpu_custom_call" | custom-call | bytes 12582912 | tf_op jit(solution)/shard_map/spread/pallas_call | solution.py:72
  23.0 3.0 %collective-permute-done.4 = bf16[4,2,128,128]{3,2,1,0:T(8,128)(2,1)S(1)} collective-permute-done((bf16[4,2,128,128]{3,2,1,0:T(8,128)(2,1)S(1)}, bf16[4,2,128,128]{3,2,1,0:T(8,128)(2,1)S(1)}, u32[]{:S(2)}, u32[]{:S(2)}) %collective-permute-start.4) | collective-permute-done | bytes 262176 | tf_op jit(solution)/shard_map/ppermute | solution.py:27
  26.2 2.3 %fusion.17 = f32[1024,128]{1,0:T(8,128)S(1)} fusion(bf16[1024,4096]{1,0:T(8,128)(2,1)S(1)} %spread.1, bf16[4096,128]{1,0:T(8,128)(2,1)S(1)} %bitcast.64), kind=kOutput, calls=%fused_computation.95 | convolution fusion | flops 1073741824 | bytes 9961472 | tf_op jit(solution)/shard_map/dot_general | solution.py:195
  28.5 4.3 %collective-permute-start.7 = (bf16[4,128,128]{2,1,0:T(8,128)(2,1)S(1)}, bf16[4,128,128]{2,1,0:T(8,128)(2,1)S(1)}, u32[]{:S(2)}, u32[]{:S(2)}) collective-permute-start(bf16[4,128,128]{2,1,0:T(8,128)(2,1)S(1)} %bitcast.68), channel_id=1, source_target_pairs={{0,32},{32,0},{64,96},{96,64},{128,160},{160,128},{192,224},{224,1... | collective-permute-start | bytes 393224 | tf_op jit(solution)/shard_map/ppermute | solution.py:39
  33.9 6.1 %collective-permute-start.8 = (bf16[128,128]{1,0:T(8,128)(2,1)S(1)}, bf16[128,128]{1,0:T(8,128)(2,1)S(1)}, u32[]{:S(2)}, u32[]{:S(2)}) collective-permute-start(bf16[128,128]{1,0:T(8,128)(2,1)S(1)} %get-tuple-element.29), channel_id=1, source_target_pairs={{0,192},{32,224},{64,0},{96,32},{128,64},{160,96},{192,128},{224,1... | collective-permute-start | bytes 98312 | tf_op jit(solution)/shard_map/ppermute | solution.py:31
  41.0 2.3 %collective-permute-start.10 = (bf16[128,128]{1,0:T(8,128)(2,1)S(1)}, bf16[128,128]{1,0:T(8,128)(2,1)S(1)}, u32[]{:S(2)}, u32[]{:S(2)}) collective-permute-start(bf16[128,128]{1,0:T(8,128)(2,1)S(1)} %get-tuple-element.27), channel_id=1, source_target_pairs={{0,64},{32,96},{64,128},{96,160},{128,192},{160,224},{192,0},{224,... | collective-permute-start | bytes 98312 | tf_op jit(solution)/shard_map/ppermute | solution.py:31
  43.3 3.4 %collective-permute-done.9.in2 = bf16[128,128]{1,0:T(8,128)(2,1)S(1)} collective-permute-done((bf16[128,128]{1,0:T(8,128)(2,1)S(1)}, bf16[128,128]{1,0:T(8,128)(2,1)S(1)}, u32[]{:S(2)}, u32[]{:S(2)}) %collective-permute-start.9) | collective-permute-done | bytes 32800 | tf_op jit(solution)/shard_map/ppermute | solution.py:31
  46.7 1.5 %middle.1 = (bf16[128,512]{1,0:T(8,128)(2,1)}, bf16[4,288,128]{2,1,0:T(8,128)(2,1)S(1)}, f32[160,128]{1,0:T(8,128)S(1)}) custom-call(s32[2]{0:T(128)S(1)} %pad_add_fusion.place, f32[128,128]{1,0:T(8,128)S(1)} %slice_bitcast_fusion.3.own, bf16[128,128]{1,0:T(8,128)(2,1)S(1)} %collective-permute-done.8.in1, bf16[128,128]{1,0:T(8,128)(2,1)S(1)} %collective-permute-done.9.in2, ...), custom_call_target="tpu_custom_call" | custom-call | flops 83886080 | bytes 655360 | tf_op jit(solution)/shard_map/middle/pallas_call | solution.py:131
  48.5 3.3 %collective-permute-start.13 = (bf16[288,128]{1,0:T(8,128)(2,1)S(1)}, bf16[288,128]{1,0:T(8,128)(2,1)S(1)}, u32[]{:S(2)}, u32[]{:S(2)}) collective-permute-start(bf16[288,128]{1,0:T(8,128)(2,1)S(1)} %get-tuple-element.20), channel_id=1, source_target_pairs={{0,192},{32,224},{64,0},{96,32},{128,64},{160,96},{192,128},{224,1... | collective-permute-start | bytes 221192 | tf_op jit(solution)/shard_map/ppermute | solution.py:31
  51.9 3.6 %collective-permute-start.12 = (bf16[288,128]{1,0:T(8,128)(2,1)S(1)}, bf16[288,128]{1,0:T(8,128)(2,1)S(1)}, u32[]{:S(2)}, u32[]{:S(2)}) collective-permute-start(bf16[288,128]{1,0:T(8,128)(2,1)S(1)} %get-tuple-element.21), channel_id=1, source_target_pairs={{0,128},{32,160},{64,192},{96,224},{128,0},{160,32},{192,64},{224,... | collective-permute-start | bytes 221192 | tf_op jit(solution)/shard_map/ppermute | solution.py:31
  55.4 4.5 %collective-permute-done.12 = bf16[288,128]{1,0:T(8,128)(2,1)S(1)} collective-permute-done((bf16[288,128]{1,0:T(8,128)(2,1)S(1)}, bf16[288,128]{1,0:T(8,128)(2,1)S(1)}, u32[]{:S(2)}, u32[]{:S(2)}) %collective-permute-start.12) | collective-permute-done | bytes 73760 | tf_op jit(solution)/shard_map/ppermute | solution.py:31
  60.1 3.4 %collective-permute-start.14 = (bf16[672,128]{1,0:T(8,128)(2,1)S(1)}, bf16[672,128]{1,0:T(8,128)(2,1)S(1)}, u32[]{:S(2)}, u32[]{:S(2)}) collective-permute-start(bf16[672,128]{1,0:T(8,128)(2,1)S(1)} %constant_dynamic-update-slice_fusion), channel_id=1, source_target_pairs={{0,32},{32,0},{64,96},{96,64},{128,160},{160,128},{192,224},{224,1... | collective-permute-start | bytes 516104 | tf_op jit(solution)/shard_map/ppermute | solution.py:39
  63.5 1.0 %collective-permute-done.14 = bf16[672,128]{1,0:T(8,128)(2,1)S(1)} collective-permute-done((bf16[672,128]{1,0:T(8,128)(2,1)S(1)}, bf16[672,128]{1,0:T(8,128)(2,1)S(1)}, u32[]{:S(2)}, u32[]{:S(2)}) %collective-permute-start.14) | collective-permute-done | bytes 172064 | tf_op jit(solution)/shard_map/ppermute | solution.py:39
  65.2 2.4 %fusion.16 = (bf16[4096,128]{1,0:T(8,128)(2,1)S(1)}, f32[4096,128]{1,0:T(8,128)S(1)}) fusion(bf16[1024,4096]{1,0:T(8,128)(2,1)S(1)} %spread.1, bf16[1024,128]{1,0:T(8,128)(2,1)S(1)} %slice_dynamic-update-slice_fusion), kind=kOutput, calls=%fused_computation.94 | convolution fusion | flops 1074266112 | bytes 11796480 | tf_op jit(solution)/shard_map/dot_general | solution.py:210
  67.8 1.4 %collective-permute-start.17 = (bf16[1104,128]{1,0:T(8,128)(2,1)S(1)}, bf16[1104,128]{1,0:T(8,128)(2,1)S(1)}, u32[]{:S(2)}, u32[]{:S(2)}) collective-permute-start(bf16[1104,128]{1,0:T(8,128)(2,1)S(1)} %get-tuple-element.42), channel_id=1, source_target_pairs={{0,16},{1,17},{2,18},{3,19},{4,20},{5,21},{6,22},{7,23},{8,24},{9,... | collective-permute-start | bytes 847880 | tf_op jit(solution)/shard_map/ppermute | solution.py:27
  69.3 1.6 %collective-permute-start.16 = (bf16[1104,128]{1,0:T(8,128)(2,1)S(1)}, bf16[1104,128]{1,0:T(8,128)(2,1)S(1)}, u32[]{:S(2)}, u32[]{:S(2)}) collective-permute-start(bf16[1104,128]{1,0:T(8,128)(2,1)S(1)} %get-tuple-element.41), channel_id=1, source_target_pairs={{0,24},{1,25},{2,26},{3,27},{4,28},{5,29},{6,30},{7,31},{8,0},{9,1... | collective-permute-start | bytes 847880 | tf_op jit(solution)/shard_map/ppermute | solution.py:27
  70.9 6.9 %collective-permute-done.18 = bf16[1104,128]{1,0:T(8,128)(2,1)S(1)} collective-permute-done((bf16[1104,128]{1,0:T(8,128)(2,1)S(1)}, bf16[1104,128]{1,0:T(8,128)(2,1)S(1)}, u32[]{:S(2)}, u32[]{:S(2)}) %collective-permute-start.18) | collective-permute-done | bytes 282656 | tf_op jit(solution)/shard_map/ppermute | solution.py:27
  78.7 1.5 %collective-permute-start.20 = (bf16[336,128]{1,0:T(8,128)(2,1)S(1)}, bf16[336,128]{1,0:T(8,128)(2,1)S(1)}, u32[]{:S(2)}, u32[]{:S(2)}) collective-permute-start(bf16[336,128]{1,0:T(8,128)(2,1)S(1)} %get-tuple-element.39), channel_id=1, source_target_pairs={{0,4},{1,5},{2,6},{3,7},{4,0},{5,1},{6,2},{7,3},{8,12},{9,13},{10,... | collective-permute-start | bytes 258056 | tf_op jit(solution)/shard_map/ppermute | solution.py:27
  80.2 1.2 %collective-permute-start.19 = (bf16[336,128]{1,0:T(8,128)(2,1)S(1)}, bf16[336,128]{1,0:T(8,128)(2,1)S(1)}, u32[]{:S(2)}, u32[]{:S(2)}) collective-permute-start(bf16[336,128]{1,0:T(8,128)(2,1)S(1)} %get-tuple-element.38), channel_id=1, source_target_pairs={{0,6},{1,7},{2,0},{3,1},{4,2},{5,3},{6,4},{7,5},{8,14},{9,15},{10,... | collective-permute-start | bytes 258056 | tf_op jit(solution)/shard_map/ppermute | solution.py:27
  81.4 2.8 %collective-permute-done.21 = bf16[336,128]{1,0:T(8,128)(2,1)S(1)} collective-permute-done((bf16[336,128]{1,0:T(8,128)(2,1)S(1)}, bf16[336,128]{1,0:T(8,128)(2,1)S(1)}, u32[]{:S(2)}, u32[]{:S(2)}) %collective-permute-start.21) | collective-permute-done | bytes 86048 | tf_op jit(solution)/shard_map/ppermute | solution.py:27
  85.8 2.6 %collective-permute-done.23 = bf16[64,128]{1,0:T(8,128)(2,1)S(1)} collective-permute-done((bf16[64,128]{1,0:T(8,128)(2,1)S(1)}, bf16[64,128]{1,0:T(8,128)(2,1)S(1)}, u32[]{:S(2)}, u32[]{:S(2)}) %collective-permute-start.23) | collective-permute-done | bytes 16416 | tf_op jit(solution)/shard_map/ppermute | solution.py:35
  88.4 1.4 %collective-permute-start.24 = (bf16[128,128]{1,0:T(8,128)(2,1)S(1)}, bf16[128,128]{1,0:T(8,128)(2,1)S(1)}, u32[]{:S(2)}, u32[]{:S(2)}) collective-permute-start(bf16[128,128]{1,0:T(8,128)(2,1)S(1)} %pad_maximum_fusion.10), channel_id=1, source_target_pairs={{0,192},{32,224},{64,128},{96,160},{128,64},{160,96},{192,0},{224,... | collective-permute-start | bytes 98312 | tf_op jit(solution)/shard_map/ppermute | solution.py:35
  90.3 1.4 %collective-permute-start.22 = (bf16[128,128]{1,0:T(8,128)(2,1)S(1)}, bf16[128,128]{1,0:T(8,128)(2,1)S(1)}, u32[]{:S(2)}, u32[]{:S(2)}) collective-permute-start(bf16[128,128]{1,0:T(8,128)(2,1)S(1)} %slice.295), channel_id=1, source_target_pairs={{0,1},{1,0},{2,3},{3,2},{4,5},{5,4},{6,7},{7,6},{8,9},{9,8},{10,11... | collective-permute-start | bytes 98312 | tf_op jit(solution)/shard_map/ppermute | solution.py:43
  91.8 1.6 %collective-permute-done.24 = bf16[128,128]{1,0:T(8,128)(2,1)S(1)} collective-permute-done((bf16[128,128]{1,0:T(8,128)(2,1)S(1)}, bf16[128,128]{1,0:T(8,128)(2,1)S(1)}, u32[]{:S(2)}, u32[]{:S(2)}) %collective-permute-start.24) | collective-permute-done | bytes 32800 | tf_op jit(solution)/shard_map/ppermute | solution.py:35
  93.3 6.1 %collective-permute-start.25 = (bf16[256,128]{1,0:T(8,128)(2,1)S(1)}, bf16[256,128]{1,0:T(8,128)(2,1)S(1)}, u32[]{:S(2)}, u32[]{:S(2)}) collective-permute-start(bf16[256,128]{1,0:T(8,128)(2,1)S(1)} %pad_maximum_fusion.9.near), channel_id=1, source_target_pairs={{0,32},{32,0},{64,96},{96,64},{128,160},{160,128},{192,224},{224,1... | collective-permute-start | bytes 196616 | tf_op jit(solution)/shard_map/ppermute | solution.py:39
  100.3 1.3 %settle.1 = f32[128,512]{1,0:T(8,128)} custom-call(s32[2]{0:T(128)S(1)} %pad_add_fusion.place, bf16[256,128]{1,0:T(8,128)(2,1)S(1)} %pad_maximum_fusion.9.near, bf16[256,128]{1,0:T(8,128)(2,1)S(1)} %collective-permute-done.25.far), custom_call_target="tpu_custom_call" | custom-call | tf_op jit(solution)/shard_map/settle/pallas_call | solution.py:164
  (68 shorter events, 12.7 us)
Async XLA Ops:
  0.6 4.1 %collective-permute-start = (bf16[128,128]{1,0:T(8,128)(2,1)}, bf16[128,128]{1,0:T(8,128)(2,1)S(1)}, u32[]{:S(2)}, u32[]{:S(2)}) collective-permute-start(bf16[128,128]{1,0:T(8,128)(2,1)} %param.7), channel_id=1, source_target_pairs={{0,1},{1,0},{2,3},{3,2},{4,5},{5,4},{6,7},{7,6},{8,9},{9,8},{10,11... | collective-permute-start | bytes 98312 | tf_op jit(solution)/shard_map/ppermute | solution.py:43
  5.5 3.9 %collective-permute-start.3 = (bf16[2,128,128]{2,1,0:T(8,128)(2,1)S(1)}, bf16[2,128,128]{2,1,0:T(8,128)(2,1)S(1)}, u32[]{:S(2)}, u32[]{:S(2)}) collective-permute-start(bf16[2,128,128]{2,1,0:T(8,128)(2,1)S(1)} %get-tuple-element.37), channel_id=1, source_target_pairs={{0,6},{1,7},{2,0},{3,1},{4,2},{5,3},{6,4},{7,5},{8,14},{9,15},{10,... | collective-permute-start | bytes 196616 | tf_op jit(solution)/shard_map/ppermute | solution.py:27
  8.0 4.7 %collective-permute-start.2 = (bf16[2,128,128]{2,1,0:T(8,128)(2,1)S(1)}, bf16[2,128,128]{2,1,0:T(8,128)(2,1)S(1)}, u32[]{:S(2)}, u32[]{:S(2)}) collective-permute-start(bf16[2,128,128]{2,1,0:T(8,128)(2,1)S(1)} %get-tuple-element.37), channel_id=1, source_target_pairs={{0,4},{1,5},{2,6},{3,7},{4,0},{5,1},{6,2},{7,3},{8,12},{9,13},{10,... | collective-permute-start | bytes 196616 | tf_op jit(solution)/shard_map/ppermute | solution.py:27
  8.5 4.8 %collective-permute-start.1 = (bf16[2,128,128]{2,1,0:T(8,128)(2,1)S(1)}, bf16[2,128,128]{2,1,0:T(8,128)(2,1)S(1)}, u32[]{:S(2)}, u32[]{:S(2)}) collective-permute-start(bf16[2,128,128]{2,1,0:T(8,128)(2,1)S(1)} %get-tuple-element.37), channel_id=1, source_target_pairs={{0,2},{1,3},{2,4},{3,5},{4,6},{5,7},{6,0},{7,1},{8,10},{9,11},{10,... | collective-permute-start | bytes 196616 | tf_op jit(solution)/shard_map/ppermute | solution.py:27
  13.4 8.9 %collective-permute-start.6 = (bf16[4,2,128,128]{3,2,1,0:T(8,128)(2,1)S(1)}, bf16[4,2,128,128]{3,2,1,0:T(8,128)(2,1)S(1)}, u32[]{:S(2)}, u32[]{:S(2)}) collective-permute-start(bf16[4,2,128,128]{3,2,1,0:T(8,128)(2,1)S(1)} %get-tuple-element.26), channel_id=1, source_target_pairs={{0,24},{1,25},{2,26},{3,27},{4,28},{5,29},{6,30},{7,31},{8,0},{9,1... | collective-permute-start | bytes 786440 | tf_op jit(solution)/shard_map/ppermute | solution.py:27
  16.2 6.8 %collective-permute-start.5 = (bf16[4,2,128,128]{3,2,1,0:T(8,128)(2,1)S(1)}, bf16[4,2,128,128]{3,2,1,0:T(8,128)(2,1)S(1)}, u32[]{:S(2)}, u32[]{:S(2)}) collective-permute-start(bf16[4,2,128,128]{3,2,1,0:T(8,128)(2,1)S(1)} %get-tuple-element.26), channel_id=1, source_target_pairs={{0,16},{1,17},{2,18},{3,19},{4,20},{5,21},{6,22},{7,23},{8,24},{9,... | collective-permute-start | bytes 786440 | tf_op jit(solution)/shard_map/ppermute | solution.py:27
  16.6 9.5 %collective-permute-start.4 = (bf16[4,2,128,128]{3,2,1,0:T(8,128)(2,1)S(1)}, bf16[4,2,128,128]{3,2,1,0:T(8,128)(2,1)S(1)}, u32[]{:S(2)}, u32[]{:S(2)}) collective-permute-start(bf16[4,2,128,128]{3,2,1,0:T(8,128)(2,1)S(1)} %get-tuple-element.26), channel_id=1, source_target_pairs={{0,8},{1,9},{2,10},{3,11},{4,12},{5,13},{6,14},{7,15},{8,16},{9,17... | collective-permute-start | bytes 786440 | tf_op jit(solution)/shard_map/ppermute | solution.py:27
  18.6 2.2 %copy-start = (bf16[1,1,128,128,128]{4,3,2,1,0:T(8,128)(2,1)S(1)}, bf16[1,1,128,128,128]{4,3,2,1,0:T(8,128)(2,1)}, u32[]{:S(2)}) copy-start(bf16[1,1,128,128,128]{4,3,2,1,0:T(8,128)(2,1)} %param.10) | copy-start | bytes 12582916
  22.3 24.4 %copy-start.1 = (bf16[128,512]{1,0:T(8,128)(2,1)S(1)}, bf16[128,512]{1,0:T(8,128)(2,1)}, u32[]{:S(2)}) copy-start(bf16[128,512]{1,0:T(8,128)(2,1)} %weight.1) | copy-start | bytes 393220
  22.3 24.4 %copy-start.2 = (bf16[128,512]{1,0:T(8,128)(2,1)S(1)}, bf16[128,512]{1,0:T(8,128)(2,1)}, u32[]{:S(2)}) copy-start(bf16[128,512]{1,0:T(8,128)(2,1)} %cot.1) | copy-start | bytes 393220
  22.3 24.4 %copy-start.3 = (f32[512]{0:T(512)S(1)}, f32[512]{0:T(512)}, u32[]{:S(2)}) copy-start(f32[512]{0:T(512)} %param.9) | copy-start | bytes 6148
  28.5 5.3 %collective-permute-start.7 = (bf16[4,128,128]{2,1,0:T(8,128)(2,1)S(1)}, bf16[4,128,128]{2,1,0:T(8,128)(2,1)S(1)}, u32[]{:S(2)}, u32[]{:S(2)}) collective-permute-start(bf16[4,128,128]{2,1,0:T(8,128)(2,1)S(1)} %bitcast.68), channel_id=1, source_target_pairs={{0,32},{32,0},{64,96},{96,64},{128,160},{160,128},{192,224},{224,1... | collective-permute-start | bytes 393224 | tf_op jit(solution)/shard_map/ppermute | solution.py:39
  33.9 9.4 %collective-permute-start.8 = (bf16[128,128]{1,0:T(8,128)(2,1)S(1)}, bf16[128,128]{1,0:T(8,128)(2,1)S(1)}, u32[]{:S(2)}, u32[]{:S(2)}) collective-permute-start(bf16[128,128]{1,0:T(8,128)(2,1)S(1)} %get-tuple-element.29), channel_id=1, source_target_pairs={{0,192},{32,224},{64,0},{96,32},{128,64},{160,96},{192,128},{224,1... | collective-permute-start | bytes 98312 | tf_op jit(solution)/shard_map/ppermute | solution.py:31
  40.0 6.7 %collective-permute-start.9 = (bf16[128,128]{1,0:T(8,128)(2,1)S(1)}, bf16[128,128]{1,0:T(8,128)(2,1)S(1)}, u32[]{:S(2)}, u32[]{:S(2)}) collective-permute-start(bf16[128,128]{1,0:T(8,128)(2,1)S(1)} %get-tuple-element.28), channel_id=1, source_target_pairs={{0,128},{32,160},{64,192},{96,224},{128,0},{160,32},{192,64},{224,... | collective-permute-start | bytes 98312 | tf_op jit(solution)/shard_map/ppermute | solution.py:31
  41.0 5.7 %collective-permute-start.10 = (bf16[128,128]{1,0:T(8,128)(2,1)S(1)}, bf16[128,128]{1,0:T(8,128)(2,1)S(1)}, u32[]{:S(2)}, u32[]{:S(2)}) collective-permute-start(bf16[128,128]{1,0:T(8,128)(2,1)S(1)} %get-tuple-element.27), channel_id=1, source_target_pairs={{0,64},{32,96},{64,128},{96,160},{128,192},{160,224},{192,0},{224,... | collective-permute-start | bytes 98312 | tf_op jit(solution)/shard_map/ppermute | solution.py:31
  48.2 7.2 %collective-permute-start.11 = (bf16[288,128]{1,0:T(8,128)(2,1)S(1)}, bf16[288,128]{1,0:T(8,128)(2,1)S(1)}, u32[]{:S(2)}, u32[]{:S(2)}) collective-permute-start(bf16[288,128]{1,0:T(8,128)(2,1)S(1)} %get-tuple-element.19), channel_id=1, source_target_pairs={{0,64},{32,96},{64,128},{96,160},{128,192},{160,224},{192,0},{224,... | collective-permute-start | bytes 221192 | tf_op jit(solution)/shard_map/ppermute | solution.py:31
  48.5 6.9 %collective-permute-start.13 = (bf16[288,128]{1,0:T(8,128)(2,1)S(1)}, bf16[288,128]{1,0:T(8,128)(2,1)S(1)}, u32[]{:S(2)}, u32[]{:S(2)}) collective-permute-start(bf16[288,128]{1,0:T(8,128)(2,1)S(1)} %get-tuple-element.20), channel_id=1, source_target_pairs={{0,192},{32,224},{64,0},{96,32},{128,64},{160,96},{192,128},{224,1... | collective-permute-start | bytes 221192 | tf_op jit(solution)/shard_map/ppermute | solution.py:31
  51.9 8.1 %collective-permute-start.12 = (bf16[288,128]{1,0:T(8,128)(2,1)S(1)}, bf16[288,128]{1,0:T(8,128)(2,1)S(1)}, u32[]{:S(2)}, u32[]{:S(2)}) collective-permute-start(bf16[288,128]{1,0:T(8,128)(2,1)S(1)} %get-tuple-element.21), channel_id=1, source_target_pairs={{0,128},{32,160},{64,192},{96,224},{128,0},{160,32},{192,64},{224,... | collective-permute-start | bytes 221192 | tf_op jit(solution)/shard_map/ppermute | solution.py:31
  60.1 4.4 %collective-permute-start.14 = (bf16[672,128]{1,0:T(8,128)(2,1)S(1)}, bf16[672,128]{1,0:T(8,128)(2,1)S(1)}, u32[]{:S(2)}, u32[]{:S(2)}) collective-permute-start(bf16[672,128]{1,0:T(8,128)(2,1)S(1)} %constant_dynamic-update-slice_fusion), channel_id=1, source_target_pairs={{0,32},{32,0},{64,96},{96,64},{128,160},{160,128},{192,224},{224,1... | collective-permute-start | bytes 516104 | tf_op jit(solution)/shard_map/ppermute | solution.py:39
  64.5 3.1 %collective-permute-start.15 = (f32[80,128]{1,0:T(8,128)S(1)}, f32[80,128]{1,0:T(8,128)S(1)}, u32[]{:S(2)}, u32[]{:S(2)}) collective-permute-start(f32[80,128]{1,0:T(8,128)S(1)} %slice_add_fusion.3), channel_id=1, source_target_pairs={{0,1},{1,0},{2,3},{3,2},{4,5},{5,4},{6,7},{7,6},{8,9},{9,8},{10,11... | collective-permute-start | bytes 122888 | tf_op jit(solution)/shard_map/ppermute | solution.py:43
  67.7 10.1 %collective-permute-start.18 = (bf16[1104,128]{1,0:T(8,128)(2,1)S(1)}, bf16[1104,128]{1,0:T(8,128)(2,1)S(1)}, u32[]{:S(2)}, u32[]{:S(2)}) collective-permute-start(bf16[1104,128]{1,0:T(8,128)(2,1)S(1)} %get-tuple-element.43), channel_id=1, source_target_pairs={{0,8},{1,9},{2,10},{3,11},{4,12},{5,13},{6,14},{7,15},{8,16},{9,17... | collective-permute-start | bytes 847880 | tf_op jit(solution)/shard_map/ppermute | solution.py:27
  67.8 10.0 %collective-permute-start.17 = (bf16[1104,128]{1,0:T(8,128)(2,1)S(1)}, bf16[1104,128]{1,0:T(8,128)(2,1)S(1)}, u32[]{:S(2)}, u32[]{:S(2)}) collective-permute-start(bf16[1104,128]{1,0:T(8,128)(2,1)S(1)} %get-tuple-element.42), channel_id=1, source_target_pairs={{0,16},{1,17},{2,18},{3,19},{4,20},{5,21},{6,22},{7,23},{8,24},{9,... | collective-permute-start | bytes 847880 | tf_op jit(solution)/shard_map/ppermute | solution.py:27
  69.3 9.1 %collective-permute-start.16 = (bf16[1104,128]{1,0:T(8,128)(2,1)S(1)}, bf16[1104,128]{1,0:T(8,128)(2,1)S(1)}, u32[]{:S(2)}, u32[]{:S(2)}) collective-permute-start(bf16[1104,128]{1,0:T(8,128)(2,1)S(1)} %get-tuple-element.41), channel_id=1, source_target_pairs={{0,24},{1,25},{2,26},{3,27},{4,28},{5,29},{6,30},{7,31},{8,0},{9,1... | collective-permute-start | bytes 847880 | tf_op jit(solution)/shard_map/ppermute | solution.py:27
  78.6 5.5 %collective-permute-start.21 = (bf16[336,128]{1,0:T(8,128)(2,1)S(1)}, bf16[336,128]{1,0:T(8,128)(2,1)S(1)}, u32[]{:S(2)}, u32[]{:S(2)}) collective-permute-start(bf16[336,128]{1,0:T(8,128)(2,1)S(1)} %get-tuple-element.40), channel_id=1, source_target_pairs={{0,2},{1,3},{2,4},{3,5},{4,6},{5,7},{6,0},{7,1},{8,10},{9,11},{10,... | collective-permute-start | bytes 258056 | tf_op jit(solution)/shard_map/ppermute | solution.py:27
  78.7 5.5 %collective-permute-start.20 = (bf16[336,128]{1,0:T(8,128)(2,1)S(1)}, bf16[336,128]{1,0:T(8,128)(2,1)S(1)}, u32[]{:S(2)}, u32[]{:S(2)}) collective-permute-start(bf16[336,128]{1,0:T(8,128)(2,1)S(1)} %get-tuple-element.39), channel_id=1, source_target_pairs={{0,4},{1,5},{2,6},{3,7},{4,0},{5,1},{6,2},{7,3},{8,12},{9,13},{10,... | collective-permute-start | bytes 258056 | tf_op jit(solution)/shard_map/ppermute | solution.py:27
  80.2 4.5 %collective-permute-start.19 = (bf16[336,128]{1,0:T(8,128)(2,1)S(1)}, bf16[336,128]{1,0:T(8,128)(2,1)S(1)}, u32[]{:S(2)}, u32[]{:S(2)}) collective-permute-start(bf16[336,128]{1,0:T(8,128)(2,1)S(1)} %get-tuple-element.38), channel_id=1, source_target_pairs={{0,6},{1,7},{2,0},{3,1},{4,2},{5,3},{6,4},{7,5},{8,14},{9,15},{10,... | collective-permute-start | bytes 258056 | tf_op jit(solution)/shard_map/ppermute | solution.py:27
  84.8 3.6 %collective-permute-start.23 = (bf16[64,128]{1,0:T(8,128)(2,1)S(1)}, bf16[64,128]{1,0:T(8,128)(2,1)S(1)}, u32[]{:S(2)}, u32[]{:S(2)}) collective-permute-start(bf16[64,128]{1,0:T(8,128)(2,1)S(1)} %slice.296), channel_id=1, source_target_pairs={{0,64},{32,96},{64,0},{96,32},{128,192},{160,224},{192,128},{224,1... | collective-permute-start | bytes 49160 | tf_op jit(solution)/shard_map/ppermute | solution.py:35
  88.4 5.0 %collective-permute-start.24 = (bf16[128,128]{1,0:T(8,128)(2,1)S(1)}, bf16[128,128]{1,0:T(8,128)(2,1)S(1)}, u32[]{:S(2)}, u32[]{:S(2)}) collective-permute-start(bf16[128,128]{1,0:T(8,128)(2,1)S(1)} %pad_maximum_fusion.10), channel_id=1, source_target_pairs={{0,192},{32,224},{64,128},{96,160},{128,64},{160,96},{192,0},{224,... | collective-permute-start | bytes 98312 | tf_op jit(solution)/shard_map/ppermute | solution.py:35
  90.3 9.1 %collective-permute-start.22 = (bf16[128,128]{1,0:T(8,128)(2,1)S(1)}, bf16[128,128]{1,0:T(8,128)(2,1)S(1)}, u32[]{:S(2)}, u32[]{:S(2)}) collective-permute-start(bf16[128,128]{1,0:T(8,128)(2,1)S(1)} %slice.295), channel_id=1, source_target_pairs={{0,1},{1,0},{2,3},{3,2},{4,5},{5,4},{6,7},{7,6},{8,9},{9,8},{10,11... | collective-permute-start | bytes 98312 | tf_op jit(solution)/shard_map/ppermute | solution.py:43
  93.3 7.0 %collective-permute-start.25 = (bf16[256,128]{1,0:T(8,128)(2,1)S(1)}, bf16[256,128]{1,0:T(8,128)(2,1)S(1)}, u32[]{:S(2)}, u32[]{:S(2)}) collective-permute-start(bf16[256,128]{1,0:T(8,128)(2,1)S(1)} %pad_maximum_fusion.9.near), channel_id=1, source_target_pairs={{0,32},{32,0},{64,96},{96,64},{128,160},{160,128},{192,224},{224,1... | collective-permute-start | bytes 196616 | tf_op jit(solution)/shard_map/ppermute | solution.py:39

commit v2 on v1

--- a/solution.py
+++ b/solution.py
@@ -9,26 +9,17 @@
 VMEM = pltpu.VMEM
 
 
-def ring(i, count, inner, step):
-    digit = (i // inner) % count
-    return i + ((digit + step) % count - digit) * inner
-
-
 def mirror(i, count, inner, mask):
     digit = (i // inner) % count
     return i + ((digit ^ mask) - digit) * inner
 
 
-def move_xy(v, step, turn):
+def swap_xy(v, mask, turn):
     pairs = []
     for i in range(256):
         row, col = i // 32, i % 32
-        pairs.append((i, row * 32 + ring(col, 4, 2 if row % 2 == turn else 8, step)))
+        pairs.append((i, row * 32 + mirror(col, 4, 2 if row % 2 == turn else 8, mask)))
     return lax.ppermute(v, ("row", "col"), pairs)
-
-
-def move_h(v, step):
-    return lax.ppermute(v, "row", [(i, ring(i, 4, 2, step)) for i in range(8)])
 
 
 def swap_h(v, mask):
@@ -108,16 +99,19 @@
     rows = whole.shape[0] // 8
     tail = jnp.concatenate(
         [sums[:, j * lanes : (j + 1) * lanes] for j in range(blocks)]
-        + [jnp.zeros((rows - blocks, lanes), F32)]
+        + [jnp.zeros((16 - blocks, lanes), F32)]
     )
+    last = 2 * blocks * rows
+    gw_ref[last:, :] = tail
     for h in range(4):
         sent_ref[h, :size, :] = back
+        sent_ref[h, size + last :, :] = tail.astype(BF)
         for k in range(2):
-            at = (lax.rem(place[0] + h, 4) * 2 + (place[1] ^ k)) * rows
+            at = ((place[0] ^ h) * 2 + (place[1] ^ k)) * rows
             at = pl.ds(pl.multiple_of(at, rows), rows)
-            for j in range(blocks + 1):
-                piece = whole[at, j * lanes : (j + 1) * lanes] if j < blocks else tail
-                to = (k * (blocks + 1) + j) * rows
+            for j in range(blocks):
+                piece = whole[at, j * lanes : (j + 1) * lanes]
+                to = (k * blocks + j) * rows
                 sent_ref[h, size + to : size + to + rows, :] = piece.astype(BF)
                 if h == 0:
                     gw_ref[to : to + rows, :] = piece
@@ -126,7 +120,7 @@
 def middle(place, own, arrived, weight, bias, cotangent):
     size, width = cotangent.shape
     feats = weight.shape[0]
-    share = (feats // 4) * (width // feats + 1)
+    share = (feats // 4) * (width // feats) + 16
     vmem = pl.BlockSpec(memory_space=VMEM)
     return pl.pallas_call(
         middle_kernel,
@@ -151,8 +145,8 @@
     blocks = out_ref.shape[1] // lanes
     rows = near.shape[0] // 4 // blocks
     for k, part in ((0, near), (1, far)):
-        for first, bits in enumerate((0, 1, 3, 2)):
-            at = ((place[0] ^ bits) * 2 + (place[1] ^ k)) * rows
+        for first in range(4):
+            at = ((place[0] ^ first) * 2 + (place[1] ^ k)) * rows
             at = pl.ds(pl.multiple_of(at, rows), rows)
             for j in range(blocks):
                 start = (first * blocks + j) * rows
@@ -181,29 +175,31 @@
     here = jnp.stack([h, k]).astype(jnp.int32)
 
     tile_row, tile_col = places // 32, places % 32
-    far_h, far_k = (h - tile_row // 2) % 4, (k - tile_row) % 2
-    far_x, far_y, far_z = (x - tile_col // 8) % 4, (y - tile_col // 2) % 4, (z - tile_col) % 2
+    far_h, far_k = h ^ (tile_row // 2), k ^ (tile_row % 2)
+    far_x, far_y, far_z = x ^ (tile_col // 8), y ^ ((tile_col // 2) % 4), z ^ (tile_col % 2)
     put_row = (far_k * 4 + far_h).astype(jnp.int32)
-    put_col = (jnp.where(k == 0, far_x * 4 + far_y, far_y * 4 + far_x) * 2 + far_z).astype(jnp.int32)
+    first, second = jnp.where(k == 0, far_y, far_x), jnp.where(k == 0, far_x, far_y)
+    put_col = (second * 8 + first * 2 + far_z).astype(jnp.int32)
     dense = spread(tile_values[0, 0], tile_count[0], put_row, put_col, 8, 32)
 
     source = jnp.stack([features, swap_z(features)])
     for turn in (0, 1):
-        source = jnp.stack([source] + [move_xy(source, s, turn) for s in (1, 2, 3)])
+        source = jnp.stack([source] + [swap_xy(source, bits, turn) for bits in (1, 2, 3)])
     source = source.reshape(-1, feats)
 
     part = jnp.dot(dense, source, preferred_element_type=F32).reshape(2, 4, size, feats)
     half = part[0] + swap_k(part[1].astype(BF)).astype(F32)
     sent = half.astype(BF)
-    arrived = [move_h(sent[s], -s) for s in (1, 2, 3)]
+    arrived = [swap_h(sent[s], s) for s in (1, 2, 3)]
     hidden_out, sent, gw = middle(here, half[0], arrived, weight, bias, cotangent)
 
-    arrived = [move_h(sent[s], s) for s in (1, 2, 3)]
+    arrived = [swap_h(sent[s], s) for s in (1, 2, 3)]
     target = jnp.concatenate([sent[0][:size]] + [v[:size] for v in arrived])
     gw = gw + sum(v[size:].astype(F32) for v in arrived)
-    share = gw.shape[0] // 2
-    arrived = swap_k(jnp.concatenate([target, pair(gw[share:])]))
-    gw = gw[:share] + unpair(arrived[4 * size :])
+    share = (gw.shape[0] - 16) // 2
+    own, other, sums = gw[:share], gw[share : 2 * share], gw[2 * share :]
+    arrived = swap_k(jnp.concatenate([target, pair(jnp.concatenate([other, sums]))]))
+    gw = jnp.concatenate([own, unpair(pair(sums))]) + unpair(arrived[4 * size :])
     target = jnp.concatenate([target, arrived[: 4 * size]])
     gw = gw + swap_z(gw)
 
@@ -212,17 +208,15 @@
         grad = grad.reshape(4, -1, feats)
         rows = grad.shape[1]
         low, extra = grad.astype(BF), gw.astype(BF)
-        arrived = [move_xy(jnp.concatenate([low[s], extra]), -s, turn) for s in (1, 2, 3)]
+        arrived = [swap_xy(jnp.concatenate([low[s], extra]), s, turn) for s in (1, 2, 3)]
         grad = grad[0] + sum(v[:rows].astype(F32) for v in arrived)
         one, two, three = [v[rows:].astype(F32) for v in arrived]
         gw = (extra.astype(F32) + two) + (one + three)
     grad_features = (grad[:size] + swap_z(grad[size:].astype(BF)).astype(F32)).astype(BF)
 
-    share = share * width // (width + feats)
     grad_bias = gw[share : share + width // feats].reshape(width)
     gw = gw[:share].astype(BF)
-    gw = jnp.concatenate([gw, swap_h(gw, 1)])
-    gw = jnp.concatenate([gw, swap_h(gw, 3)])
+    gw = jnp.concatenate([gw] + [swap_h(gw, s) for s in (1, 2, 3)])
     grad_weight = settle(here, gw, swap_k(gw), feats, width)
     return (hidden_out, grad_features, grad_weight, grad_bias)
 

time: 102 us -> 97.1 us (0.952)
  waiting for transfers between devices: 34.6 us -> 31.3 us
  starting transfers between devices: 50.7 us -> 49.1 us
    ppermute x2 -> x9, starting transfers between devices: 2.33 us -> 19.7 us  [swap_h(): lax.ppermute(v, 'row', [(i, mirror(i, 4, 2, mask)) for i in range(8)])]
    ppermute x18 -> x12, starting transfers between devices: 30 us -> 13.5 us  [swap_xy(): return lax.ppermute(v, ('row', 'col'), pairs)]
    ppermute x18 -> x12, waiting for transfers between devices: 26.7 us -> 16.9 us  [swap_xy(): return lax.ppermute(v, ('row', 'col'), pairs)]
    ppermute x2 -> x9, waiting for transfers between devices: 4.15 us -> 10.4 us  [swap_h(): lax.ppermute(v, 'row', [(i, mirror(i, 4, 2, mask)) for i in range(8)])]
    ppermute x3, starting transfers between devices: 13.8 us -> 12 us  [swap_k(): return lax.ppermute(v, 'row', [(i, i ^ 1) for i in range(8)])]
  transfers between devices with their start and end apart: 26 -> 27, of which waited for: 17 -> 19; matrix products, arithmetic and copies ran while one was open for 4% -> 5% of each run, Pallas kernels for 1% -> 2%
where the time goes in v2:
time: 97.1 us; the launch traced here: 96.9 us
  starting transfers between devices  49.1 us (51%)
  waiting for transfers between devices  31.3 us (32%)
  matrix products  4.76 us (5%)
  Pallas kernels  4.45 us (5%)
  local copies, waits for them, and re-layouts  3.01 us (3%)
  other arithmetic  2.71 us (3%)
  between operations  1.56 us (2%)
    ppermute x9, starting transfers between devices, swap_h(): lax.ppermute(v, 'row', [(i, mirror(i, 4, 2, mask)) for i in range(8)])  19.7 us
    ppermute x12, waiting for transfers between devices, swap_xy(): return lax.ppermute(v, ('row', 'col'), pairs)  16.9 us
    ppermute x12, starting transfers between devices, swap_xy(): return lax.ppermute(v, ('row', 'col'), pairs)  13.5 us
    ppermute x3, starting transfers between devices, swap_k(): return lax.ppermute(v, 'row', [(i, i ^ 1) for i in range(8)])  12 us
    ppermute x9, waiting for transfers between devices, swap_h(): lax.ppermute(v, 'row', [(i, mirror(i, 4, 2, mask)) for i in range(8)])  10.4 us
    ppermute x3, starting transfers between devices, swap_z(): return lax.ppermute(v, 'col', [(i, i ^ 1) for i in range(32)])  3.96 us
    dot_general x1, matrix products, local(): lax.dot_general(dense, target, (((0,), (0,)), ((), ())), preferred_elemen...  2.42 us
    dot_general x1, matrix products, local(): jnp.dot(dense, source, preferred_element_type=F32)  2.34 us
  transfers between devices with their start and end apart: 27, of which 19 were waited for; matrix products, arithmetic and copies ran while one was open for 5% of the time, Pallas kernels for 2%

profile of v2, /device:TPU:1, one launch (start us, length us, event | category | flops | bytes accessed | tf_op | source)
XLA Modules:
  0.0 96.9 jit_solution(2058943515196370720)
XLA Ops:
  0.6 2.6 %collective-permute-start = (bf16[128,128]{1,0:T(8,128)(2,1)}, bf16[128,128]{1,0:T(8,128)(2,1)S(1)}, u32[]{:S(2)}, u32[]{:S(2)}) collective-permute-start(bf16[128,128]{1,0:T(8,128)(2,1)} %param.7), channel_id=1, source_target_pairs={{0,1},{1,0},{2,3},{3,2},{4,5},{5,4},{6,7},{7,6},{8,9},{9,8},{10,11... | collective-permute-start | bytes 98312 | tf_op jit(solution)/shard_map/ppermute | solution.py:34
  3.2 1.5 %collective-permute-done = bf16[128,128]{1,0:T(8,128)(2,1)S(1)} collective-permute-done((bf16[128,128]{1,0:T(8,128)(2,1)}, bf16[128,128]{1,0:T(8,128)(2,1)S(1)}, u32[]{:S(2)}, u32[]{:S(2)}) %collective-permute-start) | collective-permute-done | bytes 32800 | tf_op jit(solution)/shard_map/ppermute | solution.py:34
  5.5 2.6 %collective-permute-start.3 = (bf16[2,128,128]{2,1,0:T(8,128)(2,1)S(1)}, bf16[2,128,128]{2,1,0:T(8,128)(2,1)S(1)}, u32[]{:S(2)}, u32[]{:S(2)}) collective-permute-start(bf16[2,128,128]{2,1,0:T(8,128)(2,1)S(1)} %get-tuple-element.37), channel_id=1, source_target_pairs={{0,6},{1,7},{2,4},{3,5},{4,2},{5,3},{6,0},{7,1},{8,14},{9,15},{10,... | collective-permute-start | bytes 196616 | tf_op jit(solution)/shard_map/ppermute | solution.py:22
  9.9 2.8 %collective-permute-done.2 = bf16[2,128,128]{2,1,0:T(8,128)(2,1)S(1)} collective-permute-done((bf16[2,128,128]{2,1,0:T(8,128)(2,1)S(1)}, bf16[2,128,128]{2,1,0:T(8,128)(2,1)S(1)}, u32[]{:S(2)}, u32[]{:S(2)}) %collective-permute-start.2) | collective-permute-done | bytes 65568 | tf_op jit(solution)/shard_map/ppermute | solution.py:22
  12.7 2.8 %collective-permute-start.6 = (bf16[4,2,128,128]{3,2,1,0:T(8,128)(2,1)S(1)}, bf16[4,2,128,128]{3,2,1,0:T(8,128)(2,1)S(1)}, u32[]{:S(2)}, u32[]{:S(2)}) collective-permute-start(bf16[4,2,128,128]{3,2,1,0:T(8,128)(2,1)S(1)} %get-tuple-element.26), channel_id=1, source_target_pairs={{0,24},{1,25},{2,26},{3,27},{4,28},{5,29},{6,30},{7,31},{8,16},{9,... | collective-permute-start | bytes 786440 | tf_op jit(solution)/shard_map/ppermute | solution.py:22
  17.6 2.2 %copy-done = bf16[1,1,128,128,128]{4,3,2,1,0:T(8,128)(2,1)S(1)} copy-done((bf16[1,1,128,128,128]{4,3,2,1,0:T(8,128)(2,1)S(1)}, bf16[1,1,128,128,128]{4,3,2,1,0:T(8,128)(2,1)}, u32[]{:S(2)}) %copy-start) | copy-done | bytes 4194328
  19.8 1.7 %spread.1 = bf16[1024,4096]{1,0:T(8,128)(2,1)S(1)} custom-call(s32[1]{0:T(128)} %bitcast.60.count_ref, s32[128]{0:T(128)S(1)} %get-tuple-element.45.put_row, s32[128]{0:T(128)S(1)} %get-tuple-element.44.put_col, bf16[128,128,128]{2,1,0:T(8,128)(2,1)S(1)} %bitcast.61), custom_call_target="tpu_custom_call" | custom-call | bytes 12582912 | tf_op jit(solution)/shard_map/spread/pallas_call | solution.py:63
  23.3 2.3 %fusion.19 = f32[1024,128]{1,0:T(8,128)S(1)} fusion(bf16[1024,4096]{1,0:T(8,128)(2,1)S(1)} %spread.1, bf16[4096,128]{1,0:T(8,128)(2,1)S(1)} %bitcast.64), kind=kOutput, calls=%fused_computation.90 | convolution fusion | flops 1073741824 | bytes 9961472 | tf_op jit(solution)/shard_map/dot_general | solution.py:190
  25.6 4.4 %collective-permute-start.7 = (bf16[4,128,128]{2,1,0:T(8,128)(2,1)S(1)}, bf16[4,128,128]{2,1,0:T(8,128)(2,1)S(1)}, u32[]{:S(2)}, u32[]{:S(2)}) collective-permute-start(bf16[4,128,128]{2,1,0:T(8,128)(2,1)S(1)} %bitcast.68), channel_id=1, source_target_pairs={{0,32},{32,0},{64,96},{96,64},{128,160},{160,128},{192,224},{224,1... | collective-permute-start | bytes 393224 | tf_op jit(solution)/shard_map/ppermute | solution.py:30
  31.1 3.1 %collective-permute-start.8 = (bf16[128,128]{1,0:T(8,128)(2,1)S(1)}, bf16[128,128]{1,0:T(8,128)(2,1)S(1)}, u32[]{:S(2)}, u32[]{:S(2)}) collective-permute-start(bf16[128,128]{1,0:T(8,128)(2,1)S(1)} %get-tuple-element.29), channel_id=1, source_target_pairs={{0,64},{32,96},{64,0},{96,32},{128,192},{160,224},{192,128},{224,1... | collective-permute-start | bytes 98312 | tf_op jit(solution)/shard_map/ppermute | solution.py:26
  34.1 5.1 %collective-permute-start.9 = (bf16[128,128]{1,0:T(8,128)(2,1)S(1)}, bf16[128,128]{1,0:T(8,128)(2,1)S(1)}, u32[]{:S(2)}, u32[]{:S(2)}) collective-permute-start(bf16[128,128]{1,0:T(8,128)(2,1)S(1)} %get-tuple-element.28), channel_id=1, source_target_pairs={{0,128},{32,160},{64,192},{96,224},{128,0},{160,32},{192,64},{224,... | collective-permute-start | bytes 98312 | tf_op jit(solution)/shard_map/ppermute | solution.py:26
  39.3 1.7 %collective-permute-done.9.in2 = bf16[128,128]{1,0:T(8,128)(2,1)S(1)} collective-permute-done((bf16[128,128]{1,0:T(8,128)(2,1)S(1)}, bf16[128,128]{1,0:T(8,128)(2,1)S(1)}, u32[]{:S(2)}, u32[]{:S(2)}) %collective-permute-start.9) | collective-permute-done | bytes 32800 | tf_op jit(solution)/shard_map/ppermute | solution.py:26
  40.9 3.2 %collective-permute-done.10.in3 = bf16[128,128]{1,0:T(8,128)(2,1)S(1)} collective-permute-done((bf16[128,128]{1,0:T(8,128)(2,1)S(1)}, bf16[128,128]{1,0:T(8,128)(2,1)S(1)}, u32[]{:S(2)}, u32[]{:S(2)}) %collective-permute-start.10) | collective-permute-done | bytes 32800 | tf_op jit(solution)/shard_map/ppermute | solution.py:26
  44.1 1.5 %middle.1 = (bf16[128,512]{1,0:T(8,128)(2,1)}, bf16[4,272,128]{2,1,0:T(8,128)(2,1)S(1)}, f32[144,128]{1,0:T(8,128)S(1)}) custom-call(s32[2]{0:T(128)S(1)} %pad_add_fusion.place, f32[128,128]{1,0:T(8,128)S(1)} %slice_bitcast_fusion.3.own, bf16[128,128]{1,0:T(8,128)(2,1)S(1)} %collective-permute-done.8.in1, bf16[128,128]{1,0:T(8,128)(2,1)S(1)} %collective-permute-done.9.in2, ...), custom_call_target="tpu_custom_call" | custom-call | flops 83886080 | bytes 655360 | tf_op jit(solution)/shard_map/middle/pallas_call | solution.py:125
  45.6 1.1 %collective-permute-start.13 = (bf16[272,128]{1,0:T(8,128)(2,1)S(1)}, bf16[272,128]{1,0:T(8,128)(2,1)S(1)}, u32[]{:S(2)}, u32[]{:S(2)}) collective-permute-start(bf16[272,128]{1,0:T(8,128)(2,1)S(1)} %get-tuple-element.20), channel_id=1, source_target_pairs={{0,192},{32,224},{64,128},{96,160},{128,64},{160,96},{192,0},{224,... | collective-permute-start | bytes 208904 | tf_op jit(solution)/shard_map/ppermute | solution.py:26
  46.7 3.5 %collective-permute-start.12 = (bf16[272,128]{1,0:T(8,128)(2,1)S(1)}, bf16[272,128]{1,0:T(8,128)(2,1)S(1)}, u32[]{:S(2)}, u32[]{:S(2)}) collective-permute-start(bf16[272,128]{1,0:T(8,128)(2,1)S(1)} %get-tuple-element.21), channel_id=1, source_target_pairs={{0,128},{32,160},{64,192},{96,224},{128,0},{160,32},{192,64},{224,... | collective-permute-start | bytes 208904 | tf_op jit(solution)/shard_map/ppermute | solution.py:26
  50.2 1.2 %collective-permute-start.11 = (bf16[272,128]{1,0:T(8,128)(2,1)S(1)}, bf16[272,128]{1,0:T(8,128)(2,1)S(1)}, u32[]{:S(2)}, u32[]{:S(2)}) collective-permute-start(bf16[272,128]{1,0:T(8,128)(2,1)S(1)} %get-tuple-element.19), channel_id=1, source_target_pairs={{0,64},{32,96},{64,0},{96,32},{128,192},{160,224},{192,128},{224,1... | collective-permute-start | bytes 208904 | tf_op jit(solution)/shard_map/ppermute | solution.py:26
  51.4 2.5 %collective-permute-done.12 = bf16[272,128]{1,0:T(8,128)(2,1)S(1)} collective-permute-done((bf16[272,128]{1,0:T(8,128)(2,1)S(1)}, bf16[272,128]{1,0:T(8,128)(2,1)S(1)}, u32[]{:S(2)}, u32[]{:S(2)}) %collective-permute-start.12) | collective-permute-done | bytes 69664 | tf_op jit(solution)/shard_map/ppermute | solution.py:26
  53.9 2.1 %collective-permute-done.11 = bf16[272,128]{1,0:T(8,128)(2,1)S(1)} collective-permute-done((bf16[272,128]{1,0:T(8,128)(2,1)S(1)}, bf16[272,128]{1,0:T(8,128)(2,1)S(1)}, u32[]{:S(2)}, u32[]{:S(2)}) %collective-permute-start.11) | collective-permute-done | bytes 69664 | tf_op jit(solution)/shard_map/ppermute | solution.py:26
  56.1 3.7 %collective-permute-start.14 = (bf16[672,128]{1,0:T(8,128)(2,1)S(1)}, bf16[672,128]{1,0:T(8,128)(2,1)S(1)}, u32[]{:S(2)}, u32[]{:S(2)}) collective-permute-start(bf16[672,128]{1,0:T(8,128)(2,1)S(1)} %constant_dynamic-update-slice_fusion), channel_id=1, source_target_pairs={{0,32},{32,0},{64,96},{96,64},{128,160},{160,128},{192,224},{224,1... | collective-permute-start | bytes 516104 | tf_op jit(solution)/shard_map/ppermute | solution.py:30
  61.2 2.4 %fusion.18 = (bf16[4096,128]{1,0:T(8,128)(2,1)S(1)}, f32[4096,128]{1,0:T(8,128)S(1)}) fusion(bf16[1024,4096]{1,0:T(8,128)(2,1)S(1)} %spread.1, bf16[1024,128]{1,0:T(8,128)(2,1)S(1)} %slice_dynamic-update-slice_fusion), kind=kOutput, calls=%fused_computation.89 | convolution fusion | flops 1074266112 | bytes 11796480 | tf_op jit(solution)/shard_map/dot_general | solution.py:206
  64.1 1.1 %collective-permute-start.18 = (bf16[1104,128]{1,0:T(8,128)(2,1)S(1)}, bf16[1104,128]{1,0:T(8,128)(2,1)S(1)}, u32[]{:S(2)}, u32[]{:S(2)}) collective-permute-start(bf16[1104,128]{1,0:T(8,128)(2,1)S(1)} %get-tuple-element.43), channel_id=1, source_target_pairs={{0,24},{1,25},{2,26},{3,27},{4,28},{5,29},{6,30},{7,31},{8,16},{9,... | collective-permute-start | bytes 847880 | tf_op jit(solution)/shard_map/ppermute | solution.py:22
  66.0 1.4 %collective-permute-start.16 = (bf16[1104,128]{1,0:T(8,128)(2,1)S(1)}, bf16[1104,128]{1,0:T(8,128)(2,1)S(1)}, u32[]{:S(2)}, u32[]{:S(2)}) collective-permute-start(bf16[1104,128]{1,0:T(8,128)(2,1)S(1)} %get-tuple-element.41), channel_id=1, source_target_pairs={{0,8},{1,9},{2,10},{3,11},{4,12},{5,13},{6,14},{7,15},{8,0},{9,1},... | collective-permute-start | bytes 847880 | tf_op jit(solution)/shard_map/ppermute | solution.py:22
  67.4 6.7 %collective-permute-done.18 = bf16[1104,128]{1,0:T(8,128)(2,1)S(1)} collective-permute-done((bf16[1104,128]{1,0:T(8,128)(2,1)S(1)}, bf16[1104,128]{1,0:T(8,128)(2,1)S(1)}, u32[]{:S(2)}, u32[]{:S(2)}) %collective-permute-start.18) | collective-permute-done | bytes 282656 | tf_op jit(solution)/shard_map/ppermute | solution.py:22
  75.0 2.6 %collective-permute-start.21 = (bf16[336,128]{1,0:T(8,128)(2,1)S(1)}, bf16[336,128]{1,0:T(8,128)(2,1)S(1)}, u32[]{:S(2)}, u32[]{:S(2)}) collective-permute-start(bf16[336,128]{1,0:T(8,128)(2,1)S(1)} %get-tuple-element.40), channel_id=1, source_target_pairs={{0,6},{1,7},{2,4},{3,5},{4,2},{5,3},{6,0},{7,1},{8,14},{9,15},{10,... | collective-permute-start | bytes 258056 | tf_op jit(solution)/shard_map/ppermute | solution.py:22
  78.3 1.6 %collective-permute-done.21 = bf16[336,128]{1,0:T(8,128)(2,1)S(1)} collective-permute-done((bf16[336,128]{1,0:T(8,128)(2,1)S(1)}, bf16[336,128]{1,0:T(8,128)(2,1)S(1)}, u32[]{:S(2)}, u32[]{:S(2)}) %collective-permute-start.21) | collective-permute-done | bytes 86048 | tf_op jit(solution)/shard_map/ppermute | solution.py:22
  79.9 2.5 %collective-permute-done.20 = bf16[336,128]{1,0:T(8,128)(2,1)S(1)} collective-permute-done((bf16[336,128]{1,0:T(8,128)(2,1)S(1)}, bf16[336,128]{1,0:T(8,128)(2,1)S(1)}, u32[]{:S(2)}, u32[]{:S(2)}) %collective-permute-start.20) | collective-permute-done | bytes 86048 | tf_op jit(solution)/shard_map/ppermute | solution.py:22
  82.4 2.0 %collective-permute-start.25 = (bf16[64,128]{1,0:T(8,128)(2,1)S(1)}, bf16[64,128]{1,0:T(8,128)(2,1)S(1)}, u32[]{:S(2)}, u32[]{:S(2)}) collective-permute-start(bf16[64,128]{1,0:T(8,128)(2,1)S(1)} %slice.295), channel_id=1, source_target_pairs={{0,192},{32,224},{64,128},{96,160},{128,64},{160,96},{192,0},{224,... | collective-permute-start | bytes 49160 | tf_op jit(solution)/shard_map/ppermute | solution.py:26
  84.4 3.0 %collective-permute-start.24 = (bf16[64,128]{1,0:T(8,128)(2,1)S(1)}, bf16[64,128]{1,0:T(8,128)(2,1)S(1)}, u32[]{:S(2)}, u32[]{:S(2)}) collective-permute-start(bf16[64,128]{1,0:T(8,128)(2,1)S(1)} %slice.295), channel_id=1, source_target_pairs={{0,128},{32,160},{64,192},{96,224},{128,0},{160,32},{192,64},{224,... | collective-permute-start | bytes 49160 | tf_op jit(solution)/shard_map/ppermute | solution.py:26
  88.8 1.1 %collective-permute-start.22 = (bf16[128,128]{1,0:T(8,128)(2,1)S(1)}, bf16[128,128]{1,0:T(8,128)(2,1)S(1)}, u32[]{:S(2)}, u32[]{:S(2)}) collective-permute-start(bf16[128,128]{1,0:T(8,128)(2,1)S(1)} %slice.294), channel_id=1, source_target_pairs={{0,1},{1,0},{2,3},{3,2},{4,5},{5,4},{6,7},{7,6},{8,9},{9,8},{10,11... | collective-permute-start | bytes 98312 | tf_op jit(solution)/shard_map/ppermute | solution.py:34
  90.9 3.9 %collective-permute-start.26 = (bf16[256,128]{1,0:T(8,128)(2,1)S(1)}, bf16[256,128]{1,0:T(8,128)(2,1)S(1)}, u32[]{:S(2)}, u32[]{:S(2)}) collective-permute-start(bf16[256,128]{1,0:T(8,128)(2,1)S(1)} %pad_maximum_fusion.9.near), channel_id=1, source_target_pairs={{0,32},{32,0},{64,96},{96,64},{128,160},{160,128},{192,224},{224,1... | collective-permute-start | bytes 196616 | tf_op jit(solution)/shard_map/ppermute | solution.py:30
  95.6 1.3 %settle.1 = f32[128,512]{1,0:T(8,128)} custom-call(s32[2]{0:T(128)S(1)} %pad_add_fusion.place, bf16[256,128]{1,0:T(8,128)(2,1)S(1)} %pad_maximum_fusion.9.near, bf16[256,128]{1,0:T(8,128)(2,1)S(1)} %collective-permute-done.26.far), custom_call_target="tpu_custom_call" | custom-call | tf_op jit(solution)/shard_map/settle/pallas_call | solution.py:158
  (71 shorter events, 14.5 us)
Async XLA Ops:
  0.6 4.1 %collective-permute-start = (bf16[128,128]{1,0:T(8,128)(2,1)}, bf16[128,128]{1,0:T(8,128)(2,1)S(1)}, u32[]{:S(2)}, u32[]{:S(2)}) collective-permute-start(bf16[128,128]{1,0:T(8,128)(2,1)} %param.7), channel_id=1, source_target_pairs={{0,1},{1,0},{2,3},{3,2},{4,5},{5,4},{6,7},{7,6},{8,9},{9,8},{10,11... | collective-permute-start | bytes 98312 | tf_op jit(solution)/shard_map/ppermute | solution.py:34
  5.5 4.4 %collective-permute-start.3 = (bf16[2,128,128]{2,1,0:T(8,128)(2,1)S(1)}, bf16[2,128,128]{2,1,0:T(8,128)(2,1)S(1)}, u32[]{:S(2)}, u32[]{:S(2)}) collective-permute-start(bf16[2,128,128]{2,1,0:T(8,128)(2,1)S(1)} %get-tuple-element.37), channel_id=1, source_target_pairs={{0,6},{1,7},{2,4},{3,5},{4,2},{5,3},{6,0},{7,1},{8,14},{9,15},{10,... | collective-permute-start | bytes 196616 | tf_op jit(solution)/shard_map/ppermute | solution.py:22
  8.0 4.6 %collective-permute-start.2 = (bf16[2,128,128]{2,1,0:T(8,128)(2,1)S(1)}, bf16[2,128,128]{2,1,0:T(8,128)(2,1)S(1)}, u32[]{:S(2)}, u32[]{:S(2)}) collective-permute-start(bf16[2,128,128]{2,1,0:T(8,128)(2,1)S(1)} %get-tuple-element.37), channel_id=1, source_target_pairs={{0,4},{1,5},{2,6},{3,7},{4,0},{5,1},{6,2},{7,3},{8,12},{9,13},{10,... | collective-permute-start | bytes 196616 | tf_op jit(solution)/shard_map/ppermute | solution.py:22
  8.6 4.1 %collective-permute-start.1 = (bf16[2,128,128]{2,1,0:T(8,128)(2,1)S(1)}, bf16[2,128,128]{2,1,0:T(8,128)(2,1)S(1)}, u32[]{:S(2)}, u32[]{:S(2)}) collective-permute-start(bf16[2,128,128]{2,1,0:T(8,128)(2,1)S(1)} %get-tuple-element.37), channel_id=1, source_target_pairs={{0,2},{1,3},{2,0},{3,1},{4,6},{5,7},{6,4},{7,5},{8,10},{9,11},{10,... | collective-permute-start | bytes 196616 | tf_op jit(solution)/shard_map/ppermute | solution.py:22
  12.7 8.9 %collective-permute-start.6 = (bf16[4,2,128,128]{3,2,1,0:T(8,128)(2,1)S(1)}, bf16[4,2,128,128]{3,2,1,0:T(8,128)(2,1)S(1)}, u32[]{:S(2)}, u32[]{:S(2)}) collective-permute-start(bf16[4,2,128,128]{3,2,1,0:T(8,128)(2,1)S(1)} %get-tuple-element.26), channel_id=1, source_target_pairs={{0,24},{1,25},{2,26},{3,27},{4,28},{5,29},{6,30},{7,31},{8,16},{9,... | collective-permute-start | bytes 786440 | tf_op jit(solution)/shard_map/ppermute | solution.py:22
  15.5 6.7 %collective-permute-start.5 = (bf16[4,2,128,128]{3,2,1,0:T(8,128)(2,1)S(1)}, bf16[4,2,128,128]{3,2,1,0:T(8,128)(2,1)S(1)}, u32[]{:S(2)}, u32[]{:S(2)}) collective-permute-start(bf16[4,2,128,128]{3,2,1,0:T(8,128)(2,1)S(1)} %get-tuple-element.26), channel_id=1, source_target_pairs={{0,16},{1,17},{2,18},{3,19},{4,20},{5,21},{6,22},{7,23},{8,24},{9,... | collective-permute-start | bytes 786440 | tf_op jit(solution)/shard_map/ppermute | solution.py:22
  15.9 7.2 %collective-permute-start.4 = (bf16[4,2,128,128]{3,2,1,0:T(8,128)(2,1)S(1)}, bf16[4,2,128,128]{3,2,1,0:T(8,128)(2,1)S(1)}, u32[]{:S(2)}, u32[]{:S(2)}) collective-permute-start(bf16[4,2,128,128]{3,2,1,0:T(8,128)(2,1)S(1)} %get-tuple-element.26), channel_id=1, source_target_pairs={{0,8},{1,9},{2,10},{3,11},{4,12},{5,13},{6,14},{7,15},{8,0},{9,1},... | collective-permute-start | bytes 786440 | tf_op jit(solution)/shard_map/ppermute | solution.py:22
  17.6 2.2 %copy-start = (bf16[1,1,128,128,128]{4,3,2,1,0:T(8,128)(2,1)S(1)}, bf16[1,1,128,128,128]{4,3,2,1,0:T(8,128)(2,1)}, u32[]{:S(2)}) copy-start(bf16[1,1,128,128,128]{4,3,2,1,0:T(8,128)(2,1)} %param.10) | copy-start | bytes 12582916
  21.5 22.7 %copy-start.1 = (bf16[128,512]{1,0:T(8,128)(2,1)S(1)}, bf16[128,512]{1,0:T(8,128)(2,1)}, u32[]{:S(2)}) copy-start(bf16[128,512]{1,0:T(8,128)(2,1)} %weight.1) | copy-start | bytes 393220
  21.5 22.7 %copy-start.2 = (bf16[128,512]{1,0:T(8,128)(2,1)S(1)}, bf16[128,512]{1,0:T(8,128)(2,1)}, u32[]{:S(2)}) copy-start(bf16[128,512]{1,0:T(8,128)(2,1)} %cot.1) | copy-start | bytes 393220
  21.5 22.6 %copy-start.3 = (f32[512]{0:T(512)S(1)}, f32[512]{0:T(512)}, u32[]{:S(2)}) copy-start(f32[512]{0:T(512)} %param.9) | copy-start | bytes 6148
  25.6 5.4 %collective-permute-start.7 = (bf16[4,128,128]{2,1,0:T(8,128)(2,1)S(1)}, bf16[4,128,128]{2,1,0:T(8,128)(2,1)S(1)}, u32[]{:S(2)}, u32[]{:S(2)}) collective-permute-start(bf16[4,128,128]{2,1,0:T(8,128)(2,1)S(1)} %bitcast.68), channel_id=1, source_target_pairs={{0,32},{32,0},{64,96},{96,64},{128,160},{160,128},{192,224},{224,1... | collective-permute-start | bytes 393224 | tf_op jit(solution)/shard_map/ppermute | solution.py:30
  31.1 8.2 %collective-permute-start.8 = (bf16[128,128]{1,0:T(8,128)(2,1)S(1)}, bf16[128,128]{1,0:T(8,128)(2,1)S(1)}, u32[]{:S(2)}, u32[]{:S(2)}) collective-permute-start(bf16[128,128]{1,0:T(8,128)(2,1)S(1)} %get-tuple-element.29), channel_id=1, source_target_pairs={{0,64},{32,96},{64,0},{96,32},{128,192},{160,224},{192,128},{224,1... | collective-permute-start | bytes 98312 | tf_op jit(solution)/shard_map/ppermute | solution.py:26
  34.1 6.8 %collective-permute-start.9 = (bf16[128,128]{1,0:T(8,128)(2,1)S(1)}, bf16[128,128]{1,0:T(8,128)(2,1)S(1)}, u32[]{:S(2)}, u32[]{:S(2)}) collective-permute-start(bf16[128,128]{1,0:T(8,128)(2,1)S(1)} %get-tuple-element.28), channel_id=1, source_target_pairs={{0,128},{32,160},{64,192},{96,224},{128,0},{160,32},{192,64},{224,... | collective-permute-start | bytes 98312 | tf_op jit(solution)/shard_map/ppermute | solution.py:26
  39.3 4.9 %collective-permute-start.10 = (bf16[128,128]{1,0:T(8,128)(2,1)S(1)}, bf16[128,128]{1,0:T(8,128)(2,1)S(1)}, u32[]{:S(2)}, u32[]{:S(2)}) collective-permute-start(bf16[128,128]{1,0:T(8,128)(2,1)S(1)} %get-tuple-element.27), channel_id=1, source_target_pairs={{0,192},{32,224},{64,128},{96,160},{128,64},{160,96},{192,0},{224,... | collective-permute-start | bytes 98312 | tf_op jit(solution)/shard_map/ppermute | solution.py:26
  45.6 5.8 %collective-permute-start.13 = (bf16[272,128]{1,0:T(8,128)(2,1)S(1)}, bf16[272,128]{1,0:T(8,128)(2,1)S(1)}, u32[]{:S(2)}, u32[]{:S(2)}) collective-permute-start(bf16[272,128]{1,0:T(8,128)(2,1)S(1)} %get-tuple-element.20), channel_id=1, source_target_pairs={{0,192},{32,224},{64,128},{96,160},{128,64},{160,96},{192,0},{224,... | collective-permute-start | bytes 208904 | tf_op jit(solution)/shard_map/ppermute | solution.py:26
  46.7 7.2 %collective-permute-start.12 = (bf16[272,128]{1,0:T(8,128)(2,1)S(1)}, bf16[272,128]{1,0:T(8,128)(2,1)S(1)}, u32[]{:S(2)}, u32[]{:S(2)}) collective-permute-start(bf16[272,128]{1,0:T(8,128)(2,1)S(1)} %get-tuple-element.21), channel_id=1, source_target_pairs={{0,128},{32,160},{64,192},{96,224},{128,0},{160,32},{192,64},{224,... | collective-permute-start | bytes 208904 | tf_op jit(solution)/shard_map/ppermute | solution.py:26
  50.2 5.8 %collective-permute-start.11 = (bf16[272,128]{1,0:T(8,128)(2,1)S(1)}, bf16[272,128]{1,0:T(8,128)(2,1)S(1)}, u32[]{:S(2)}, u32[]{:S(2)}) collective-permute-start(bf16[272,128]{1,0:T(8,128)(2,1)S(1)} %get-tuple-element.19), channel_id=1, source_target_pairs={{0,64},{32,96},{64,0},{96,32},{128,192},{160,224},{192,128},{224,1... | collective-permute-start | bytes 208904 | tf_op jit(solution)/shard_map/ppermute | solution.py:26
  56.1 4.7 %collective-permute-start.14 = (bf16[672,128]{1,0:T(8,128)(2,1)S(1)}, bf16[672,128]{1,0:T(8,128)(2,1)S(1)}, u32[]{:S(2)}, u32[]{:S(2)}) collective-permute-start(bf16[672,128]{1,0:T(8,128)(2,1)S(1)} %constant_dynamic-update-slice_fusion), channel_id=1, source_target_pairs={{0,32},{32,0},{64,96},{96,64},{128,160},{160,128},{192,224},{224,1... | collective-permute-start | bytes 516104 | tf_op jit(solution)/shard_map/ppermute | solution.py:30
  60.9 3.1 %collective-permute-start.15 = (f32[80,128]{1,0:T(8,128)S(1)}, f32[80,128]{1,0:T(8,128)S(1)}, u32[]{:S(2)}, u32[]{:S(2)}) collective-permute-start(f32[80,128]{1,0:T(8,128)S(1)} %maximum_add_fusion), channel_id=1, source_target_pairs={{0,1},{1,0},{2,3},{3,2},{4,5},{5,4},{6,7},{7,6},{8,9},{9,8},{10,11... | collective-permute-start | bytes 122888 | tf_op jit(solution)/shard_map/ppermute | solution.py:34
  64.1 10.1 %collective-permute-start.18 = (bf16[1104,128]{1,0:T(8,128)(2,1)S(1)}, bf16[1104,128]{1,0:T(8,128)(2,1)S(1)}, u32[]{:S(2)}, u32[]{:S(2)}) collective-permute-start(bf16[1104,128]{1,0:T(8,128)(2,1)S(1)} %get-tuple-element.43), channel_id=1, source_target_pairs={{0,24},{1,25},{2,26},{3,27},{4,28},{5,29},{6,30},{7,31},{8,16},{9,... | collective-permute-start | bytes 847880 | tf_op jit(solution)/shard_map/ppermute | solution.py:22
  65.2 9.0 %collective-permute-start.17 = (bf16[1104,128]{1,0:T(8,128)(2,1)S(1)}, bf16[1104,128]{1,0:T(8,128)(2,1)S(1)}, u32[]{:S(2)}, u32[]{:S(2)}) collective-permute-start(bf16[1104,128]{1,0:T(8,128)(2,1)S(1)} %get-tuple-element.42), channel_id=1, source_target_pairs={{0,16},{1,17},{2,18},{3,19},{4,20},{5,21},{6,22},{7,23},{8,24},{9,... | collective-permute-start | bytes 847880 | tf_op jit(solution)/shard_map/ppermute | solution.py:22
  66.0 8.8 %collective-permute-start.16 = (bf16[1104,128]{1,0:T(8,128)(2,1)S(1)}, bf16[1104,128]{1,0:T(8,128)(2,1)S(1)}, u32[]{:S(2)}, u32[]{:S(2)}) collective-permute-start(bf16[1104,128]{1,0:T(8,128)(2,1)S(1)} %get-tuple-element.41), channel_id=1, source_target_pairs={{0,8},{1,9},{2,10},{3,11},{4,12},{5,13},{6,14},{7,15},{8,0},{9,1},... | collective-permute-start | bytes 847880 | tf_op jit(solution)/shard_map/ppermute | solution.py:22
  75.0 4.9 %collective-permute-start.21 = (bf16[336,128]{1,0:T(8,128)(2,1)S(1)}, bf16[336,128]{1,0:T(8,128)(2,1)S(1)}, u32[]{:S(2)}, u32[]{:S(2)}) collective-permute-start(bf16[336,128]{1,0:T(8,128)(2,1)S(1)} %get-tuple-element.40), channel_id=1, source_target_pairs={{0,6},{1,7},{2,4},{3,5},{4,2},{5,3},{6,0},{7,1},{8,14},{9,15},{10,... | collective-permute-start | bytes 258056 | tf_op jit(solution)/shard_map/ppermute | solution.py:22
  77.5 4.8 %collective-permute-start.20 = (bf16[336,128]{1,0:T(8,128)(2,1)S(1)}, bf16[336,128]{1,0:T(8,128)(2,1)S(1)}, u32[]{:S(2)}, u32[]{:S(2)}) collective-permute-start(bf16[336,128]{1,0:T(8,128)(2,1)S(1)} %get-tuple-element.39), channel_id=1, source_target_pairs={{0,4},{1,5},{2,6},{3,7},{4,0},{5,1},{6,2},{7,3},{8,12},{9,13},{10,... | collective-permute-start | bytes 258056 | tf_op jit(solution)/shard_map/ppermute | solution.py:22
  78.1 4.3 %collective-permute-start.19 = (bf16[336,128]{1,0:T(8,128)(2,1)S(1)}, bf16[336,128]{1,0:T(8,128)(2,1)S(1)}, u32[]{:S(2)}, u32[]{:S(2)}) collective-permute-start(bf16[336,128]{1,0:T(8,128)(2,1)S(1)} %get-tuple-element.38), channel_id=1, source_target_pairs={{0,2},{1,3},{2,0},{3,1},{4,6},{5,7},{6,4},{7,5},{8,10},{9,11},{10,... | collective-permute-start | bytes 258056 | tf_op jit(solution)/shard_map/ppermute | solution.py:22
  82.4 7.5 %collective-permute-start.25 = (bf16[64,128]{1,0:T(8,128)(2,1)S(1)}, bf16[64,128]{1,0:T(8,128)(2,1)S(1)}, u32[]{:S(2)}, u32[]{:S(2)}) collective-permute-start(bf16[64,128]{1,0:T(8,128)(2,1)S(1)} %slice.295), channel_id=1, source_target_pairs={{0,192},{32,224},{64,128},{96,160},{128,64},{160,96},{192,0},{224,... | collective-permute-start | bytes 49160 | tf_op jit(solution)/shard_map/ppermute | solution.py:26
  84.4 6.5 %collective-permute-start.24 = (bf16[64,128]{1,0:T(8,128)(2,1)S(1)}, bf16[64,128]{1,0:T(8,128)(2,1)S(1)}, u32[]{:S(2)}, u32[]{:S(2)}) collective-permute-start(bf16[64,128]{1,0:T(8,128)(2,1)S(1)} %slice.295), channel_id=1, source_target_pairs={{0,128},{32,160},{64,192},{96,224},{128,0},{160,32},{192,64},{224,... | collective-permute-start | bytes 49160 | tf_op jit(solution)/shard_map/ppermute | solution.py:26
  87.3 3.5 %collective-permute-start.23 = (bf16[64,128]{1,0:T(8,128)(2,1)S(1)}, bf16[64,128]{1,0:T(8,128)(2,1)S(1)}, u32[]{:S(2)}, u32[]{:S(2)}) collective-permute-start(bf16[64,128]{1,0:T(8,128)(2,1)S(1)} %slice.295), channel_id=1, source_target_pairs={{0,64},{32,96},{64,0},{96,32},{128,192},{160,224},{192,128},{224,1... | collective-permute-start | bytes 49160 | tf_op jit(solution)/shard_map/ppermute | solution.py:26
  88.8 6.0 %collective-permute-start.22 = (bf16[128,128]{1,0:T(8,128)(2,1)S(1)}, bf16[128,128]{1,0:T(8,128)(2,1)S(1)}, u32[]{:S(2)}, u32[]{:S(2)}) collective-permute-start(bf16[128,128]{1,0:T(8,128)(2,1)S(1)} %slice.294), channel_id=1, source_target_pairs={{0,1},{1,0},{2,3},{3,2},{4,5},{5,4},{6,7},{7,6},{8,9},{9,8},{10,11... | collective-permute-start | bytes 98312 | tf_op jit(solution)/shard_map/ppermute | solution.py:34
  90.9 4.8 %collective-permute-start.26 = (bf16[256,128]{1,0:T(8,128)(2,1)S(1)}, bf16[256,128]{1,0:T(8,128)(2,1)S(1)}, u32[]{:S(2)}, u32[]{:S(2)}) collective-permute-start(bf16[256,128]{1,0:T(8,128)(2,1)S(1)} %pad_maximum_fusion.9.near), channel_id=1, source_target_pairs={{0,32},{32,0},{64,96},{96,64},{128,160},{160,128},{192,224},{224,1... | collective-permute-start | bytes 196616 | tf_op jit(solution)/shard_map/ppermute | solution.py:30

commit v3 on v2

--- a/solution.py
+++ b/solution.py
@@ -140,29 +140,54 @@
     )(place, own, *arrived, weight, bias[None, :], cotangent)
 
 
-def settle_kernel(place, near, far, out_ref):
-    lanes = near.shape[1]
+def settle_kernel(place, own, one, two, three, far, out_ref, bias_ref):
+    lanes = own.shape[1]
     blocks = out_ref.shape[1] // lanes
-    rows = near.shape[0] // 4 // blocks
-    for k, part in ((0, near), (1, far)):
-        for first in range(4):
-            at = ((place[0] ^ first) * 2 + (place[1] ^ k)) * rows
-            at = pl.ds(pl.multiple_of(at, rows), rows)
-            for j in range(blocks):
-                start = (first * blocks + j) * rows
-                out_ref[at, j * lanes : (j + 1) * lanes] = part[start : start + rows, :].astype(F32)
-
-
-def settle(place, near, far, feats, width):
+    rows = out_ref.shape[0] // 8
+    share = blocks * rows
+    parts = [(0, bits, ref, 0) for bits, ref in enumerate((own, one, two, three))]
+    parts += [(1, bits, far, bits * share) for bits in range(4)]
+    for k, bits, ref, start in parts:
+        at = pl.ds(pl.multiple_of(((place[0] ^ bits) * 2 + (place[1] ^ k)) * rows, rows), rows)
+        for j in range(blocks):
+            piece = ref[start + j * rows : start + (j + 1) * rows, :]
+            out_ref[at, j * lanes : (j + 1) * lanes] = piece.astype(F32)
+    mine, other = own[share:, :].astype(F32), far[4 * share :, :].astype(F32)
+    sums = jnp.where(place[1] == 0, mine, other)
+    for j in range(blocks):
+        bias_ref[:, j * lanes : (j + 1) * lanes] = sums[j : j + 1, :] + sums[8 + j : 9 + j, :]
+
+
+def settle(place, own, arrived, far, feats, width):
     vmem = pl.BlockSpec(memory_space=VMEM)
     return pl.pallas_call(
         settle_kernel,
-        out_shape=jax.ShapeDtypeStruct((feats, width), F32),
-        in_specs=[pl.BlockSpec(memory_space=pltpu.SMEM), vmem, vmem],
-        out_specs=vmem,
+        out_shape=(
+            jax.ShapeDtypeStruct((feats, width), F32),
+            jax.ShapeDtypeStruct((1, width), F32),
+        ),
+        in_specs=[pl.BlockSpec(memory_space=pltpu.SMEM)] + [vmem] * 5,
+        out_specs=(vmem, vmem),
         compiler_params=pltpu.CompilerParams(vmem_limit_bytes=16 * 2**20),
         name="settle",
-    )(place, near, far)
+    )(place, own, *arrived, far)
+
+
+def near_kernel(v_ref, out_ref):
+    out_ref[...] = v_ref[...]
+
+
+def near_copy(v):
+    vmem = pl.BlockSpec(memory_space=VMEM)
+    return pl.pallas_call(
+        near_kernel,
+        out_shape=jax.ShapeDtypeStruct(v.shape, v.dtype),
+        in_specs=[vmem],
+        out_specs=vmem,
+        compiler_params=pltpu.CompilerParams(vmem_limit_bytes=4 * 2**20),
+        cost_estimate=pl.CostEstimate(flops=0, bytes_accessed=4 * v.size, transcendentals=0),
+        name="near_copy",
+    )(v)
 
 
 def local(features, weight, bias, tile_values, tile_index, tile_count, cotangent):
@@ -182,7 +207,7 @@
     put_col = (second * 8 + first * 2 + far_z).astype(jnp.int32)
     dense = spread(tile_values[0, 0], tile_count[0], put_row, put_col, 8, 32)
 
-    source = jnp.stack([features, swap_z(features)])
+    source = jnp.stack([near_copy(features), swap_z(features)])
     for turn in (0, 1):
         source = jnp.stack([source] + [swap_xy(source, bits, turn) for bits in (1, 2, 3)])
     source = source.reshape(-1, feats)
@@ -214,11 +239,13 @@
         gw = (extra.astype(F32) + two) + (one + three)
     grad_features = (grad[:size] + swap_z(grad[size:].astype(BF)).astype(F32)).astype(BF)
 
-    grad_bias = gw[share : share + width // feats].reshape(width)
+    sums = pair(gw[share : share + 8])
     gw = gw[:share].astype(BF)
-    gw = jnp.concatenate([gw] + [swap_h(gw, s) for s in (1, 2, 3)])
-    grad_weight = settle(here, gw, swap_k(gw), feats, width)
-    return (hidden_out, grad_features, grad_weight, grad_bias)
+    arrived = [swap_h(gw, s) for s in (1, 2, 3)]
+    far = swap_k(jnp.concatenate([gw] + arrived + [sums]))
+    own = jnp.concatenate([gw, sums])
+    grad_weight, grad_bias = settle(here, own, arrived, far, feats, width)
+    return (hidden_out, grad_features, grad_weight, grad_bias.reshape(width))
 
 
 def solution(mesh):

time: 97.1 us -> 97 us (level)
    unnamed x13 -> x20, local copies, waits for them, and re-layouts: 2.27 us -> 3.1 us
  transfers between devices with their start and end apart: 27 -> 27, of which waited for: 19 -> 20; matrix products, arithmetic and copies ran while one was open for 5% -> 4% of each run, Pallas kernels for 2% -> 2%
where the time goes in v3:
time: 97 us; the launch traced here: 96.8 us
  starting transfers between devices  49.5 us (51%)
  waiting for transfers between devices  31.2 us (32%)
  matrix products  4.76 us (5%)
  Pallas kernels  4.56 us (5%)
  local copies, waits for them, and re-layouts  3.26 us (3%)
  other arithmetic  1.97 us (2%)
  between operations  1.57 us (2%)
    ppermute x9, starting transfers between devices, swap_h(): lax.ppermute(v, 'row', [(i, mirror(i, 4, 2, mask)) for i in range(8)])  19.7 us
    ppermute x12, waiting for transfers between devices, swap_xy(): return lax.ppermute(v, ('row', 'col'), pairs)  16.8 us
    ppermute x12, starting transfers between devices, swap_xy(): return lax.ppermute(v, ('row', 'col'), pairs)  13.5 us
    ppermute x3, starting transfers between devices, swap_k(): return lax.ppermute(v, 'row', [(i, i ^ 1) for i in range(8)])  12.2 us
    ppermute x9, waiting for transfers between devices, swap_h(): lax.ppermute(v, 'row', [(i, mirror(i, 4, 2, mask)) for i in range(8)])  11.1 us
    ppermute x3, starting transfers between devices, swap_z(): return lax.ppermute(v, 'col', [(i, i ^ 1) for i in range(32)])  4.05 us
    unnamed x20, local copies, waits for them, and re-layouts  3.1 us
    dot_general x1, matrix products, local(): lax.dot_general(dense, target, (((0,), (0,)), ((), ())), preferred_elemen...  2.42 us
  transfers between devices with their start and end apart: 27, of which 20 were waited for; matrix products, arithmetic and copies ran while one was open for 4% of the time, Pallas kernels for 2%

profile of v3, /device:TPU:1, one launch (start us, length us, event | category | flops | bytes accessed | tf_op | source)
XLA Modules:
  0.0 96.8 jit_solution(11235369806910786351)
XLA Ops:
  0.6 2.6 %collective-permute-start = (bf16[128,128]{1,0:T(8,128)(2,1)}, bf16[128,128]{1,0:T(8,128)(2,1)S(1)}, u32[]{:S(2)}, u32[]{:S(2)}) collective-permute-start(bf16[128,128]{1,0:T(8,128)(2,1)} %v_ref.1), channel_id=1, source_target_pairs={{0,1},{1,0},{2,3},{3,2},{4,5},{5,4},{6,7},{7,6},{8,9},{9,8},{10,11... | collective-permute-start | bytes 98312 | tf_op jit(solution)/shard_map/ppermute | solution.py:34
  4.7 2.6 %collective-permute-start.3 = (bf16[2,128,128]{2,1,0:T(8,128)(2,1)S(1)}, bf16[2,128,128]{2,1,0:T(8,128)(2,1)S(1)}, u32[]{:S(2)}, u32[]{:S(2)}) collective-permute-start(bf16[2,128,128]{2,1,0:T(8,128)(2,1)S(1)} %get-tuple-element.47), channel_id=1, source_target_pairs={{0,6},{1,7},{2,4},{3,5},{4,2},{5,3},{6,0},{7,1},{8,14},{9,15},{10,... | collective-permute-start | bytes 196616 | tf_op jit(solution)/shard_map/ppermute | solution.py:22
  9.1 2.8 %collective-permute-done.2 = bf16[2,128,128]{2,1,0:T(8,128)(2,1)S(1)} collective-permute-done((bf16[2,128,128]{2,1,0:T(8,128)(2,1)S(1)}, bf16[2,128,128]{2,1,0:T(8,128)(2,1)S(1)}, u32[]{:S(2)}, u32[]{:S(2)}) %collective-permute-start.2) | collective-permute-done | bytes 65568 | tf_op jit(solution)/shard_map/ppermute | solution.py:22
  12.0 2.8 %collective-permute-start.6 = (bf16[4,2,128,128]{3,2,1,0:T(8,128)(2,1)S(1)}, bf16[4,2,128,128]{3,2,1,0:T(8,128)(2,1)S(1)}, u32[]{:S(2)}, u32[]{:S(2)}) collective-permute-start(bf16[4,2,128,128]{3,2,1,0:T(8,128)(2,1)S(1)} %get-tuple-element.36), channel_id=1, source_target_pairs={{0,24},{1,25},{2,26},{3,27},{4,28},{5,29},{6,30},{7,31},{8,16},{9,... | collective-permute-start | bytes 786440 | tf_op jit(solution)/shard_map/ppermute | solution.py:22
  16.8 2.2 %copy-done = bf16[1,1,128,128,128]{4,3,2,1,0:T(8,128)(2,1)S(1)} copy-done((bf16[1,1,128,128,128]{4,3,2,1,0:T(8,128)(2,1)S(1)}, bf16[1,1,128,128,128]{4,3,2,1,0:T(8,128)(2,1)}, u32[]{:S(2)}) %copy-start) | copy-done | bytes 4194328
  19.0 1.8 %spread.1 = bf16[1024,4096]{1,0:T(8,128)(2,1)S(1)} custom-call(s32[1]{0:T(128)} %bitcast.59.count_ref, s32[128]{0:T(128)S(1)} %get-tuple-element.55.put_row, s32[128]{0:T(128)S(1)} %get-tuple-element.54.put_col, bf16[128,128,128]{2,1,0:T(8,128)(2,1)S(1)} %bitcast.60), custom_call_target="tpu_custom_call" | custom-call | bytes 12582912 | tf_op jit(solution)/shard_map/spread/pallas_call | solution.py:63
  22.5 2.3 %fusion.19 = f32[1024,128]{1,0:T(8,128)S(1)} fusion(bf16[1024,4096]{1,0:T(8,128)(2,1)S(1)} %spread.1, bf16[4096,128]{1,0:T(8,128)(2,1)S(1)} %bitcast.64), kind=kOutput, calls=%fused_computation.97 | convolution fusion | flops 1073741824 | bytes 9961472 | tf_op jit(solution)/shard_map/dot_general | solution.py:215
  24.9 4.4 %collective-permute-start.7 = (bf16[4,128,128]{2,1,0:T(8,128)(2,1)S(1)}, bf16[4,128,128]{2,1,0:T(8,128)(2,1)S(1)}, u32[]{:S(2)}, u32[]{:S(2)}) collective-permute-start(bf16[4,128,128]{2,1,0:T(8,128)(2,1)S(1)} %bitcast.68), channel_id=1, source_target_pairs={{0,32},{32,0},{64,96},{96,64},{128,160},{160,128},{192,224},{224,1... | collective-permute-start | bytes 393224 | tf_op jit(solution)/shard_map/ppermute | solution.py:30
  30.3 3.1 %collective-permute-start.8 = (bf16[128,128]{1,0:T(8,128)(2,1)S(1)}, bf16[128,128]{1,0:T(8,128)(2,1)S(1)}, u32[]{:S(2)}, u32[]{:S(2)}) collective-permute-start(bf16[128,128]{1,0:T(8,128)(2,1)S(1)} %get-tuple-element.39), channel_id=1, source_target_pairs={{0,64},{32,96},{64,0},{96,32},{128,192},{160,224},{192,128},{224,1... | collective-permute-start | bytes 98312 | tf_op jit(solution)/shard_map/ppermute | solution.py:26
  33.4 5.1 %collective-permute-start.9 = (bf16[128,128]{1,0:T(8,128)(2,1)S(1)}, bf16[128,128]{1,0:T(8,128)(2,1)S(1)}, u32[]{:S(2)}, u32[]{:S(2)}) collective-permute-start(bf16[128,128]{1,0:T(8,128)(2,1)S(1)} %get-tuple-element.38), channel_id=1, source_target_pairs={{0,128},{32,160},{64,192},{96,224},{128,0},{160,32},{192,64},{224,... | collective-permute-start | bytes 98312 | tf_op jit(solution)/shard_map/ppermute | solution.py:26
  38.5 1.7 %collective-permute-done.9.in2 = bf16[128,128]{1,0:T(8,128)(2,1)S(1)} collective-permute-done((bf16[128,128]{1,0:T(8,128)(2,1)S(1)}, bf16[128,128]{1,0:T(8,128)(2,1)S(1)}, u32[]{:S(2)}, u32[]{:S(2)}) %collective-permute-start.9) | collective-permute-done | bytes 32800 | tf_op jit(solution)/shard_map/ppermute | solution.py:26
  40.2 3.2 %collective-permute-done.10.in3 = bf16[128,128]{1,0:T(8,128)(2,1)S(1)} collective-permute-done((bf16[128,128]{1,0:T(8,128)(2,1)S(1)}, bf16[128,128]{1,0:T(8,128)(2,1)S(1)}, u32[]{:S(2)}, u32[]{:S(2)}) %collective-permute-start.10) | collective-permute-done | bytes 32800 | tf_op jit(solution)/shard_map/ppermute | solution.py:26
  43.4 1.5 %middle.1 = (bf16[128,512]{1,0:T(8,128)(2,1)}, bf16[4,272,128]{2,1,0:T(8,128)(2,1)S(1)}, f32[144,128]{1,0:T(8,128)S(1)}) custom-call(s32[2]{0:T(128)S(1)} %pad_add_fusion.place, f32[128,128]{1,0:T(8,128)S(1)} %slice_bitcast_fusion.3.own, bf16[128,128]{1,0:T(8,128)(2,1)S(1)} %collective-permute-done.8.in1, bf16[128,128]{1,0:T(8,128)(2,1)S(1)} %collective-permute-done.9.in2, ...), custom_call_target="tpu_custom_call" | custom-call | flops 83886080 | bytes 655360 | tf_op jit(solution)/shard_map/middle/pallas_call | solution.py:125
  46.0 3.5 %collective-permute-start.12 = (bf16[272,128]{1,0:T(8,128)(2,1)S(1)}, bf16[272,128]{1,0:T(8,128)(2,1)S(1)}, u32[]{:S(2)}, u32[]{:S(2)}) collective-permute-start(bf16[272,128]{1,0:T(8,128)(2,1)S(1)} %get-tuple-element.31), channel_id=1, source_target_pairs={{0,128},{32,160},{64,192},{96,224},{128,0},{160,32},{192,64},{224,... | collective-permute-start | bytes 208904 | tf_op jit(solution)/shard_map/ppermute | solution.py:26
  49.4 1.2 %collective-permute-start.11 = (bf16[272,128]{1,0:T(8,128)(2,1)S(1)}, bf16[272,128]{1,0:T(8,128)(2,1)S(1)}, u32[]{:S(2)}, u32[]{:S(2)}) collective-permute-start(bf16[272,128]{1,0:T(8,128)(2,1)S(1)} %get-tuple-element.29), channel_id=1, source_target_pairs={{0,64},{32,96},{64,0},{96,32},{128,192},{160,224},{192,128},{224,1... | collective-permute-start | bytes 208904 | tf_op jit(solution)/shard_map/ppermute | solution.py:26
  50.6 2.5 %collective-permute-done.12 = bf16[272,128]{1,0:T(8,128)(2,1)S(1)} collective-permute-done((bf16[272,128]{1,0:T(8,128)(2,1)S(1)}, bf16[272,128]{1,0:T(8,128)(2,1)S(1)}, u32[]{:S(2)}, u32[]{:S(2)}) %collective-permute-start.12) | collective-permute-done | bytes 69664 | tf_op jit(solution)/shard_map/ppermute | solution.py:26
  53.1 2.1 %collective-permute-done.11 = bf16[272,128]{1,0:T(8,128)(2,1)S(1)} collective-permute-done((bf16[272,128]{1,0:T(8,128)(2,1)S(1)}, bf16[272,128]{1,0:T(8,128)(2,1)S(1)}, u32[]{:S(2)}, u32[]{:S(2)}) %collective-permute-start.11) | collective-permute-done | bytes 69664 | tf_op jit(solution)/shard_map/ppermute | solution.py:26
  55.4 3.7 %collective-permute-start.14 = (bf16[672,128]{1,0:T(8,128)(2,1)S(1)}, bf16[672,128]{1,0:T(8,128)(2,1)S(1)}, u32[]{:S(2)}, u32[]{:S(2)}) collective-permute-start(bf16[672,128]{1,0:T(8,128)(2,1)S(1)} %constant_dynamic-update-slice_fusion), channel_id=1, source_target_pairs={{0,32},{32,0},{64,96},{96,64},{128,160},{160,128},{192,224},{224,1... | collective-permute-start | bytes 516104 | tf_op jit(solution)/shard_map/ppermute | solution.py:30
  60.4 2.4 %fusion.18 = (bf16[4096,128]{1,0:T(8,128)(2,1)S(1)}, f32[4096,128]{1,0:T(8,128)S(1)}) fusion(bf16[1024,4096]{1,0:T(8,128)(2,1)S(1)} %spread.1, bf16[1024,128]{1,0:T(8,128)(2,1)S(1)} %slice_dynamic-update-slice_fusion), kind=kOutput, calls=%fused_computation.96 | convolution fusion | flops 1074266112 | bytes 11796480 | tf_op jit(solution)/shard_map/dot_general | solution.py:231
  63.3 1.1 %collective-permute-start.18 = (bf16[1104,128]{1,0:T(8,128)(2,1)S(1)}, bf16[1104,128]{1,0:T(8,128)(2,1)S(1)}, u32[]{:S(2)}, u32[]{:S(2)}) collective-permute-start(bf16[1104,128]{1,0:T(8,128)(2,1)S(1)} %get-tuple-element.53), channel_id=1, source_target_pairs={{0,24},{1,25},{2,26},{3,27},{4,28},{5,29},{6,30},{7,31},{8,16},{9,... | collective-permute-start | bytes 847880 | tf_op jit(solution)/shard_map/ppermute | solution.py:22
  65.2 1.4 %collective-permute-start.16 = (bf16[1104,128]{1,0:T(8,128)(2,1)S(1)}, bf16[1104,128]{1,0:T(8,128)(2,1)S(1)}, u32[]{:S(2)}, u32[]{:S(2)}) collective-permute-start(bf16[1104,128]{1,0:T(8,128)(2,1)S(1)} %get-tuple-element.51), channel_id=1, source_target_pairs={{0,8},{1,9},{2,10},{3,11},{4,12},{5,13},{6,14},{7,15},{8,0},{9,1},... | collective-permute-start | bytes 847880 | tf_op jit(solution)/shard_map/ppermute | solution.py:22
  66.7 6.7 %collective-permute-done.18 = bf16[1104,128]{1,0:T(8,128)(2,1)S(1)} collective-permute-done((bf16[1104,128]{1,0:T(8,128)(2,1)S(1)}, bf16[1104,128]{1,0:T(8,128)(2,1)S(1)}, u32[]{:S(2)}, u32[]{:S(2)}) %collective-permute-start.18) | collective-permute-done | bytes 282656 | tf_op jit(solution)/shard_map/ppermute | solution.py:22
  74.2 2.6 %collective-permute-start.21 = (bf16[336,128]{1,0:T(8,128)(2,1)S(1)}, bf16[336,128]{1,0:T(8,128)(2,1)S(1)}, u32[]{:S(2)}, u32[]{:S(2)}) collective-permute-start(bf16[336,128]{1,0:T(8,128)(2,1)S(1)} %get-tuple-element.50), channel_id=1, source_target_pairs={{0,6},{1,7},{2,4},{3,5},{4,2},{5,3},{6,0},{7,1},{8,14},{9,15},{10,... | collective-permute-start | bytes 258056 | tf_op jit(solution)/shard_map/ppermute | solution.py:22
  77.6 1.6 %collective-permute-done.21 = bf16[336,128]{1,0:T(8,128)(2,1)S(1)} collective-permute-done((bf16[336,128]{1,0:T(8,128)(2,1)S(1)}, bf16[336,128]{1,0:T(8,128)(2,1)S(1)}, u32[]{:S(2)}, u32[]{:S(2)}) %collective-permute-start.21) | collective-permute-done | bytes 86048 | tf_op jit(solution)/shard_map/ppermute | solution.py:22
  79.1 2.5 %collective-permute-done.20 = bf16[336,128]{1,0:T(8,128)(2,1)S(1)} collective-permute-done((bf16[336,128]{1,0:T(8,128)(2,1)S(1)}, bf16[336,128]{1,0:T(8,128)(2,1)S(1)}, u32[]{:S(2)}, u32[]{:S(2)}) %collective-permute-start.20) | collective-permute-done | bytes 86048 | tf_op jit(solution)/shard_map/ppermute | solution.py:22
  81.7 1.6 %collective-permute-start.23 = (bf16[64,128]{1,0:T(8,128)(2,1)S(1)}, bf16[64,128]{1,0:T(8,128)(2,1)S(1)}, u32[]{:S(2)}, u32[]{:S(2)}) collective-permute-start(bf16[64,128]{1,0:T(8,128)(2,1)S(1)} %get-tuple-element.19), channel_id=1, source_target_pairs={{0,64},{32,96},{64,0},{96,32},{128,192},{160,224},{192,128},{224,1... | collective-permute-start | bytes 49160 | tf_op jit(solution)/shard_map/ppermute | solution.py:26
  83.3 2.4 %collective-permute-start.24 = (bf16[64,128]{1,0:T(8,128)(2,1)S(1)}, bf16[64,128]{1,0:T(8,128)(2,1)S(1)}, u32[]{:S(2)}, u32[]{:S(2)}) collective-permute-start(bf16[64,128]{1,0:T(8,128)(2,1)S(1)} %get-tuple-element.19), channel_id=1, source_target_pairs={{0,128},{32,160},{64,192},{96,224},{128,0},{160,32},{192,64},{224,... | collective-permute-start | bytes 49160 | tf_op jit(solution)/shard_map/ppermute | solution.py:26
  85.7 1.7 %collective-permute-start.25 = (bf16[64,128]{1,0:T(8,128)(2,1)S(1)}, bf16[64,128]{1,0:T(8,128)(2,1)S(1)}, u32[]{:S(2)}, u32[]{:S(2)}) collective-permute-start(bf16[64,128]{1,0:T(8,128)(2,1)S(1)} %get-tuple-element.19), channel_id=1, source_target_pairs={{0,192},{32,224},{64,128},{96,160},{128,64},{160,96},{192,0},{224,... | collective-permute-start | bytes 49160 | tf_op jit(solution)/shard_map/ppermute | solution.py:26
  87.5 1.2 %collective-permute-start.22 = (bf16[128,128]{1,0:T(8,128)(2,1)S(1)}, bf16[128,128]{1,0:T(8,128)(2,1)S(1)}, u32[]{:S(2)}, u32[]{:S(2)}) collective-permute-start(bf16[128,128]{1,0:T(8,128)(2,1)S(1)} %slice.295), channel_id=1, source_target_pairs={{0,1},{1,0},{2,3},{3,2},{4,5},{5,4},{6,7},{7,6},{8,9},{9,8},{10,11... | collective-permute-start | bytes 98312 | tf_op jit(solution)/shard_map/ppermute | solution.py:34
  88.7 1.1 %collective-permute-done.24.two = bf16[64,128]{1,0:T(8,128)(2,1)S(1)} collective-permute-done((bf16[64,128]{1,0:T(8,128)(2,1)S(1)}, bf16[64,128]{1,0:T(8,128)(2,1)S(1)}, u32[]{:S(2)}, u32[]{:S(2)}) %collective-permute-start.24) | collective-permute-done | bytes 16416 | tf_op jit(solution)/shard_map/ppermute | solution.py:26
  90.4 4.1 %collective-permute-start.26 = (bf16[272,128]{1,0:T(8,128)(2,1)S(1)}, bf16[272,128]{1,0:T(8,128)(2,1)S(1)}, u32[]{:S(2)}, u32[]{:S(2)}) collective-permute-start(bf16[272,128]{1,0:T(8,128)(2,1)S(1)} %get-tuple-element.14), channel_id=1, source_target_pairs={{0,32},{32,0},{64,96},{96,64},{128,160},{160,128},{192,224},{224,1... | collective-permute-start | bytes 208904 | tf_op jit(solution)/shard_map/ppermute | solution.py:30
  95.5 1.3 %settle.1 = (f32[128,512]{1,0:T(8,128)}, f32[1,512]{1,0:T(1,128)}) custom-call(s32[2]{0:T(128)S(1)} %pad_add_fusion.place, bf16[80,128]{1,0:T(8,128)(2,1)S(1)} %pad_maximum_fusion.9.own, bf16[64,128]{1,0:T(8,128)(2,1)S(1)} %collective-permute-done.23.one, bf16[64,128]{1,0:T(8,128)(2,1)S(1)} %collective-permute-done.24.two, ...), custom_call_target="tpu_custom_call" | custom-call | tf_op jit(solution)/shard_map/settle/pallas_call | solution.py:163
  (78 shorter events, 14.5 us)
Async XLA Ops:
  0.6 4.1 %collective-permute-start = (bf16[128,128]{1,0:T(8,128)(2,1)}, bf16[128,128]{1,0:T(8,128)(2,1)S(1)}, u32[]{:S(2)}, u32[]{:S(2)}) collective-permute-start(bf16[128,128]{1,0:T(8,128)(2,1)} %v_ref.1), channel_id=1, source_target_pairs={{0,1},{1,0},{2,3},{3,2},{4,5},{5,4},{6,7},{7,6},{8,9},{9,8},{10,11... | collective-permute-start | bytes 98312 | tf_op jit(solution)/shard_map/ppermute | solution.py:34
  3.2 0.8 copy-start.3
  4.7 4.4 %collective-permute-start.3 = (bf16[2,128,128]{2,1,0:T(8,128)(2,1)S(1)}, bf16[2,128,128]{2,1,0:T(8,128)(2,1)S(1)}, u32[]{:S(2)}, u32[]{:S(2)}) collective-permute-start(bf16[2,128,128]{2,1,0:T(8,128)(2,1)S(1)} %get-tuple-element.47), channel_id=1, source_target_pairs={{0,6},{1,7},{2,4},{3,5},{4,2},{5,3},{6,0},{7,1},{8,14},{9,15},{10,... | collective-permute-start | bytes 196616 | tf_op jit(solution)/shard_map/ppermute | solution.py:22
  7.3 4.6 %collective-permute-start.2 = (bf16[2,128,128]{2,1,0:T(8,128)(2,1)S(1)}, bf16[2,128,128]{2,1,0:T(8,128)(2,1)S(1)}, u32[]{:S(2)}, u32[]{:S(2)}) collective-permute-start(bf16[2,128,128]{2,1,0:T(8,128)(2,1)S(1)} %get-tuple-element.47), channel_id=1, source_target_pairs={{0,4},{1,5},{2,6},{3,7},{4,0},{5,1},{6,2},{7,3},{8,12},{9,13},{10,... | collective-permute-start | bytes 196616 | tf_op jit(solution)/shard_map/ppermute | solution.py:22
  7.8 4.1 %collective-permute-start.1 = (bf16[2,128,128]{2,1,0:T(8,128)(2,1)S(1)}, bf16[2,128,128]{2,1,0:T(8,128)(2,1)S(1)}, u32[]{:S(2)}, u32[]{:S(2)}) collective-permute-start(bf16[2,128,128]{2,1,0:T(8,128)(2,1)S(1)} %get-tuple-element.47), channel_id=1, source_target_pairs={{0,2},{1,3},{2,0},{3,1},{4,6},{5,7},{6,4},{7,5},{8,10},{9,11},{10,... | collective-permute-start | bytes 196616 | tf_op jit(solution)/shard_map/ppermute | solution.py:22
  12.0 8.9 %collective-permute-start.6 = (bf16[4,2,128,128]{3,2,1,0:T(8,128)(2,1)S(1)}, bf16[4,2,128,128]{3,2,1,0:T(8,128)(2,1)S(1)}, u32[]{:S(2)}, u32[]{:S(2)}) collective-permute-start(bf16[4,2,128,128]{3,2,1,0:T(8,128)(2,1)S(1)} %get-tuple-element.36), channel_id=1, source_target_pairs={{0,24},{1,25},{2,26},{3,27},{4,28},{5,29},{6,30},{7,31},{8,16},{9,... | collective-permute-start | bytes 786440 | tf_op jit(solution)/shard_map/ppermute | solution.py:22
  14.8 6.7 %collective-permute-start.5 = (bf16[4,2,128,128]{3,2,1,0:T(8,128)(2,1)S(1)}, bf16[4,2,128,128]{3,2,1,0:T(8,128)(2,1)S(1)}, u32[]{:S(2)}, u32[]{:S(2)}) collective-permute-start(bf16[4,2,128,128]{3,2,1,0:T(8,128)(2,1)S(1)} %get-tuple-element.36), channel_id=1, source_target_pairs={{0,16},{1,17},{2,18},{3,19},{4,20},{5,21},{6,22},{7,23},{8,24},{9,... | collective-permute-start | bytes 786440 | tf_op jit(solution)/shard_map/ppermute | solution.py:22
  15.1 7.2 %collective-permute-start.4 = (bf16[4,2,128,128]{3,2,1,0:T(8,128)(2,1)S(1)}, bf16[4,2,128,128]{3,2,1,0:T(8,128)(2,1)S(1)}, u32[]{:S(2)}, u32[]{:S(2)}) collective-permute-start(bf16[4,2,128,128]{3,2,1,0:T(8,128)(2,1)S(1)} %get-tuple-element.36), channel_id=1, source_target_pairs={{0,8},{1,9},{2,10},{3,11},{4,12},{5,13},{6,14},{7,15},{8,0},{9,1},... | collective-permute-start | bytes 786440 | tf_op jit(solution)/shard_map/ppermute | solution.py:22
  16.8 2.2 %copy-start = (bf16[1,1,128,128,128]{4,3,2,1,0:T(8,128)(2,1)S(1)}, bf16[1,1,128,128,128]{4,3,2,1,0:T(8,128)(2,1)}, u32[]{:S(2)}) copy-start(bf16[1,1,128,128,128]{4,3,2,1,0:T(8,128)(2,1)} %param.10) | copy-start | bytes 12582916
  20.8 22.6 %copy-start.1 = (bf16[128,512]{1,0:T(8,128)(2,1)S(1)}, bf16[128,512]{1,0:T(8,128)(2,1)}, u32[]{:S(2)}) copy-start(bf16[128,512]{1,0:T(8,128)(2,1)} %weight.1) | copy-start | bytes 393220
  20.8 22.6 %copy-start.2 = (bf16[128,512]{1,0:T(8,128)(2,1)S(1)}, bf16[128,512]{1,0:T(8,128)(2,1)}, u32[]{:S(2)}) copy-start(bf16[128,512]{1,0:T(8,128)(2,1)} %cot.1) | copy-start | bytes 393220
  20.8 22.5 %copy-start.4 = (f32[512]{0:T(512)S(1)}, f32[512]{0:T(512)}, u32[]{:S(2)}) copy-start(f32[512]{0:T(512)} %param.9) | copy-start | bytes 6148
  24.9 5.4 %collective-permute-start.7 = (bf16[4,128,128]{2,1,0:T(8,128)(2,1)S(1)}, bf16[4,128,128]{2,1,0:T(8,128)(2,1)S(1)}, u32[]{:S(2)}, u32[]{:S(2)}) collective-permute-start(bf16[4,128,128]{2,1,0:T(8,128)(2,1)S(1)} %bitcast.68), channel_id=1, source_target_pairs={{0,32},{32,0},{64,96},{96,64},{128,160},{160,128},{192,224},{224,1... | collective-permute-start | bytes 393224 | tf_op jit(solution)/shard_map/ppermute | solution.py:30
  30.3 8.2 %collective-permute-start.8 = (bf16[128,128]{1,0:T(8,128)(2,1)S(1)}, bf16[128,128]{1,0:T(8,128)(2,1)S(1)}, u32[]{:S(2)}, u32[]{:S(2)}) collective-permute-start(bf16[128,128]{1,0:T(8,128)(2,1)S(1)} %get-tuple-element.39), channel_id=1, source_target_pairs={{0,64},{32,96},{64,0},{96,32},{128,192},{160,224},{192,128},{224,1... | collective-permute-start | bytes 98312 | tf_op jit(solution)/shard_map/ppermute | solution.py:26
  33.4 6.8 %collective-permute-start.9 = (bf16[128,128]{1,0:T(8,128)(2,1)S(1)}, bf16[128,128]{1,0:T(8,128)(2,1)S(1)}, u32[]{:S(2)}, u32[]{:S(2)}) collective-permute-start(bf16[128,128]{1,0:T(8,128)(2,1)S(1)} %get-tuple-element.38), channel_id=1, source_target_pairs={{0,128},{32,160},{64,192},{96,224},{128,0},{160,32},{192,64},{224,... | collective-permute-start | bytes 98312 | tf_op jit(solution)/shard_map/ppermute | solution.py:26
  38.5 4.9 %collective-permute-start.10 = (bf16[128,128]{1,0:T(8,128)(2,1)S(1)}, bf16[128,128]{1,0:T(8,128)(2,1)S(1)}, u32[]{:S(2)}, u32[]{:S(2)}) collective-permute-start(bf16[128,128]{1,0:T(8,128)(2,1)S(1)} %get-tuple-element.37), channel_id=1, source_target_pairs={{0,192},{32,224},{64,128},{96,160},{128,64},{160,96},{192,0},{224,... | collective-permute-start | bytes 98312 | tf_op jit(solution)/shard_map/ppermute | solution.py:26
  44.9 5.8 %collective-permute-start.13 = (bf16[272,128]{1,0:T(8,128)(2,1)S(1)}, bf16[272,128]{1,0:T(8,128)(2,1)S(1)}, u32[]{:S(2)}, u32[]{:S(2)}) collective-permute-start(bf16[272,128]{1,0:T(8,128)(2,1)S(1)} %get-tuple-element.30), channel_id=1, source_target_pairs={{0,192},{32,224},{64,128},{96,160},{128,64},{160,96},{192,0},{224,... | collective-permute-start | bytes 208904 | tf_op jit(solution)/shard_map/ppermute | solution.py:26
  46.0 7.2 %collective-permute-start.12 = (bf16[272,128]{1,0:T(8,128)(2,1)S(1)}, bf16[272,128]{1,0:T(8,128)(2,1)S(1)}, u32[]{:S(2)}, u32[]{:S(2)}) collective-permute-start(bf16[272,128]{1,0:T(8,128)(2,1)S(1)} %get-tuple-element.31), channel_id=1, source_target_pairs={{0,128},{32,160},{64,192},{96,224},{128,0},{160,32},{192,64},{224,... | collective-permute-start | bytes 208904 | tf_op jit(solution)/shard_map/ppermute | solution.py:26
  49.4 5.8 %collective-permute-start.11 = (bf16[272,128]{1,0:T(8,128)(2,1)S(1)}, bf16[272,128]{1,0:T(8,128)(2,1)S(1)}, u32[]{:S(2)}, u32[]{:S(2)}) collective-permute-start(bf16[272,128]{1,0:T(8,128)(2,1)S(1)} %get-tuple-element.29), channel_id=1, source_target_pairs={{0,64},{32,96},{64,0},{96,32},{128,192},{160,224},{192,128},{224,1... | collective-permute-start | bytes 208904 | tf_op jit(solution)/shard_map/ppermute | solution.py:26
  55.4 4.7 %collective-permute-start.14 = (bf16[672,128]{1,0:T(8,128)(2,1)S(1)}, bf16[672,128]{1,0:T(8,128)(2,1)S(1)}, u32[]{:S(2)}, u32[]{:S(2)}) collective-permute-start(bf16[672,128]{1,0:T(8,128)(2,1)S(1)} %constant_dynamic-update-slice_fusion), channel_id=1, source_target_pairs={{0,32},{32,0},{64,96},{96,64},{128,160},{160,128},{192,224},{224,1... | collective-permute-start | bytes 516104 | tf_op jit(solution)/shard_map/ppermute | solution.py:30
  60.1 3.1 %collective-permute-start.15 = (f32[80,128]{1,0:T(8,128)S(1)}, f32[80,128]{1,0:T(8,128)S(1)}, u32[]{:S(2)}, u32[]{:S(2)}) collective-permute-start(f32[80,128]{1,0:T(8,128)S(1)} %maximum_add_fusion), channel_id=1, source_target_pairs={{0,1},{1,0},{2,3},{3,2},{4,5},{5,4},{6,7},{7,6},{8,9},{9,8},{10,11... | collective-permute-start | bytes 122888 | tf_op jit(solution)/shard_map/ppermute | solution.py:34
  63.3 10.1 %collective-permute-start.18 = (bf16[1104,128]{1,0:T(8,128)(2,1)S(1)}, bf16[1104,128]{1,0:T(8,128)(2,1)S(1)}, u32[]{:S(2)}, u32[]{:S(2)}) collective-permute-start(bf16[1104,128]{1,0:T(8,128)(2,1)S(1)} %get-tuple-element.53), channel_id=1, source_target_pairs={{0,24},{1,25},{2,26},{3,27},{4,28},{5,29},{6,30},{7,31},{8,16},{9,... | collective-permute-start | bytes 847880 | tf_op jit(solution)/shard_map/ppermute | solution.py:22
  64.4 9.0 %collective-permute-start.17 = (bf16[1104,128]{1,0:T(8,128)(2,1)S(1)}, bf16[1104,128]{1,0:T(8,128)(2,1)S(1)}, u32[]{:S(2)}, u32[]{:S(2)}) collective-permute-start(bf16[1104,128]{1,0:T(8,128)(2,1)S(1)} %get-tuple-element.52), channel_id=1, source_target_pairs={{0,16},{1,17},{2,18},{3,19},{4,20},{5,21},{6,22},{7,23},{8,24},{9,... | collective-permute-start | bytes 847880 | tf_op jit(solution)/shard_map/ppermute | solution.py:22
  65.2 8.8 %collective-permute-start.16 = (bf16[1104,128]{1,0:T(8,128)(2,1)S(1)}, bf16[1104,128]{1,0:T(8,128)(2,1)S(1)}, u32[]{:S(2)}, u32[]{:S(2)}) collective-permute-start(bf16[1104,128]{1,0:T(8,128)(2,1)S(1)} %get-tuple-element.51), channel_id=1, source_target_pairs={{0,8},{1,9},{2,10},{3,11},{4,12},{5,13},{6,14},{7,15},{8,0},{9,1},... | collective-permute-start | bytes 847880 | tf_op jit(solution)/shard_map/ppermute | solution.py:22
  74.2 4.9 %collective-permute-start.21 = (bf16[336,128]{1,0:T(8,128)(2,1)S(1)}, bf16[336,128]{1,0:T(8,128)(2,1)S(1)}, u32[]{:S(2)}, u32[]{:S(2)}) collective-permute-start(bf16[336,128]{1,0:T(8,128)(2,1)S(1)} %get-tuple-element.50), channel_id=1, source_target_pairs={{0,6},{1,7},{2,4},{3,5},{4,2},{5,3},{6,0},{7,1},{8,14},{9,15},{10,... | collective-permute-start | bytes 258056 | tf_op jit(solution)/shard_map/ppermute | solution.py:22
  76.8 4.8 %collective-permute-start.20 = (bf16[336,128]{1,0:T(8,128)(2,1)S(1)}, bf16[336,128]{1,0:T(8,128)(2,1)S(1)}, u32[]{:S(2)}, u32[]{:S(2)}) collective-permute-start(bf16[336,128]{1,0:T(8,128)(2,1)S(1)} %get-tuple-element.49), channel_id=1, source_target_pairs={{0,4},{1,5},{2,6},{3,7},{4,0},{5,1},{6,2},{7,3},{8,12},{9,13},{10,... | collective-permute-start | bytes 258056 | tf_op jit(solution)/shard_map/ppermute | solution.py:22
  77.3 4.3 %collective-permute-start.19 = (bf16[336,128]{1,0:T(8,128)(2,1)S(1)}, bf16[336,128]{1,0:T(8,128)(2,1)S(1)}, u32[]{:S(2)}, u32[]{:S(2)}) collective-permute-start(bf16[336,128]{1,0:T(8,128)(2,1)S(1)} %get-tuple-element.48), channel_id=1, source_target_pairs={{0,2},{1,3},{2,0},{3,1},{4,6},{5,7},{6,4},{7,5},{8,10},{9,11},{10,... | collective-permute-start | bytes 258056 | tf_op jit(solution)/shard_map/ppermute | solution.py:22
  81.7 7.0 %collective-permute-start.23 = (bf16[64,128]{1,0:T(8,128)(2,1)S(1)}, bf16[64,128]{1,0:T(8,128)(2,1)S(1)}, u32[]{:S(2)}, u32[]{:S(2)}) collective-permute-start(bf16[64,128]{1,0:T(8,128)(2,1)S(1)} %get-tuple-element.19), channel_id=1, source_target_pairs={{0,64},{32,96},{64,0},{96,32},{128,192},{160,224},{192,128},{224,1... | collective-permute-start | bytes 49160 | tf_op jit(solution)/shard_map/ppermute | solution.py:26
  83.3 6.5 %collective-permute-start.24 = (bf16[64,128]{1,0:T(8,128)(2,1)S(1)}, bf16[64,128]{1,0:T(8,128)(2,1)S(1)}, u32[]{:S(2)}, u32[]{:S(2)}) collective-permute-start(bf16[64,128]{1,0:T(8,128)(2,1)S(1)} %get-tuple-element.19), channel_id=1, source_target_pairs={{0,128},{32,160},{64,192},{96,224},{128,0},{160,32},{192,64},{224,... | collective-permute-start | bytes 49160 | tf_op jit(solution)/shard_map/ppermute | solution.py:26
  85.7 4.7 %collective-permute-start.25 = (bf16[64,128]{1,0:T(8,128)(2,1)S(1)}, bf16[64,128]{1,0:T(8,128)(2,1)S(1)}, u32[]{:S(2)}, u32[]{:S(2)}) collective-permute-start(bf16[64,128]{1,0:T(8,128)(2,1)S(1)} %get-tuple-element.19), channel_id=1, source_target_pairs={{0,192},{32,224},{64,128},{96,160},{128,64},{160,96},{192,0},{224,... | collective-permute-start | bytes 49160 | tf_op jit(solution)/shard_map/ppermute | solution.py:26
  87.5 7.1 %collective-permute-start.22 = (bf16[128,128]{1,0:T(8,128)(2,1)S(1)}, bf16[128,128]{1,0:T(8,128)(2,1)S(1)}, u32[]{:S(2)}, u32[]{:S(2)}) collective-permute-start(bf16[128,128]{1,0:T(8,128)(2,1)S(1)} %slice.295), channel_id=1, source_target_pairs={{0,1},{1,0},{2,3},{3,2},{4,5},{5,4},{6,7},{7,6},{8,9},{9,8},{10,11... | collective-permute-start | bytes 98312 | tf_op jit(solution)/shard_map/ppermute | solution.py:34
  90.4 5.0 %collective-permute-start.26 = (bf16[272,128]{1,0:T(8,128)(2,1)S(1)}, bf16[272,128]{1,0:T(8,128)(2,1)S(1)}, u32[]{:S(2)}, u32[]{:S(2)}) collective-permute-start(bf16[272,128]{1,0:T(8,128)(2,1)S(1)} %get-tuple-element.14), channel_id=1, source_target_pairs={{0,32},{32,0},{64,96},{96,64},{128,160},{160,128},{192,224},{224,1... | collective-permute-start | bytes 208904 | tf_op jit(solution)/shard_map/ppermute | solution.py:30

commit v4 on v3

--- a/solution.py
+++ b/solution.py
@@ -204,21 +204,23 @@
     far_x, far_y, far_z = x ^ (tile_col // 8), y ^ ((tile_col // 2) % 4), z ^ (tile_col % 2)
     put_row = (far_k * 4 + far_h).astype(jnp.int32)
     first, second = jnp.where(k == 0, far_y, far_x), jnp.where(k == 0, far_x, far_y)
+    second = second ^ (second >> 1)
     put_col = (second * 8 + first * 2 + far_z).astype(jnp.int32)
     dense = spread(tile_values[0, 0], tile_count[0], put_row, put_col, 8, 32)
 
     source = jnp.stack([near_copy(features), swap_z(features)])
     for turn in (0, 1):
-        source = jnp.stack([source] + [swap_xy(source, bits, turn) for bits in (1, 2, 3)])
+        source = jnp.stack([source] + [swap_xy(source, bits, turn) for bits in ((1, 3, 2) if turn else (1, 2, 3))])
     source = source.reshape(-1, feats)
 
     part = jnp.dot(dense, source, preferred_element_type=F32).reshape(2, 4, size, feats)
     half = part[0] + swap_k(part[1].astype(BF)).astype(F32)
     sent = half.astype(BF)
-    arrived = [swap_h(sent[s], s) for s in (1, 2, 3)]
+    arrived = [swap_h(sent[s], s) for s in (2, 3, 1)]
     hidden_out, sent, gw = middle(here, half[0], arrived, weight, bias, cotangent)
 
-    arrived = [swap_h(sent[s], s) for s in (1, 2, 3)]
+    one, three, two = [swap_h(sent[s], s) for s in (1, 3, 2)]
+    arrived = [one, two, three]
     target = jnp.concatenate([sent[0][:size]] + [v[:size] for v in arrived])
     gw = gw + sum(v[size:].astype(F32) for v in arrived)
     share = (gw.shape[0] - 16) // 2
@@ -233,15 +235,17 @@
         grad = grad.reshape(4, -1, feats)
         rows = grad.shape[1]
         low, extra = grad.astype(BF), gw.astype(BF)
-        arrived = [swap_xy(jnp.concatenate([low[s], extra]), s, turn) for s in (1, 2, 3)]
+        order = (1, 3, 2) if turn else (1, 2, 3)
+        arrived = [swap_xy(jnp.concatenate([low[i + 1], extra]), order[i], turn) for i in range(3)]
         grad = grad[0] + sum(v[:rows].astype(F32) for v in arrived)
-        one, two, three = [v[rows:].astype(F32) for v in arrived]
+        one, two, three = [arrived[order.index(bits)][rows:].astype(F32) for bits in (1, 2, 3)]
         gw = (extra.astype(F32) + two) + (one + three)
     grad_features = (grad[:size] + swap_z(grad[size:].astype(BF)).astype(F32)).astype(BF)
 
     sums = pair(gw[share : share + 8])
     gw = gw[:share].astype(BF)
-    arrived = [swap_h(gw, s) for s in (1, 2, 3)]
+    three, two, one = [swap_h(gw, s) for s in (3, 2, 1)]
+    arrived = [one, two, three]
     far = swap_k(jnp.concatenate([gw] + arrived + [sums]))
     own = jnp.concatenate([gw, sums])
     grad_weight, grad_bias = settle(here, own, arrived, far, feats, width)

time: 97 us -> 96.3 us (level)
  transfers between devices with their start and end apart: 27 -> 27, of which waited for: 20 -> 18; matrix products, arithmetic and copies ran while one was open for 4% -> 4% of each run, Pallas kernels for 2% -> 1%
where the time goes in v4:
time: 96.3 us; the launch traced here: 96.1 us
  starting transfers between devices  49.2 us (51%)
  waiting for transfers between devices  31.2 us (32%)
  matrix products  4.76 us (5%)
  Pallas kernels  4.07 us (4%)
  local copies, waits for them, and re-layouts  3.26 us (3%)
  other arithmetic  1.97 us (2%)
  between operations  1.58 us (2%)
    ppermute x9, starting transfers between devices, swap_h(): lax.ppermute(v, 'row', [(i, mirror(i, 4, 2, mask)) for i in range(8)])  19.8 us
    ppermute x12, waiting for transfers between devices, swap_xy(): return lax.ppermute(v, ('row', 'col'), pairs)  17 us
    ppermute x12, starting transfers between devices, swap_xy(): return lax.ppermute(v, ('row', 'col'), pairs)  13.2 us
    ppermute x3, starting transfers between devices, swap_k(): return lax.ppermute(v, 'row', [(i, i ^ 1) for i in range(8)])  12.1 us
    ppermute x9, waiting for transfers between devices, swap_h(): lax.ppermute(v, 'row', [(i, mirror(i, 4, 2, mask)) for i in range(8)])  11 us
    ppermute x3, starting transfers between devices, swap_z(): return lax.ppermute(v, 'col', [(i, i ^ 1) for i in range(32)])  4.05 us
    unnamed x20, local copies, waits for them, and re-layouts  3.1 us
    dot_general x1, matrix products, local(): lax.dot_general(dense, target, (((0,), (0,)), ((), ())), preferred_elemen...  2.42 us
  transfers between devices with their start and end apart: 27, of which 18 were waited for; matrix products, arithmetic and copies ran while one was open for 4% of the time, Pallas kernels for 1%

profile of v4, /device:TPU:1, one launch (start us, length us, event | category | flops | bytes accessed | tf_op | source)
XLA Modules:
  0.0 96.1 jit_solution(3867578559248815743)
XLA Ops:
  0.6 2.6 %collective-permute-start = (bf16[128,128]{1,0:T(8,128)(2,1)}, bf16[128,128]{1,0:T(8,128)(2,1)S(1)}, u32[]{:S(2)}, u32[]{:S(2)}) collective-permute-start(bf16[128,128]{1,0:T(8,128)(2,1)} %v_ref.1), channel_id=1, source_target_pairs={{0,1},{1,0},{2,3},{3,2},{4,5},{5,4},{6,7},{7,6},{8,9},{9,8},{10,11... | collective-permute-start | bytes 98312 | tf_op jit(solution)/shard_map/ppermute | solution.py:34
  4.7 2.6 %collective-permute-start.3 = (bf16[2,128,128]{2,1,0:T(8,128)(2,1)S(1)}, bf16[2,128,128]{2,1,0:T(8,128)(2,1)S(1)}, u32[]{:S(2)}, u32[]{:S(2)}) collective-permute-start(bf16[2,128,128]{2,1,0:T(8,128)(2,1)S(1)} %get-tuple-element.47), channel_id=1, source_target_pairs={{0,6},{1,7},{2,4},{3,5},{4,2},{5,3},{6,0},{7,1},{8,14},{9,15},{10,... | collective-permute-start | bytes 196616 | tf_op jit(solution)/shard_map/ppermute | solution.py:22
  8.1 1.1 %collective-permute-done.3 = bf16[2,128,128]{2,1,0:T(8,128)(2,1)S(1)} collective-permute-done((bf16[2,128,128]{2,1,0:T(8,128)(2,1)S(1)}, bf16[2,128,128]{2,1,0:T(8,128)(2,1)S(1)}, u32[]{:S(2)}, u32[]{:S(2)}) %collective-permute-start.3) | collective-permute-done | bytes 65568 | tf_op jit(solution)/shard_map/ppermute | solution.py:22
  9.1 2.8 %collective-permute-done.2 = bf16[2,128,128]{2,1,0:T(8,128)(2,1)S(1)} collective-permute-done((bf16[2,128,128]{2,1,0:T(8,128)(2,1)S(1)}, bf16[2,128,128]{2,1,0:T(8,128)(2,1)S(1)}, u32[]{:S(2)}, u32[]{:S(2)}) %collective-permute-start.2) | collective-permute-done | bytes 65568 | tf_op jit(solution)/shard_map/ppermute | solution.py:22
  12.0 3.0 %collective-permute-start.6 = (bf16[4,2,128,128]{3,2,1,0:T(8,128)(2,1)S(1)}, bf16[4,2,128,128]{3,2,1,0:T(8,128)(2,1)S(1)}, u32[]{:S(2)}, u32[]{:S(2)}) collective-permute-start(bf16[4,2,128,128]{3,2,1,0:T(8,128)(2,1)S(1)} %get-tuple-element.36), channel_id=1, source_target_pairs={{0,16},{1,17},{2,18},{3,19},{4,20},{5,21},{6,22},{7,23},{8,24},{9,... | collective-permute-start | bytes 786440 | tf_op jit(solution)/shard_map/ppermute | solution.py:22
  17.1 2.2 %copy-done = bf16[1,1,128,128,128]{4,3,2,1,0:T(8,128)(2,1)S(1)} copy-done((bf16[1,1,128,128,128]{4,3,2,1,0:T(8,128)(2,1)S(1)}, bf16[1,1,128,128,128]{4,3,2,1,0:T(8,128)(2,1)}, u32[]{:S(2)}) %copy-start) | copy-done | bytes 4194328
  19.3 1.3 %spread.1 = bf16[1024,4096]{1,0:T(8,128)(2,1)S(1)} custom-call(s32[1]{0:T(128)} %bitcast.59.count_ref, s32[128]{0:T(128)S(1)} %get-tuple-element.55.put_row, s32[128]{0:T(128)S(1)} %get-tuple-element.54.put_col, bf16[128,128,128]{2,1,0:T(8,128)(2,1)S(1)} %bitcast.60), custom_call_target="tpu_custom_call" | custom-call | bytes 12582912 | tf_op jit(solution)/shard_map/spread/pallas_call | solution.py:63
  20.7 1.2 %collective-permute-done.5 = bf16[4,2,128,128]{3,2,1,0:T(8,128)(2,1)S(1)} collective-permute-done((bf16[4,2,128,128]{3,2,1,0:T(8,128)(2,1)S(1)}, bf16[4,2,128,128]{3,2,1,0:T(8,128)(2,1)S(1)}, u32[]{:S(2)}, u32[]{:S(2)}) %collective-permute-start.5) | collective-permute-done | bytes 262176 | tf_op jit(solution)/shard_map/ppermute | solution.py:22
  22.4 2.3 %fusion.19 = f32[1024,128]{1,0:T(8,128)S(1)} fusion(bf16[1024,4096]{1,0:T(8,128)(2,1)S(1)} %spread.1, bf16[4096,128]{1,0:T(8,128)(2,1)S(1)} %bitcast.64), kind=kOutput, calls=%fused_computation.98 | convolution fusion | flops 1073741824 | bytes 9961472 | tf_op jit(solution)/shard_map/dot_general | solution.py:216
  24.8 4.2 %collective-permute-start.7 = (bf16[4,128,128]{2,1,0:T(8,128)(2,1)S(1)}, bf16[4,128,128]{2,1,0:T(8,128)(2,1)S(1)}, u32[]{:S(2)}, u32[]{:S(2)}) collective-permute-start(bf16[4,128,128]{2,1,0:T(8,128)(2,1)S(1)} %bitcast.68), channel_id=1, source_target_pairs={{0,32},{32,0},{64,96},{96,64},{128,160},{160,128},{192,224},{224,1... | collective-permute-start | bytes 393224 | tf_op jit(solution)/shard_map/ppermute | solution.py:30
  30.0 7.2 %collective-permute-start.8 = (bf16[128,128]{1,0:T(8,128)(2,1)S(1)}, bf16[128,128]{1,0:T(8,128)(2,1)S(1)}, u32[]{:S(2)}, u32[]{:S(2)}) collective-permute-start(bf16[128,128]{1,0:T(8,128)(2,1)S(1)} %get-tuple-element.39), channel_id=1, source_target_pairs={{0,128},{32,160},{64,192},{96,224},{128,0},{160,32},{192,64},{224,... | collective-permute-start | bytes 98312 | tf_op jit(solution)/shard_map/ppermute | solution.py:26
  37.1 1.2 %collective-permute-start.10 = (bf16[128,128]{1,0:T(8,128)(2,1)S(1)}, bf16[128,128]{1,0:T(8,128)(2,1)S(1)}, u32[]{:S(2)}, u32[]{:S(2)}) collective-permute-start(bf16[128,128]{1,0:T(8,128)(2,1)S(1)} %get-tuple-element.37), channel_id=1, source_target_pairs={{0,64},{32,96},{64,0},{96,32},{128,192},{160,224},{192,128},{224,1... | collective-permute-start | bytes 98312 | tf_op jit(solution)/shard_map/ppermute | solution.py:26
  38.5 3.5 %collective-permute-done.9.in2 = bf16[128,128]{1,0:T(8,128)(2,1)S(1)} collective-permute-done((bf16[128,128]{1,0:T(8,128)(2,1)S(1)}, bf16[128,128]{1,0:T(8,128)(2,1)S(1)}, u32[]{:S(2)}, u32[]{:S(2)}) %collective-permute-start.9) | collective-permute-done | bytes 32800 | tf_op jit(solution)/shard_map/ppermute | solution.py:26
  42.0 1.5 %middle.1 = (bf16[128,512]{1,0:T(8,128)(2,1)}, bf16[4,272,128]{2,1,0:T(8,128)(2,1)S(1)}, f32[144,128]{1,0:T(8,128)S(1)}) custom-call(s32[2]{0:T(128)S(1)} %pad_add_fusion.place, f32[128,128]{1,0:T(8,128)S(1)} %slice_bitcast_fusion.3.own, bf16[128,128]{1,0:T(8,128)(2,1)S(1)} %collective-permute-done.8.in1, bf16[128,128]{1,0:T(8,128)(2,1)S(1)} %collective-permute-done.9.in2, ...), custom_call_target="tpu_custom_call" | custom-call | flops 83886080 | bytes 655360 | tf_op jit(solution)/shard_map/middle/pallas_call | solution.py:125
  43.5 2.7 %collective-permute-start.13 = (bf16[272,128]{1,0:T(8,128)(2,1)S(1)}, bf16[272,128]{1,0:T(8,128)(2,1)S(1)}, u32[]{:S(2)}, u32[]{:S(2)}) collective-permute-start(bf16[272,128]{1,0:T(8,128)(2,1)S(1)} %get-tuple-element.30), channel_id=1, source_target_pairs={{0,192},{32,224},{64,128},{96,160},{128,64},{160,96},{192,0},{224,... | collective-permute-start | bytes 208904 | tf_op jit(solution)/shard_map/ppermute | solution.py:26
  46.2 2.0 %collective-permute-start.12 = (bf16[272,128]{1,0:T(8,128)(2,1)S(1)}, bf16[272,128]{1,0:T(8,128)(2,1)S(1)}, u32[]{:S(2)}, u32[]{:S(2)}) collective-permute-start(bf16[272,128]{1,0:T(8,128)(2,1)S(1)} %get-tuple-element.31), channel_id=1, source_target_pairs={{0,128},{32,160},{64,192},{96,224},{128,0},{160,32},{192,64},{224,... | collective-permute-start | bytes 208904 | tf_op jit(solution)/shard_map/ppermute | solution.py:26
  49.3 4.8 %collective-permute-done.12 = bf16[272,128]{1,0:T(8,128)(2,1)S(1)} collective-permute-done((bf16[272,128]{1,0:T(8,128)(2,1)S(1)}, bf16[272,128]{1,0:T(8,128)(2,1)S(1)}, u32[]{:S(2)}, u32[]{:S(2)}) %collective-permute-start.12) | collective-permute-done | bytes 69664 | tf_op jit(solution)/shard_map/ppermute | solution.py:26
  54.2 3.9 %collective-permute-start.14 = (bf16[672,128]{1,0:T(8,128)(2,1)S(1)}, bf16[672,128]{1,0:T(8,128)(2,1)S(1)}, u32[]{:S(2)}, u32[]{:S(2)}) collective-permute-start(bf16[672,128]{1,0:T(8,128)(2,1)S(1)} %constant_dynamic-update-slice_fusion), channel_id=1, source_target_pairs={{0,32},{32,0},{64,96},{96,64},{128,160},{160,128},{192,224},{224,1... | collective-permute-start | bytes 516104 | tf_op jit(solution)/shard_map/ppermute | solution.py:30
  59.4 2.4 %fusion.18 = (bf16[4096,128]{1,0:T(8,128)(2,1)S(1)}, f32[4096,128]{1,0:T(8,128)S(1)}) fusion(bf16[1024,4096]{1,0:T(8,128)(2,1)S(1)} %spread.1, bf16[1024,128]{1,0:T(8,128)(2,1)S(1)} %slice_dynamic-update-slice_fusion), kind=kOutput, calls=%fused_computation.97 | convolution fusion | flops 1074266112 | bytes 11796480 | tf_op jit(solution)/shard_map/dot_general | solution.py:233
  62.3 1.6 %collective-permute-start.18 = (bf16[1104,128]{1,0:T(8,128)(2,1)S(1)}, bf16[1104,128]{1,0:T(8,128)(2,1)S(1)}, u32[]{:S(2)}, u32[]{:S(2)}) collective-permute-start(bf16[1104,128]{1,0:T(8,128)(2,1)S(1)} %get-tuple-element.53), channel_id=1, source_target_pairs={{0,16},{1,17},{2,18},{3,19},{4,20},{5,21},{6,22},{7,23},{8,24},{9,... | collective-permute-start | bytes 847880 | tf_op jit(solution)/shard_map/ppermute | solution.py:22
  65.1 4.6 %collective-permute-done.18 = bf16[1104,128]{1,0:T(8,128)(2,1)S(1)} collective-permute-done((bf16[1104,128]{1,0:T(8,128)(2,1)S(1)}, bf16[1104,128]{1,0:T(8,128)(2,1)S(1)}, u32[]{:S(2)}, u32[]{:S(2)}) %collective-permute-start.18) | collective-permute-done | bytes 282656 | tf_op jit(solution)/shard_map/ppermute | solution.py:22
  69.7 3.0 %collective-permute-done.17 = bf16[1104,128]{1,0:T(8,128)(2,1)S(1)} collective-permute-done((bf16[1104,128]{1,0:T(8,128)(2,1)S(1)}, bf16[1104,128]{1,0:T(8,128)(2,1)S(1)}, u32[]{:S(2)}, u32[]{:S(2)}) %collective-permute-start.17) | collective-permute-done | bytes 282656 | tf_op jit(solution)/shard_map/ppermute | solution.py:22
  72.9 2.4 %collective-permute-start.21 = (bf16[336,128]{1,0:T(8,128)(2,1)S(1)}, bf16[336,128]{1,0:T(8,128)(2,1)S(1)}, u32[]{:S(2)}, u32[]{:S(2)}) collective-permute-start(bf16[336,128]{1,0:T(8,128)(2,1)S(1)} %get-tuple-element.50), channel_id=1, source_target_pairs={{0,6},{1,7},{2,4},{3,5},{4,2},{5,3},{6,0},{7,1},{8,14},{9,15},{10,... | collective-permute-start | bytes 258056 | tf_op jit(solution)/shard_map/ppermute | solution.py:22
  76.2 1.3 %collective-permute-done.21 = bf16[336,128]{1,0:T(8,128)(2,1)S(1)} collective-permute-done((bf16[336,128]{1,0:T(8,128)(2,1)S(1)}, bf16[336,128]{1,0:T(8,128)(2,1)S(1)}, u32[]{:S(2)}, u32[]{:S(2)}) %collective-permute-start.21) | collective-permute-done | bytes 86048 | tf_op jit(solution)/shard_map/ppermute | solution.py:22
  77.5 2.6 %collective-permute-done.20 = bf16[336,128]{1,0:T(8,128)(2,1)S(1)} collective-permute-done((bf16[336,128]{1,0:T(8,128)(2,1)S(1)}, bf16[336,128]{1,0:T(8,128)(2,1)S(1)}, u32[]{:S(2)}, u32[]{:S(2)}) %collective-permute-start.20) | collective-permute-done | bytes 86048 | tf_op jit(solution)/shard_map/ppermute | solution.py:22
  80.2 1.8 %collective-permute-start.23 = (bf16[64,128]{1,0:T(8,128)(2,1)S(1)}, bf16[64,128]{1,0:T(8,128)(2,1)S(1)}, u32[]{:S(2)}, u32[]{:S(2)}) collective-permute-start(bf16[64,128]{1,0:T(8,128)(2,1)S(1)} %get-tuple-element.19), channel_id=1, source_target_pairs={{0,64},{32,96},{64,0},{96,32},{128,192},{160,224},{192,128},{224,1... | collective-permute-start | bytes 49160 | tf_op jit(solution)/shard_map/ppermute | solution.py:26
  82.0 3.1 %collective-permute-start.24 = (bf16[64,128]{1,0:T(8,128)(2,1)S(1)}, bf16[64,128]{1,0:T(8,128)(2,1)S(1)}, u32[]{:S(2)}, u32[]{:S(2)}) collective-permute-start(bf16[64,128]{1,0:T(8,128)(2,1)S(1)} %get-tuple-element.19), channel_id=1, source_target_pairs={{0,128},{32,160},{64,192},{96,224},{128,0},{160,32},{192,64},{224,... | collective-permute-start | bytes 49160 | tf_op jit(solution)/shard_map/ppermute | solution.py:26
  86.0 1.2 %collective-permute-start.22 = (bf16[128,128]{1,0:T(8,128)(2,1)S(1)}, bf16[128,128]{1,0:T(8,128)(2,1)S(1)}, u32[]{:S(2)}, u32[]{:S(2)}) collective-permute-start(bf16[128,128]{1,0:T(8,128)(2,1)S(1)} %slice.295), channel_id=1, source_target_pairs={{0,1},{1,0},{2,3},{3,2},{4,5},{5,4},{6,7},{7,6},{8,9},{9,8},{10,11... | collective-permute-start | bytes 98312 | tf_op jit(solution)/shard_map/ppermute | solution.py:34
  87.2 1.2 %collective-permute-done.24.two = bf16[64,128]{1,0:T(8,128)(2,1)S(1)} collective-permute-done((bf16[64,128]{1,0:T(8,128)(2,1)S(1)}, bf16[64,128]{1,0:T(8,128)(2,1)S(1)}, u32[]{:S(2)}, u32[]{:S(2)}) %collective-permute-start.24) | collective-permute-done | bytes 16416 | tf_op jit(solution)/shard_map/ppermute | solution.py:26
  88.5 1.3 %collective-permute-done.25.three = bf16[64,128]{1,0:T(8,128)(2,1)S(1)} collective-permute-done((bf16[64,128]{1,0:T(8,128)(2,1)S(1)}, bf16[64,128]{1,0:T(8,128)(2,1)S(1)}, u32[]{:S(2)}, u32[]{:S(2)}) %collective-permute-start.25) | collective-permute-done | bytes 16416 | tf_op jit(solution)/shard_map/ppermute | solution.py:26
  89.8 4.1 %collective-permute-start.26 = (bf16[272,128]{1,0:T(8,128)(2,1)S(1)}, bf16[272,128]{1,0:T(8,128)(2,1)S(1)}, u32[]{:S(2)}, u32[]{:S(2)}) collective-permute-start(bf16[272,128]{1,0:T(8,128)(2,1)S(1)} %get-tuple-element.14), channel_id=1, source_target_pairs={{0,32},{32,0},{64,96},{96,64},{128,160},{160,128},{192,224},{224,1... | collective-permute-start | bytes 208904 | tf_op jit(solution)/shard_map/ppermute | solution.py:30
  94.8 1.3 %settle.1 = (f32[128,512]{1,0:T(8,128)}, f32[1,512]{1,0:T(1,128)}) custom-call(s32[2]{0:T(128)S(1)} %pad_add_fusion.place, bf16[80,128]{1,0:T(8,128)(2,1)S(1)} %pad_maximum_fusion.9.own, bf16[64,128]{1,0:T(8,128)(2,1)S(1)} %collective-permute-done.23.one, bf16[64,128]{1,0:T(8,128)(2,1)S(1)} %collective-permute-done.24.two, ...), custom_call_target="tpu_custom_call" | custom-call | tf_op jit(solution)/shard_map/settle/pallas_call | solution.py:163
  (78 shorter events, 12.7 us)
Async XLA Ops:
  0.6 4.1 %collective-permute-start = (bf16[128,128]{1,0:T(8,128)(2,1)}, bf16[128,128]{1,0:T(8,128)(2,1)S(1)}, u32[]{:S(2)}, u32[]{:S(2)}) collective-permute-start(bf16[128,128]{1,0:T(8,128)(2,1)} %v_ref.1), channel_id=1, source_target_pairs={{0,1},{1,0},{2,3},{3,2},{4,5},{5,4},{6,7},{7,6},{8,9},{9,8},{10,11... | collective-permute-start | bytes 98312 | tf_op jit(solution)/shard_map/ppermute | solution.py:34
  3.2 0.8 copy-start.3
  4.7 4.4 %collective-permute-start.3 = (bf16[2,128,128]{2,1,0:T(8,128)(2,1)S(1)}, bf16[2,128,128]{2,1,0:T(8,128)(2,1)S(1)}, u32[]{:S(2)}, u32[]{:S(2)}) collective-permute-start(bf16[2,128,128]{2,1,0:T(8,128)(2,1)S(1)} %get-tuple-element.47), channel_id=1, source_target_pairs={{0,6},{1,7},{2,4},{3,5},{4,2},{5,3},{6,0},{7,1},{8,14},{9,15},{10,... | collective-permute-start | bytes 196616 | tf_op jit(solution)/shard_map/ppermute | solution.py:22
  7.3 4.6 %collective-permute-start.2 = (bf16[2,128,128]{2,1,0:T(8,128)(2,1)S(1)}, bf16[2,128,128]{2,1,0:T(8,128)(2,1)S(1)}, u32[]{:S(2)}, u32[]{:S(2)}) collective-permute-start(bf16[2,128,128]{2,1,0:T(8,128)(2,1)S(1)} %get-tuple-element.47), channel_id=1, source_target_pairs={{0,4},{1,5},{2,6},{3,7},{4,0},{5,1},{6,2},{7,3},{8,12},{9,13},{10,... | collective-permute-start | bytes 196616 | tf_op jit(solution)/shard_map/ppermute | solution.py:22
  7.8 4.1 %collective-permute-start.1 = (bf16[2,128,128]{2,1,0:T(8,128)(2,1)S(1)}, bf16[2,128,128]{2,1,0:T(8,128)(2,1)S(1)}, u32[]{:S(2)}, u32[]{:S(2)}) collective-permute-start(bf16[2,128,128]{2,1,0:T(8,128)(2,1)S(1)} %get-tuple-element.47), channel_id=1, source_target_pairs={{0,2},{1,3},{2,0},{3,1},{4,6},{5,7},{6,4},{7,5},{8,10},{9,11},{10,... | collective-permute-start | bytes 196616 | tf_op jit(solution)/shard_map/ppermute | solution.py:22
  12.0 8.7 %collective-permute-start.6 = (bf16[4,2,128,128]{3,2,1,0:T(8,128)(2,1)S(1)}, bf16[4,2,128,128]{3,2,1,0:T(8,128)(2,1)S(1)}, u32[]{:S(2)}, u32[]{:S(2)}) collective-permute-start(bf16[4,2,128,128]{3,2,1,0:T(8,128)(2,1)S(1)} %get-tuple-element.36), channel_id=1, source_target_pairs={{0,16},{1,17},{2,18},{3,19},{4,20},{5,21},{6,22},{7,23},{8,24},{9,... | collective-permute-start | bytes 786440 | tf_op jit(solution)/shard_map/ppermute | solution.py:22
  15.0 6.9 %collective-permute-start.5 = (bf16[4,2,128,128]{3,2,1,0:T(8,128)(2,1)S(1)}, bf16[4,2,128,128]{3,2,1,0:T(8,128)(2,1)S(1)}, u32[]{:S(2)}, u32[]{:S(2)}) collective-permute-start(bf16[4,2,128,128]{3,2,1,0:T(8,128)(2,1)S(1)} %get-tuple-element.36), channel_id=1, source_target_pairs={{0,24},{1,25},{2,26},{3,27},{4,28},{5,29},{6,30},{7,31},{8,16},{9,... | collective-permute-start | bytes 786440 | tf_op jit(solution)/shard_map/ppermute | solution.py:22
  15.7 6.5 %collective-permute-start.4 = (bf16[4,2,128,128]{3,2,1,0:T(8,128)(2,1)S(1)}, bf16[4,2,128,128]{3,2,1,0:T(8,128)(2,1)S(1)}, u32[]{:S(2)}, u32[]{:S(2)}) collective-permute-start(bf16[4,2,128,128]{3,2,1,0:T(8,128)(2,1)S(1)} %get-tuple-element.36), channel_id=1, source_target_pairs={{0,8},{1,9},{2,10},{3,11},{4,12},{5,13},{6,14},{7,15},{8,0},{9,1},... | collective-permute-start | bytes 786440 | tf_op jit(solution)/shard_map/ppermute | solution.py:22
  17.1 2.2 %copy-start = (bf16[1,1,128,128,128]{4,3,2,1,0:T(8,128)(2,1)S(1)}, bf16[1,1,128,128,128]{4,3,2,1,0:T(8,128)(2,1)}, u32[]{:S(2)}) copy-start(bf16[1,1,128,128,128]{4,3,2,1,0:T(8,128)(2,1)} %param.10) | copy-start | bytes 12582916
  20.6 21.4 %copy-start.1 = (bf16[128,512]{1,0:T(8,128)(2,1)S(1)}, bf16[128,512]{1,0:T(8,128)(2,1)}, u32[]{:S(2)}) copy-start(bf16[128,512]{1,0:T(8,128)(2,1)} %weight.1) | copy-start | bytes 393220
  20.6 21.4 %copy-start.2 = (bf16[128,512]{1,0:T(8,128)(2,1)S(1)}, bf16[128,512]{1,0:T(8,128)(2,1)}, u32[]{:S(2)}) copy-start(bf16[128,512]{1,0:T(8,128)(2,1)} %cot.1) | copy-start | bytes 393220
  20.6 21.4 %copy-start.4 = (f32[512]{0:T(512)S(1)}, f32[512]{0:T(512)}, u32[]{:S(2)}) copy-start(f32[512]{0:T(512)} %param.9) | copy-start | bytes 6148
  24.8 5.1 %collective-permute-start.7 = (bf16[4,128,128]{2,1,0:T(8,128)(2,1)S(1)}, bf16[4,128,128]{2,1,0:T(8,128)(2,1)S(1)}, u32[]{:S(2)}, u32[]{:S(2)}) collective-permute-start(bf16[4,128,128]{2,1,0:T(8,128)(2,1)S(1)} %bitcast.68), channel_id=1, source_target_pairs={{0,32},{32,0},{64,96},{96,64},{128,160},{160,128},{192,224},{224,1... | collective-permute-start | bytes 393224 | tf_op jit(solution)/shard_map/ppermute | solution.py:30
  30.0 8.5 %collective-permute-start.8 = (bf16[128,128]{1,0:T(8,128)(2,1)S(1)}, bf16[128,128]{1,0:T(8,128)(2,1)S(1)}, u32[]{:S(2)}, u32[]{:S(2)}) collective-permute-start(bf16[128,128]{1,0:T(8,128)(2,1)S(1)} %get-tuple-element.39), channel_id=1, source_target_pairs={{0,128},{32,160},{64,192},{96,224},{128,0},{160,32},{192,64},{224,... | collective-permute-start | bytes 98312 | tf_op jit(solution)/shard_map/ppermute | solution.py:26
  37.1 4.9 %collective-permute-start.9 = (bf16[128,128]{1,0:T(8,128)(2,1)S(1)}, bf16[128,128]{1,0:T(8,128)(2,1)S(1)}, u32[]{:S(2)}, u32[]{:S(2)}) collective-permute-start(bf16[128,128]{1,0:T(8,128)(2,1)S(1)} %get-tuple-element.38), channel_id=1, source_target_pairs={{0,192},{32,224},{64,128},{96,160},{128,64},{160,96},{192,0},{224,... | collective-permute-start | bytes 98312 | tf_op jit(solution)/shard_map/ppermute | solution.py:26
  37.1 4.9 %collective-permute-start.10 = (bf16[128,128]{1,0:T(8,128)(2,1)S(1)}, bf16[128,128]{1,0:T(8,128)(2,1)S(1)}, u32[]{:S(2)}, u32[]{:S(2)}) collective-permute-start(bf16[128,128]{1,0:T(8,128)(2,1)S(1)} %get-tuple-element.37), channel_id=1, source_target_pairs={{0,64},{32,96},{64,0},{96,32},{128,192},{160,224},{192,128},{224,1... | collective-permute-start | bytes 98312 | tf_op jit(solution)/shard_map/ppermute | solution.py:26
  43.5 5.8 %collective-permute-start.13 = (bf16[272,128]{1,0:T(8,128)(2,1)S(1)}, bf16[272,128]{1,0:T(8,128)(2,1)S(1)}, u32[]{:S(2)}, u32[]{:S(2)}) collective-permute-start(bf16[272,128]{1,0:T(8,128)(2,1)S(1)} %get-tuple-element.30), channel_id=1, source_target_pairs={{0,192},{32,224},{64,128},{96,160},{128,64},{160,96},{192,0},{224,... | collective-permute-start | bytes 208904 | tf_op jit(solution)/shard_map/ppermute | solution.py:26
  46.2 7.9 %collective-permute-start.12 = (bf16[272,128]{1,0:T(8,128)(2,1)S(1)}, bf16[272,128]{1,0:T(8,128)(2,1)S(1)}, u32[]{:S(2)}, u32[]{:S(2)}) collective-permute-start(bf16[272,128]{1,0:T(8,128)(2,1)S(1)} %get-tuple-element.31), channel_id=1, source_target_pairs={{0,128},{32,160},{64,192},{96,224},{128,0},{160,32},{192,64},{224,... | collective-permute-start | bytes 208904 | tf_op jit(solution)/shard_map/ppermute | solution.py:26
  48.2 5.9 %collective-permute-start.11 = (bf16[272,128]{1,0:T(8,128)(2,1)S(1)}, bf16[272,128]{1,0:T(8,128)(2,1)S(1)}, u32[]{:S(2)}, u32[]{:S(2)}) collective-permute-start(bf16[272,128]{1,0:T(8,128)(2,1)S(1)} %get-tuple-element.29), channel_id=1, source_target_pairs={{0,64},{32,96},{64,0},{96,32},{128,192},{160,224},{192,128},{224,1... | collective-permute-start | bytes 208904 | tf_op jit(solution)/shard_map/ppermute | solution.py:26
  54.2 4.9 %collective-permute-start.14 = (bf16[672,128]{1,0:T(8,128)(2,1)S(1)}, bf16[672,128]{1,0:T(8,128)(2,1)S(1)}, u32[]{:S(2)}, u32[]{:S(2)}) collective-permute-start(bf16[672,128]{1,0:T(8,128)(2,1)S(1)} %constant_dynamic-update-slice_fusion), channel_id=1, source_target_pairs={{0,32},{32,0},{64,96},{96,64},{128,160},{160,128},{192,224},{224,1... | collective-permute-start | bytes 516104 | tf_op jit(solution)/shard_map/ppermute | solution.py:30
  59.1 3.1 %collective-permute-start.15 = (f32[80,128]{1,0:T(8,128)S(1)}, f32[80,128]{1,0:T(8,128)S(1)}, u32[]{:S(2)}, u32[]{:S(2)}) collective-permute-start(f32[80,128]{1,0:T(8,128)S(1)} %maximum_add_fusion), channel_id=1, source_target_pairs={{0,1},{1,0},{2,3},{3,2},{4,5},{5,4},{6,7},{7,6},{8,9},{9,8},{10,11... | collective-permute-start | bytes 122888 | tf_op jit(solution)/shard_map/ppermute | solution.py:34
  62.3 7.4 %collective-permute-start.18 = (bf16[1104,128]{1,0:T(8,128)(2,1)S(1)}, bf16[1104,128]{1,0:T(8,128)(2,1)S(1)}, u32[]{:S(2)}, u32[]{:S(2)}) collective-permute-start(bf16[1104,128]{1,0:T(8,128)(2,1)S(1)} %get-tuple-element.53), channel_id=1, source_target_pairs={{0,16},{1,17},{2,18},{3,19},{4,20},{5,21},{6,22},{7,23},{8,24},{9,... | collective-permute-start | bytes 847880 | tf_op jit(solution)/shard_map/ppermute | solution.py:22
  63.9 8.8 %collective-permute-start.17 = (bf16[1104,128]{1,0:T(8,128)(2,1)S(1)}, bf16[1104,128]{1,0:T(8,128)(2,1)S(1)}, u32[]{:S(2)}, u32[]{:S(2)}) collective-permute-start(bf16[1104,128]{1,0:T(8,128)(2,1)S(1)} %get-tuple-element.52), channel_id=1, source_target_pairs={{0,24},{1,25},{2,26},{3,27},{4,28},{5,29},{6,30},{7,31},{8,16},{9,... | collective-permute-start | bytes 847880 | tf_op jit(solution)/shard_map/ppermute | solution.py:22
  64.3 8.3 %collective-permute-start.16 = (bf16[1104,128]{1,0:T(8,128)(2,1)S(1)}, bf16[1104,128]{1,0:T(8,128)(2,1)S(1)}, u32[]{:S(2)}, u32[]{:S(2)}) collective-permute-start(bf16[1104,128]{1,0:T(8,128)(2,1)S(1)} %get-tuple-element.51), channel_id=1, source_target_pairs={{0,8},{1,9},{2,10},{3,11},{4,12},{5,13},{6,14},{7,15},{8,0},{9,1},... | collective-permute-start | bytes 847880 | tf_op jit(solution)/shard_map/ppermute | solution.py:22
  72.9 4.6 %collective-permute-start.21 = (bf16[336,128]{1,0:T(8,128)(2,1)S(1)}, bf16[336,128]{1,0:T(8,128)(2,1)S(1)}, u32[]{:S(2)}, u32[]{:S(2)}) collective-permute-start(bf16[336,128]{1,0:T(8,128)(2,1)S(1)} %get-tuple-element.50), channel_id=1, source_target_pairs={{0,6},{1,7},{2,4},{3,5},{4,2},{5,3},{6,0},{7,1},{8,14},{9,15},{10,... | collective-permute-start | bytes 258056 | tf_op jit(solution)/shard_map/ppermute | solution.py:22
  75.3 4.8 %collective-permute-start.20 = (bf16[336,128]{1,0:T(8,128)(2,1)S(1)}, bf16[336,128]{1,0:T(8,128)(2,1)S(1)}, u32[]{:S(2)}, u32[]{:S(2)}) collective-permute-start(bf16[336,128]{1,0:T(8,128)(2,1)S(1)} %get-tuple-element.49), channel_id=1, source_target_pairs={{0,4},{1,5},{2,6},{3,7},{4,0},{5,1},{6,2},{7,3},{8,12},{9,13},{10,... | collective-permute-start | bytes 258056 | tf_op jit(solution)/shard_map/ppermute | solution.py:22
  75.4 4.8 %collective-permute-start.19 = (bf16[336,128]{1,0:T(8,128)(2,1)S(1)}, bf16[336,128]{1,0:T(8,128)(2,1)S(1)}, u32[]{:S(2)}, u32[]{:S(2)}) collective-permute-start(bf16[336,128]{1,0:T(8,128)(2,1)S(1)} %get-tuple-element.48), channel_id=1, source_target_pairs={{0,2},{1,3},{2,0},{3,1},{4,6},{5,7},{6,4},{7,5},{8,10},{9,11},{10,... | collective-permute-start | bytes 258056 | tf_op jit(solution)/shard_map/ppermute | solution.py:22
  80.2 7.0 %collective-permute-start.23 = (bf16[64,128]{1,0:T(8,128)(2,1)S(1)}, bf16[64,128]{1,0:T(8,128)(2,1)S(1)}, u32[]{:S(2)}, u32[]{:S(2)}) collective-permute-start(bf16[64,128]{1,0:T(8,128)(2,1)S(1)} %get-tuple-element.19), channel_id=1, source_target_pairs={{0,64},{32,96},{64,0},{96,32},{128,192},{160,224},{192,128},{224,1... | collective-permute-start | bytes 49160 | tf_op jit(solution)/shard_map/ppermute | solution.py:26
  82.0 6.5 %collective-permute-start.24 = (bf16[64,128]{1,0:T(8,128)(2,1)S(1)}, bf16[64,128]{1,0:T(8,128)(2,1)S(1)}, u32[]{:S(2)}, u32[]{:S(2)}) collective-permute-start(bf16[64,128]{1,0:T(8,128)(2,1)S(1)} %get-tuple-element.19), channel_id=1, source_target_pairs={{0,128},{32,160},{64,192},{96,224},{128,0},{160,32},{192,64},{224,... | collective-permute-start | bytes 49160 | tf_op jit(solution)/shard_map/ppermute | solution.py:26
  85.1 4.7 %collective-permute-start.25 = (bf16[64,128]{1,0:T(8,128)(2,1)S(1)}, bf16[64,128]{1,0:T(8,128)(2,1)S(1)}, u32[]{:S(2)}, u32[]{:S(2)}) collective-permute-start(bf16[64,128]{1,0:T(8,128)(2,1)S(1)} %get-tuple-element.19), channel_id=1, source_target_pairs={{0,192},{32,224},{64,128},{96,160},{128,64},{160,96},{192,0},{224,... | collective-permute-start | bytes 49160 | tf_op jit(solution)/shard_map/ppermute | solution.py:26
  86.0 7.9 %collective-permute-start.22 = (bf16[128,128]{1,0:T(8,128)(2,1)S(1)}, bf16[128,128]{1,0:T(8,128)(2,1)S(1)}, u32[]{:S(2)}, u32[]{:S(2)}) collective-permute-start(bf16[128,128]{1,0:T(8,128)(2,1)S(1)} %slice.295), channel_id=1, source_target_pairs={{0,1},{1,0},{2,3},{3,2},{4,5},{5,4},{6,7},{7,6},{8,9},{9,8},{10,11... | collective-permute-start | bytes 98312 | tf_op jit(solution)/shard_map/ppermute | solution.py:34
  89.8 5.0 %collective-permute-start.26 = (bf16[272,128]{1,0:T(8,128)(2,1)S(1)}, bf16[272,128]{1,0:T(8,128)(2,1)S(1)}, u32[]{:S(2)}, u32[]{:S(2)}) collective-permute-start(bf16[272,128]{1,0:T(8,128)(2,1)S(1)} %get-tuple-element.14), channel_id=1, source_target_pairs={{0,32},{32,0},{64,96},{96,64},{128,160},{160,128},{192,224},{224,1... | collective-permute-start | bytes 208904 | tf_op jit(solution)/shard_map/ppermute | solution.py:30

commit v5 on v4

--- a/solution.py
+++ b/solution.py
@@ -204,13 +204,13 @@
     far_x, far_y, far_z = x ^ (tile_col // 8), y ^ ((tile_col // 2) % 4), z ^ (tile_col % 2)
     put_row = (far_k * 4 + far_h).astype(jnp.int32)
     first, second = jnp.where(k == 0, far_y, far_x), jnp.where(k == 0, far_x, far_y)
-    second = second ^ (second >> 1)
+    first, second = first ^ (first >> 1), second ^ (second >> 1)
     put_col = (second * 8 + first * 2 + far_z).astype(jnp.int32)
     dense = spread(tile_values[0, 0], tile_count[0], put_row, put_col, 8, 32)
 
     source = jnp.stack([near_copy(features), swap_z(features)])
     for turn in (0, 1):
-        source = jnp.stack([source] + [swap_xy(source, bits, turn) for bits in ((1, 3, 2) if turn else (1, 2, 3))])
+        source = jnp.stack([source] + [swap_xy(source, bits, turn) for bits in (1, 3, 2)])
     source = source.reshape(-1, feats)
 
     part = jnp.dot(dense, source, preferred_element_type=F32).reshape(2, 4, size, feats)
@@ -235,7 +235,7 @@
         grad = grad.reshape(4, -1, feats)
         rows = grad.shape[1]
         low, extra = grad.astype(BF), gw.astype(BF)
-        order = (1, 3, 2) if turn else (1, 2, 3)
+        order = (1, 3, 2)
         arrived = [swap_xy(jnp.concatenate([low[i + 1], extra]), order[i], turn) for i in range(3)]
         grad = grad[0] + sum(v[:rows].astype(F32) for v in arrived)
         one, two, three = [arrived[order.index(bits)][rows:].astype(F32) for bits in (1, 2, 3)]

time: 96.3 us -> 95.3 us (0.990)
  waiting for transfers between devices: 31.2 us -> 29.6 us
    ppermute x12, waiting for transfers between devices: 17 us -> 15.4 us  [swap_xy(): return lax.ppermute(v, ('row', 'col'), pairs)]
    ppermute x12, starting transfers between devices: 13.2 us -> 14.2 us  [swap_xy(): return lax.ppermute(v, ('row', 'col'), pairs)]
    ppermute x3, starting transfers between devices: 12.1 us -> 11.1 us  [swap_k(): return lax.ppermute(v, 'row', [(i, i ^ 1) for i in range(8)])]
  transfers between devices with their start and end apart: 27 -> 27, of which waited for: 18 -> 19; matrix products, arithmetic and copies ran while one was open for 4% -> 4% of each run, Pallas kernels for 1% -> 2%
where the time goes in v5:
time: 95.3 us; the launch traced here: 95.1 us
  starting transfers between devices  48.9 us (51%)
  waiting for transfers between devices  29.6 us (31%)
  Pallas kernels  5 us (5%)
  matrix products  4.76 us (5%)
  local copies, waits for them, and re-layouts  3.26 us (3%)
  other arithmetic  1.97 us (2%)
  between operations  1.58 us (2%)
    ppermute x9, starting transfers between devices, swap_h(): lax.ppermute(v, 'row', [(i, mirror(i, 4, 2, mask)) for i in range(8)])  19.7 us
    ppermute x12, waiting for transfers between devices, swap_xy(): return lax.ppermute(v, ('row', 'col'), pairs)  15.4 us
    ppermute x12, starting transfers between devices, swap_xy(): return lax.ppermute(v, ('row', 'col'), pairs)  14.2 us
    ppermute x3, starting transfers between devices, swap_k(): return lax.ppermute(v, 'row', [(i, i ^ 1) for i in range(8)])  11.1 us
    ppermute x9, waiting for transfers between devices, swap_h(): lax.ppermute(v, 'row', [(i, mirror(i, 4, 2, mask)) for i in range(8)])  11 us
    ppermute x3, starting transfers between devices, swap_z(): return lax.ppermute(v, 'col', [(i, i ^ 1) for i in range(32)])  3.91 us
    unnamed x20, local copies, waits for them, and re-layouts  3.1 us
    dot_general x1, matrix products, local(): lax.dot_general(dense, target, (((0,), (0,)), ((), ())), preferred_elemen...  2.42 us
  transfers between devices with their start and end apart: 27, of which 19 were waited for; matrix products, arithmetic and copies ran while one was open for 4% of the time, Pallas kernels for 2%

profile of v5, /device:TPU:1, one launch (start us, length us, event | category | flops | bytes accessed | tf_op | source)
XLA Modules:
  0.0 95.1 jit_solution(5924703138003963786)
XLA Ops:
  0.6 2.6 %collective-permute-start = (bf16[128,128]{1,0:T(8,128)(2,1)}, bf16[128,128]{1,0:T(8,128)(2,1)S(1)}, u32[]{:S(2)}, u32[]{:S(2)}) collective-permute-start(bf16[128,128]{1,0:T(8,128)(2,1)} %v_ref.1), channel_id=1, source_target_pairs={{0,1},{1,0},{2,3},{3,2},{4,5},{5,4},{6,7},{7,6},{8,9},{9,8},{10,11... | collective-permute-start | bytes 98312 | tf_op jit(solution)/shard_map/ppermute | solution.py:34
  4.7 2.8 %collective-permute-start.3 = (bf16[2,128,128]{2,1,0:T(8,128)(2,1)S(1)}, bf16[2,128,128]{2,1,0:T(8,128)(2,1)S(1)}, u32[]{:S(2)}, u32[]{:S(2)}) collective-permute-start(bf16[2,128,128]{2,1,0:T(8,128)(2,1)S(1)} %get-tuple-element.47), channel_id=1, source_target_pairs={{0,4},{1,5},{2,6},{3,7},{4,0},{5,1},{6,2},{7,3},{8,12},{9,13},{10,... | collective-permute-start | bytes 196616 | tf_op jit(solution)/shard_map/ppermute | solution.py:22
  9.4 2.5 %collective-permute-done.2 = bf16[2,128,128]{2,1,0:T(8,128)(2,1)S(1)} collective-permute-done((bf16[2,128,128]{2,1,0:T(8,128)(2,1)S(1)}, bf16[2,128,128]{2,1,0:T(8,128)(2,1)S(1)}, u32[]{:S(2)}, u32[]{:S(2)}) %collective-permute-start.2) | collective-permute-done | bytes 65568 | tf_op jit(solution)/shard_map/ppermute | solution.py:22
  11.9 3.0 %collective-permute-start.6 = (bf16[4,2,128,128]{3,2,1,0:T(8,128)(2,1)S(1)}, bf16[4,2,128,128]{3,2,1,0:T(8,128)(2,1)S(1)}, u32[]{:S(2)}, u32[]{:S(2)}) collective-permute-start(bf16[4,2,128,128]{3,2,1,0:T(8,128)(2,1)S(1)} %get-tuple-element.36), channel_id=1, source_target_pairs={{0,16},{1,17},{2,18},{3,19},{4,20},{5,21},{6,22},{7,23},{8,24},{9,... | collective-permute-start | bytes 786440 | tf_op jit(solution)/shard_map/ppermute | solution.py:22
  17.1 2.2 %copy-done = bf16[1,1,128,128,128]{4,3,2,1,0:T(8,128)(2,1)S(1)} copy-done((bf16[1,1,128,128,128]{4,3,2,1,0:T(8,128)(2,1)S(1)}, bf16[1,1,128,128,128]{4,3,2,1,0:T(8,128)(2,1)}, u32[]{:S(2)}) %copy-start) | copy-done | bytes 4194328
  19.3 2.2 %spread.1 = bf16[1024,4096]{1,0:T(8,128)(2,1)S(1)} custom-call(s32[1]{0:T(128)} %bitcast.59.count_ref, s32[128]{0:T(128)S(1)} %get-tuple-element.55.put_row, s32[128]{0:T(128)S(1)} %get-tuple-element.54.put_col, bf16[128,128,128]{2,1,0:T(8,128)(2,1)S(1)} %bitcast.60), custom_call_target="tpu_custom_call" | custom-call | bytes 12582912 | tf_op jit(solution)/shard_map/spread/pallas_call | solution.py:63
  22.7 2.3 %fusion.19 = f32[1024,128]{1,0:T(8,128)S(1)} fusion(bf16[1024,4096]{1,0:T(8,128)(2,1)S(1)} %spread.1, bf16[4096,128]{1,0:T(8,128)(2,1)S(1)} %bitcast.64), kind=kOutput, calls=%fused_computation.99 | convolution fusion | flops 1073741824 | bytes 9961472 | tf_op jit(solution)/shard_map/dot_general | solution.py:216
  25.0 3.6 %collective-permute-start.7 = (bf16[4,128,128]{2,1,0:T(8,128)(2,1)S(1)}, bf16[4,128,128]{2,1,0:T(8,128)(2,1)S(1)}, u32[]{:S(2)}, u32[]{:S(2)}) collective-permute-start(bf16[4,128,128]{2,1,0:T(8,128)(2,1)S(1)} %bitcast.68), channel_id=1, source_target_pairs={{0,32},{32,0},{64,96},{96,64},{128,160},{160,128},{192,224},{224,1... | collective-permute-start | bytes 393224 | tf_op jit(solution)/shard_map/ppermute | solution.py:30
  29.7 7.0 %collective-permute-start.8 = (bf16[128,128]{1,0:T(8,128)(2,1)S(1)}, bf16[128,128]{1,0:T(8,128)(2,1)S(1)}, u32[]{:S(2)}, u32[]{:S(2)}) collective-permute-start(bf16[128,128]{1,0:T(8,128)(2,1)S(1)} %get-tuple-element.39), channel_id=1, source_target_pairs={{0,128},{32,160},{64,192},{96,224},{128,0},{160,32},{192,64},{224,... | collective-permute-start | bytes 98312 | tf_op jit(solution)/shard_map/ppermute | solution.py:26
  36.7 1.2 %collective-permute-start.10 = (bf16[128,128]{1,0:T(8,128)(2,1)S(1)}, bf16[128,128]{1,0:T(8,128)(2,1)S(1)}, u32[]{:S(2)}, u32[]{:S(2)}) collective-permute-start(bf16[128,128]{1,0:T(8,128)(2,1)S(1)} %get-tuple-element.37), channel_id=1, source_target_pairs={{0,64},{32,96},{64,0},{96,32},{128,192},{160,224},{192,128},{224,1... | collective-permute-start | bytes 98312 | tf_op jit(solution)/shard_map/ppermute | solution.py:26
  38.0 3.6 %collective-permute-done.9.in2 = bf16[128,128]{1,0:T(8,128)(2,1)S(1)} collective-permute-done((bf16[128,128]{1,0:T(8,128)(2,1)S(1)}, bf16[128,128]{1,0:T(8,128)(2,1)S(1)}, u32[]{:S(2)}, u32[]{:S(2)}) %collective-permute-start.9) | collective-permute-done | bytes 32800 | tf_op jit(solution)/shard_map/ppermute | solution.py:26
  41.6 1.5 %middle.1 = (bf16[128,512]{1,0:T(8,128)(2,1)}, bf16[4,272,128]{2,1,0:T(8,128)(2,1)S(1)}, f32[144,128]{1,0:T(8,128)S(1)}) custom-call(s32[2]{0:T(128)S(1)} %pad_add_fusion.place, f32[128,128]{1,0:T(8,128)S(1)} %slice_bitcast_fusion.3.own, bf16[128,128]{1,0:T(8,128)(2,1)S(1)} %collective-permute-done.8.in1, bf16[128,128]{1,0:T(8,128)(2,1)S(1)} %collective-permute-done.9.in2, ...), custom_call_target="tpu_custom_call" | custom-call | flops 83886080 | bytes 655360 | tf_op jit(solution)/shard_map/middle/pallas_call | solution.py:125
  43.1 2.7 %collective-permute-start.13 = (bf16[272,128]{1,0:T(8,128)(2,1)S(1)}, bf16[272,128]{1,0:T(8,128)(2,1)S(1)}, u32[]{:S(2)}, u32[]{:S(2)}) collective-permute-start(bf16[272,128]{1,0:T(8,128)(2,1)S(1)} %get-tuple-element.30), channel_id=1, source_target_pairs={{0,192},{32,224},{64,128},{96,160},{128,64},{160,96},{192,0},{224,... | collective-permute-start | bytes 208904 | tf_op jit(solution)/shard_map/ppermute | solution.py:26
  45.8 2.0 %collective-permute-start.12 = (bf16[272,128]{1,0:T(8,128)(2,1)S(1)}, bf16[272,128]{1,0:T(8,128)(2,1)S(1)}, u32[]{:S(2)}, u32[]{:S(2)}) collective-permute-start(bf16[272,128]{1,0:T(8,128)(2,1)S(1)} %get-tuple-element.31), channel_id=1, source_target_pairs={{0,128},{32,160},{64,192},{96,224},{128,0},{160,32},{192,64},{224,... | collective-permute-start | bytes 208904 | tf_op jit(solution)/shard_map/ppermute | solution.py:26
  48.8 4.8 %collective-permute-done.12 = bf16[272,128]{1,0:T(8,128)(2,1)S(1)} collective-permute-done((bf16[272,128]{1,0:T(8,128)(2,1)S(1)}, bf16[272,128]{1,0:T(8,128)(2,1)S(1)}, u32[]{:S(2)}, u32[]{:S(2)}) %collective-permute-start.12) | collective-permute-done | bytes 69664 | tf_op jit(solution)/shard_map/ppermute | solution.py:26
  53.8 3.9 %collective-permute-start.14 = (bf16[672,128]{1,0:T(8,128)(2,1)S(1)}, bf16[672,128]{1,0:T(8,128)(2,1)S(1)}, u32[]{:S(2)}, u32[]{:S(2)}) collective-permute-start(bf16[672,128]{1,0:T(8,128)(2,1)S(1)} %constant_dynamic-update-slice_fusion), channel_id=1, source_target_pairs={{0,32},{32,0},{64,96},{96,64},{128,160},{160,128},{192,224},{224,1... | collective-permute-start | bytes 516104 | tf_op jit(solution)/shard_map/ppermute | solution.py:30
  59.0 2.4 %fusion.18 = (bf16[4096,128]{1,0:T(8,128)(2,1)S(1)}, f32[4096,128]{1,0:T(8,128)S(1)}) fusion(bf16[1024,4096]{1,0:T(8,128)(2,1)S(1)} %spread.1, bf16[1024,128]{1,0:T(8,128)(2,1)S(1)} %slice_dynamic-update-slice_fusion), kind=kOutput, calls=%fused_computation.98 | convolution fusion | flops 1074266112 | bytes 11796480 | tf_op jit(solution)/shard_map/dot_general | solution.py:233
  61.9 1.5 %collective-permute-start.18 = (bf16[1104,128]{1,0:T(8,128)(2,1)S(1)}, bf16[1104,128]{1,0:T(8,128)(2,1)S(1)}, u32[]{:S(2)}, u32[]{:S(2)}) collective-permute-start(bf16[1104,128]{1,0:T(8,128)(2,1)S(1)} %get-tuple-element.53), channel_id=1, source_target_pairs={{0,16},{1,17},{2,18},{3,19},{4,20},{5,21},{6,22},{7,23},{8,24},{9,... | collective-permute-start | bytes 847880 | tf_op jit(solution)/shard_map/ppermute | solution.py:22
  63.4 1.1 %collective-permute-start.17 = (bf16[1104,128]{1,0:T(8,128)(2,1)S(1)}, bf16[1104,128]{1,0:T(8,128)(2,1)S(1)}, u32[]{:S(2)}, u32[]{:S(2)}) collective-permute-start(bf16[1104,128]{1,0:T(8,128)(2,1)S(1)} %get-tuple-element.52), channel_id=1, source_target_pairs={{0,24},{1,25},{2,26},{3,27},{4,28},{5,29},{6,30},{7,31},{8,16},{9,... | collective-permute-start | bytes 847880 | tf_op jit(solution)/shard_map/ppermute | solution.py:22
  65.0 4.3 %collective-permute-done.18 = bf16[1104,128]{1,0:T(8,128)(2,1)S(1)} collective-permute-done((bf16[1104,128]{1,0:T(8,128)(2,1)S(1)}, bf16[1104,128]{1,0:T(8,128)(2,1)S(1)}, u32[]{:S(2)}, u32[]{:S(2)}) %collective-permute-start.18) | collective-permute-done | bytes 282656 | tf_op jit(solution)/shard_map/ppermute | solution.py:22
  69.3 3.0 %collective-permute-done.17 = bf16[1104,128]{1,0:T(8,128)(2,1)S(1)} collective-permute-done((bf16[1104,128]{1,0:T(8,128)(2,1)S(1)}, bf16[1104,128]{1,0:T(8,128)(2,1)S(1)}, u32[]{:S(2)}, u32[]{:S(2)}) %collective-permute-start.17) | collective-permute-done | bytes 282656 | tf_op jit(solution)/shard_map/ppermute | solution.py:22
  72.6 2.4 %collective-permute-start.21 = (bf16[336,128]{1,0:T(8,128)(2,1)S(1)}, bf16[336,128]{1,0:T(8,128)(2,1)S(1)}, u32[]{:S(2)}, u32[]{:S(2)}) collective-permute-start(bf16[336,128]{1,0:T(8,128)(2,1)S(1)} %get-tuple-element.50), channel_id=1, source_target_pairs={{0,4},{1,5},{2,6},{3,7},{4,0},{5,1},{6,2},{7,3},{8,12},{9,13},{10,... | collective-permute-start | bytes 258056 | tf_op jit(solution)/shard_map/ppermute | solution.py:22
  75.0 1.2 %collective-permute-start.20 = (bf16[336,128]{1,0:T(8,128)(2,1)S(1)}, bf16[336,128]{1,0:T(8,128)(2,1)S(1)}, u32[]{:S(2)}, u32[]{:S(2)}) collective-permute-start(bf16[336,128]{1,0:T(8,128)(2,1)S(1)} %get-tuple-element.49), channel_id=1, source_target_pairs={{0,6},{1,7},{2,4},{3,5},{4,2},{5,3},{6,0},{7,1},{8,14},{9,15},{10,... | collective-permute-start | bytes 258056 | tf_op jit(solution)/shard_map/ppermute | solution.py:22
  76.2 1.3 %collective-permute-done.21 = bf16[336,128]{1,0:T(8,128)(2,1)S(1)} collective-permute-done((bf16[336,128]{1,0:T(8,128)(2,1)S(1)}, bf16[336,128]{1,0:T(8,128)(2,1)S(1)}, u32[]{:S(2)}, u32[]{:S(2)}) %collective-permute-start.21) | collective-permute-done | bytes 86048 | tf_op jit(solution)/shard_map/ppermute | solution.py:22
  77.5 2.3 %collective-permute-done.20 = bf16[336,128]{1,0:T(8,128)(2,1)S(1)} collective-permute-done((bf16[336,128]{1,0:T(8,128)(2,1)S(1)}, bf16[336,128]{1,0:T(8,128)(2,1)S(1)}, u32[]{:S(2)}, u32[]{:S(2)}) %collective-permute-start.20) | collective-permute-done | bytes 86048 | tf_op jit(solution)/shard_map/ppermute | solution.py:22
  79.8 1.6 %collective-permute-start.23 = (bf16[64,128]{1,0:T(8,128)(2,1)S(1)}, bf16[64,128]{1,0:T(8,128)(2,1)S(1)}, u32[]{:S(2)}, u32[]{:S(2)}) collective-permute-start(bf16[64,128]{1,0:T(8,128)(2,1)S(1)} %get-tuple-element.19), channel_id=1, source_target_pairs={{0,64},{32,96},{64,0},{96,32},{128,192},{160,224},{192,128},{224,1... | collective-permute-start | bytes 49160 | tf_op jit(solution)/shard_map/ppermute | solution.py:26
  81.5 3.1 %collective-permute-start.24 = (bf16[64,128]{1,0:T(8,128)(2,1)S(1)}, bf16[64,128]{1,0:T(8,128)(2,1)S(1)}, u32[]{:S(2)}, u32[]{:S(2)}) collective-permute-start(bf16[64,128]{1,0:T(8,128)(2,1)S(1)} %get-tuple-element.19), channel_id=1, source_target_pairs={{0,128},{32,160},{64,192},{96,224},{128,0},{160,32},{192,64},{224,... | collective-permute-start | bytes 49160 | tf_op jit(solution)/shard_map/ppermute | solution.py:26
  85.6 1.1 %collective-permute-start.22 = (bf16[128,128]{1,0:T(8,128)(2,1)S(1)}, bf16[128,128]{1,0:T(8,128)(2,1)S(1)}, u32[]{:S(2)}, u32[]{:S(2)}) collective-permute-start(bf16[128,128]{1,0:T(8,128)(2,1)S(1)} %slice.295), channel_id=1, source_target_pairs={{0,1},{1,0},{2,3},{3,2},{4,5},{5,4},{6,7},{7,6},{8,9},{9,8},{10,11... | collective-permute-start | bytes 98312 | tf_op jit(solution)/shard_map/ppermute | solution.py:34
  86.7 1.4 %collective-permute-done.24.two = bf16[64,128]{1,0:T(8,128)(2,1)S(1)} collective-permute-done((bf16[64,128]{1,0:T(8,128)(2,1)S(1)}, bf16[64,128]{1,0:T(8,128)(2,1)S(1)}, u32[]{:S(2)}, u32[]{:S(2)}) %collective-permute-start.24) | collective-permute-done | bytes 16416 | tf_op jit(solution)/shard_map/ppermute | solution.py:26
  88.2 1.1 %collective-permute-done.25.three = bf16[64,128]{1,0:T(8,128)(2,1)S(1)} collective-permute-done((bf16[64,128]{1,0:T(8,128)(2,1)S(1)}, bf16[64,128]{1,0:T(8,128)(2,1)S(1)}, u32[]{:S(2)}, u32[]{:S(2)}) %collective-permute-start.25) | collective-permute-done | bytes 16416 | tf_op jit(solution)/shard_map/ppermute | solution.py:26
  89.3 3.6 %collective-permute-start.26 = (bf16[272,128]{1,0:T(8,128)(2,1)S(1)}, bf16[272,128]{1,0:T(8,128)(2,1)S(1)}, u32[]{:S(2)}, u32[]{:S(2)}) collective-permute-start(bf16[272,128]{1,0:T(8,128)(2,1)S(1)} %get-tuple-element.14), channel_id=1, source_target_pairs={{0,32},{32,0},{64,96},{96,64},{128,160},{160,128},{192,224},{224,1... | collective-permute-start | bytes 208904 | tf_op jit(solution)/shard_map/ppermute | solution.py:30
  93.8 1.3 %settle.1 = (f32[128,512]{1,0:T(8,128)}, f32[1,512]{1,0:T(1,128)}) custom-call(s32[2]{0:T(128)S(1)} %pad_add_fusion.place, bf16[80,128]{1,0:T(8,128)(2,1)S(1)} %pad_maximum_fusion.9.own, bf16[64,128]{1,0:T(8,128)(2,1)S(1)} %collective-permute-done.23.one, bf16[64,128]{1,0:T(8,128)(2,1)S(1)} %collective-permute-done.24.two, ...), custom_call_target="tpu_custom_call" | custom-call | tf_op jit(solution)/shard_map/settle/pallas_call | solution.py:163
  (78 shorter events, 13.0 us)
Async XLA Ops:
  0.6 4.1 %collective-permute-start = (bf16[128,128]{1,0:T(8,128)(2,1)}, bf16[128,128]{1,0:T(8,128)(2,1)S(1)}, u32[]{:S(2)}, u32[]{:S(2)}) collective-permute-start(bf16[128,128]{1,0:T(8,128)(2,1)} %v_ref.1), channel_id=1, source_target_pairs={{0,1},{1,0},{2,3},{3,2},{4,5},{5,4},{6,7},{7,6},{8,9},{9,8},{10,11... | collective-permute-start | bytes 98312 | tf_op jit(solution)/shard_map/ppermute | solution.py:34
  3.2 0.8 copy-start.3
  4.7 4.7 %collective-permute-start.3 = (bf16[2,128,128]{2,1,0:T(8,128)(2,1)S(1)}, bf16[2,128,128]{2,1,0:T(8,128)(2,1)S(1)}, u32[]{:S(2)}, u32[]{:S(2)}) collective-permute-start(bf16[2,128,128]{2,1,0:T(8,128)(2,1)S(1)} %get-tuple-element.47), channel_id=1, source_target_pairs={{0,4},{1,5},{2,6},{3,7},{4,0},{5,1},{6,2},{7,3},{8,12},{9,13},{10,... | collective-permute-start | bytes 196616 | tf_op jit(solution)/shard_map/ppermute | solution.py:22
  7.5 4.3 %collective-permute-start.2 = (bf16[2,128,128]{2,1,0:T(8,128)(2,1)S(1)}, bf16[2,128,128]{2,1,0:T(8,128)(2,1)S(1)}, u32[]{:S(2)}, u32[]{:S(2)}) collective-permute-start(bf16[2,128,128]{2,1,0:T(8,128)(2,1)S(1)} %get-tuple-element.47), channel_id=1, source_target_pairs={{0,6},{1,7},{2,4},{3,5},{4,2},{5,3},{6,0},{7,1},{8,14},{9,15},{10,... | collective-permute-start | bytes 196616 | tf_op jit(solution)/shard_map/ppermute | solution.py:22
  8.4 3.5 %collective-permute-start.1 = (bf16[2,128,128]{2,1,0:T(8,128)(2,1)S(1)}, bf16[2,128,128]{2,1,0:T(8,128)(2,1)S(1)}, u32[]{:S(2)}, u32[]{:S(2)}) collective-permute-start(bf16[2,128,128]{2,1,0:T(8,128)(2,1)S(1)} %get-tuple-element.47), channel_id=1, source_target_pairs={{0,2},{1,3},{2,0},{3,1},{4,6},{5,7},{6,4},{7,5},{8,10},{9,11},{10,... | collective-permute-start | bytes 196616 | tf_op jit(solution)/shard_map/ppermute | solution.py:22
  11.9 9.6 %collective-permute-start.6 = (bf16[4,2,128,128]{3,2,1,0:T(8,128)(2,1)S(1)}, bf16[4,2,128,128]{3,2,1,0:T(8,128)(2,1)S(1)}, u32[]{:S(2)}, u32[]{:S(2)}) collective-permute-start(bf16[4,2,128,128]{3,2,1,0:T(8,128)(2,1)S(1)} %get-tuple-element.36), channel_id=1, source_target_pairs={{0,16},{1,17},{2,18},{3,19},{4,20},{5,21},{6,22},{7,23},{8,24},{9,... | collective-permute-start | bytes 786440 | tf_op jit(solution)/shard_map/ppermute | solution.py:22
  14.9 6.9 %collective-permute-start.5 = (bf16[4,2,128,128]{3,2,1,0:T(8,128)(2,1)S(1)}, bf16[4,2,128,128]{3,2,1,0:T(8,128)(2,1)S(1)}, u32[]{:S(2)}, u32[]{:S(2)}) collective-permute-start(bf16[4,2,128,128]{3,2,1,0:T(8,128)(2,1)S(1)} %get-tuple-element.36), channel_id=1, source_target_pairs={{0,24},{1,25},{2,26},{3,27},{4,28},{5,29},{6,30},{7,31},{8,16},{9,... | collective-permute-start | bytes 786440 | tf_op jit(solution)/shard_map/ppermute | solution.py:22
  15.7 6.8 %collective-permute-start.4 = (bf16[4,2,128,128]{3,2,1,0:T(8,128)(2,1)S(1)}, bf16[4,2,128,128]{3,2,1,0:T(8,128)(2,1)S(1)}, u32[]{:S(2)}, u32[]{:S(2)}) collective-permute-start(bf16[4,2,128,128]{3,2,1,0:T(8,128)(2,1)S(1)} %get-tuple-element.36), channel_id=1, source_target_pairs={{0,8},{1,9},{2,10},{3,11},{4,12},{5,13},{6,14},{7,15},{8,0},{9,1},... | collective-permute-start | bytes 786440 | tf_op jit(solution)/shard_map/ppermute | solution.py:22
  17.1 2.2 %copy-start = (bf16[1,1,128,128,128]{4,3,2,1,0:T(8,128)(2,1)S(1)}, bf16[1,1,128,128,128]{4,3,2,1,0:T(8,128)(2,1)}, u32[]{:S(2)}) copy-start(bf16[1,1,128,128,128]{4,3,2,1,0:T(8,128)(2,1)} %param.10) | copy-start | bytes 12582916
  21.5 20.1 %copy-start.1 = (bf16[128,512]{1,0:T(8,128)(2,1)S(1)}, bf16[128,512]{1,0:T(8,128)(2,1)}, u32[]{:S(2)}) copy-start(bf16[128,512]{1,0:T(8,128)(2,1)} %weight.1) | copy-start | bytes 393220
  21.5 20.1 %copy-start.2 = (bf16[128,512]{1,0:T(8,128)(2,1)S(1)}, bf16[128,512]{1,0:T(8,128)(2,1)}, u32[]{:S(2)}) copy-start(bf16[128,512]{1,0:T(8,128)(2,1)} %cot.1) | copy-start | bytes 393220
  21.5 20.0 %copy-start.4 = (f32[512]{0:T(512)S(1)}, f32[512]{0:T(512)}, u32[]{:S(2)}) copy-start(f32[512]{0:T(512)} %param.9) | copy-start | bytes 6148
  25.0 4.6 %collective-permute-start.7 = (bf16[4,128,128]{2,1,0:T(8,128)(2,1)S(1)}, bf16[4,128,128]{2,1,0:T(8,128)(2,1)S(1)}, u32[]{:S(2)}, u32[]{:S(2)}) collective-permute-start(bf16[4,128,128]{2,1,0:T(8,128)(2,1)S(1)} %bitcast.68), channel_id=1, source_target_pairs={{0,32},{32,0},{64,96},{96,64},{128,160},{160,128},{192,224},{224,1... | collective-permute-start | bytes 393224 | tf_op jit(solution)/shard_map/ppermute | solution.py:30
  29.7 8.3 %collective-permute-start.8 = (bf16[128,128]{1,0:T(8,128)(2,1)S(1)}, bf16[128,128]{1,0:T(8,128)(2,1)S(1)}, u32[]{:S(2)}, u32[]{:S(2)}) collective-permute-start(bf16[128,128]{1,0:T(8,128)(2,1)S(1)} %get-tuple-element.39), channel_id=1, source_target_pairs={{0,128},{32,160},{64,192},{96,224},{128,0},{160,32},{192,64},{224,... | collective-permute-start | bytes 98312 | tf_op jit(solution)/shard_map/ppermute | solution.py:26
  36.7 4.9 %collective-permute-start.9 = (bf16[128,128]{1,0:T(8,128)(2,1)S(1)}, bf16[128,128]{1,0:T(8,128)(2,1)S(1)}, u32[]{:S(2)}, u32[]{:S(2)}) collective-permute-start(bf16[128,128]{1,0:T(8,128)(2,1)S(1)} %get-tuple-element.38), channel_id=1, source_target_pairs={{0,192},{32,224},{64,128},{96,160},{128,64},{160,96},{192,0},{224,... | collective-permute-start | bytes 98312 | tf_op jit(solution)/shard_map/ppermute | solution.py:26
  36.7 4.9 %collective-permute-start.10 = (bf16[128,128]{1,0:T(8,128)(2,1)S(1)}, bf16[128,128]{1,0:T(8,128)(2,1)S(1)}, u32[]{:S(2)}, u32[]{:S(2)}) collective-permute-start(bf16[128,128]{1,0:T(8,128)(2,1)S(1)} %get-tuple-element.37), channel_id=1, source_target_pairs={{0,64},{32,96},{64,0},{96,32},{128,192},{160,224},{192,128},{224,1... | collective-permute-start | bytes 98312 | tf_op jit(solution)/shard_map/ppermute | solution.py:26
  43.1 5.8 %collective-permute-start.13 = (bf16[272,128]{1,0:T(8,128)(2,1)S(1)}, bf16[272,128]{1,0:T(8,128)(2,1)S(1)}, u32[]{:S(2)}, u32[]{:S(2)}) collective-permute-start(bf16[272,128]{1,0:T(8,128)(2,1)S(1)} %get-tuple-element.30), channel_id=1, source_target_pairs={{0,192},{32,224},{64,128},{96,160},{128,64},{160,96},{192,0},{224,... | collective-permute-start | bytes 208904 | tf_op jit(solution)/shard_map/ppermute | solution.py:26
  45.8 7.8 %collective-permute-start.12 = (bf16[272,128]{1,0:T(8,128)(2,1)S(1)}, bf16[272,128]{1,0:T(8,128)(2,1)S(1)}, u32[]{:S(2)}, u32[]{:S(2)}) collective-permute-start(bf16[272,128]{1,0:T(8,128)(2,1)S(1)} %get-tuple-element.31), channel_id=1, source_target_pairs={{0,128},{32,160},{64,192},{96,224},{128,0},{160,32},{192,64},{224,... | collective-permute-start | bytes 208904 | tf_op jit(solution)/shard_map/ppermute | solution.py:26
  47.8 5.9 %collective-permute-start.11 = (bf16[272,128]{1,0:T(8,128)(2,1)S(1)}, bf16[272,128]{1,0:T(8,128)(2,1)S(1)}, u32[]{:S(2)}, u32[]{:S(2)}) collective-permute-start(bf16[272,128]{1,0:T(8,128)(2,1)S(1)} %get-tuple-element.29), channel_id=1, source_target_pairs={{0,64},{32,96},{64,0},{96,32},{128,192},{160,224},{192,128},{224,1... | collective-permute-start | bytes 208904 | tf_op jit(solution)/shard_map/ppermute | solution.py:26
  53.8 4.9 %collective-permute-start.14 = (bf16[672,128]{1,0:T(8,128)(2,1)S(1)}, bf16[672,128]{1,0:T(8,128)(2,1)S(1)}, u32[]{:S(2)}, u32[]{:S(2)}) collective-permute-start(bf16[672,128]{1,0:T(8,128)(2,1)S(1)} %constant_dynamic-update-slice_fusion), channel_id=1, source_target_pairs={{0,32},{32,0},{64,96},{96,64},{128,160},{160,128},{192,224},{224,1... | collective-permute-start | bytes 516104 | tf_op jit(solution)/shard_map/ppermute | solution.py:30
  58.7 3.1 %collective-permute-start.15 = (f32[80,128]{1,0:T(8,128)S(1)}, f32[80,128]{1,0:T(8,128)S(1)}, u32[]{:S(2)}, u32[]{:S(2)}) collective-permute-start(f32[80,128]{1,0:T(8,128)S(1)} %maximum_add_fusion), channel_id=1, source_target_pairs={{0,1},{1,0},{2,3},{3,2},{4,5},{5,4},{6,7},{7,6},{8,9},{9,8},{10,11... | collective-permute-start | bytes 122888 | tf_op jit(solution)/shard_map/ppermute | solution.py:34
  61.9 7.4 %collective-permute-start.18 = (bf16[1104,128]{1,0:T(8,128)(2,1)S(1)}, bf16[1104,128]{1,0:T(8,128)(2,1)S(1)}, u32[]{:S(2)}, u32[]{:S(2)}) collective-permute-start(bf16[1104,128]{1,0:T(8,128)(2,1)S(1)} %get-tuple-element.53), channel_id=1, source_target_pairs={{0,16},{1,17},{2,18},{3,19},{4,20},{5,21},{6,22},{7,23},{8,24},{9,... | collective-permute-start | bytes 847880 | tf_op jit(solution)/shard_map/ppermute | solution.py:22
  63.4 8.8 %collective-permute-start.17 = (bf16[1104,128]{1,0:T(8,128)(2,1)S(1)}, bf16[1104,128]{1,0:T(8,128)(2,1)S(1)}, u32[]{:S(2)}, u32[]{:S(2)}) collective-permute-start(bf16[1104,128]{1,0:T(8,128)(2,1)S(1)} %get-tuple-element.52), channel_id=1, source_target_pairs={{0,24},{1,25},{2,26},{3,27},{4,28},{5,29},{6,30},{7,31},{8,16},{9,... | collective-permute-start | bytes 847880 | tf_op jit(solution)/shard_map/ppermute | solution.py:22
  64.5 7.8 %collective-permute-start.16 = (bf16[1104,128]{1,0:T(8,128)(2,1)S(1)}, bf16[1104,128]{1,0:T(8,128)(2,1)S(1)}, u32[]{:S(2)}, u32[]{:S(2)}) collective-permute-start(bf16[1104,128]{1,0:T(8,128)(2,1)S(1)} %get-tuple-element.51), channel_id=1, source_target_pairs={{0,8},{1,9},{2,10},{3,11},{4,12},{5,13},{6,14},{7,15},{8,0},{9,1},... | collective-permute-start | bytes 847880 | tf_op jit(solution)/shard_map/ppermute | solution.py:22
  72.6 4.9 %collective-permute-start.21 = (bf16[336,128]{1,0:T(8,128)(2,1)S(1)}, bf16[336,128]{1,0:T(8,128)(2,1)S(1)}, u32[]{:S(2)}, u32[]{:S(2)}) collective-permute-start(bf16[336,128]{1,0:T(8,128)(2,1)S(1)} %get-tuple-element.50), channel_id=1, source_target_pairs={{0,4},{1,5},{2,6},{3,7},{4,0},{5,1},{6,2},{7,3},{8,12},{9,13},{10,... | collective-permute-start | bytes 258056 | tf_op jit(solution)/shard_map/ppermute | solution.py:22
  75.0 4.8 %collective-permute-start.20 = (bf16[336,128]{1,0:T(8,128)(2,1)S(1)}, bf16[336,128]{1,0:T(8,128)(2,1)S(1)}, u32[]{:S(2)}, u32[]{:S(2)}) collective-permute-start(bf16[336,128]{1,0:T(8,128)(2,1)S(1)} %get-tuple-element.49), channel_id=1, source_target_pairs={{0,6},{1,7},{2,4},{3,5},{4,2},{5,3},{6,0},{7,1},{8,14},{9,15},{10,... | collective-permute-start | bytes 258056 | tf_op jit(solution)/shard_map/ppermute | solution.py:22
  76.2 3.6 %collective-permute-start.19 = (bf16[336,128]{1,0:T(8,128)(2,1)S(1)}, bf16[336,128]{1,0:T(8,128)(2,1)S(1)}, u32[]{:S(2)}, u32[]{:S(2)}) collective-permute-start(bf16[336,128]{1,0:T(8,128)(2,1)S(1)} %get-tuple-element.48), channel_id=1, source_target_pairs={{0,2},{1,3},{2,0},{3,1},{4,6},{5,7},{6,4},{7,5},{8,10},{9,11},{10,... | collective-permute-start | bytes 258056 | tf_op jit(solution)/shard_map/ppermute | solution.py:22
  79.8 6.9 %collective-permute-start.23 = (bf16[64,128]{1,0:T(8,128)(2,1)S(1)}, bf16[64,128]{1,0:T(8,128)(2,1)S(1)}, u32[]{:S(2)}, u32[]{:S(2)}) collective-permute-start(bf16[64,128]{1,0:T(8,128)(2,1)S(1)} %get-tuple-element.19), channel_id=1, source_target_pairs={{0,64},{32,96},{64,0},{96,32},{128,192},{160,224},{192,128},{224,1... | collective-permute-start | bytes 49160 | tf_op jit(solution)/shard_map/ppermute | solution.py:26
  81.5 6.7 %collective-permute-start.24 = (bf16[64,128]{1,0:T(8,128)(2,1)S(1)}, bf16[64,128]{1,0:T(8,128)(2,1)S(1)}, u32[]{:S(2)}, u32[]{:S(2)}) collective-permute-start(bf16[64,128]{1,0:T(8,128)(2,1)S(1)} %get-tuple-element.19), channel_id=1, source_target_pairs={{0,128},{32,160},{64,192},{96,224},{128,0},{160,32},{192,64},{224,... | collective-permute-start | bytes 49160 | tf_op jit(solution)/shard_map/ppermute | solution.py:26
  84.6 4.7 %collective-permute-start.25 = (bf16[64,128]{1,0:T(8,128)(2,1)S(1)}, bf16[64,128]{1,0:T(8,128)(2,1)S(1)}, u32[]{:S(2)}, u32[]{:S(2)}) collective-permute-start(bf16[64,128]{1,0:T(8,128)(2,1)S(1)} %get-tuple-element.19), channel_id=1, source_target_pairs={{0,192},{32,224},{64,128},{96,160},{128,64},{160,96},{192,0},{224,... | collective-permute-start | bytes 49160 | tf_op jit(solution)/shard_map/ppermute | solution.py:26
  85.6 7.3 %collective-permute-start.22 = (bf16[128,128]{1,0:T(8,128)(2,1)S(1)}, bf16[128,128]{1,0:T(8,128)(2,1)S(1)}, u32[]{:S(2)}, u32[]{:S(2)}) collective-permute-start(bf16[128,128]{1,0:T(8,128)(2,1)S(1)} %slice.295), channel_id=1, source_target_pairs={{0,1},{1,0},{2,3},{3,2},{4,5},{5,4},{6,7},{7,6},{8,9},{9,8},{10,11... | collective-permute-start | bytes 98312 | tf_op jit(solution)/shard_map/ppermute | solution.py:34
  89.3 4.5 %collective-permute-start.26 = (bf16[272,128]{1,0:T(8,128)(2,1)S(1)}, bf16[272,128]{1,0:T(8,128)(2,1)S(1)}, u32[]{:S(2)}, u32[]{:S(2)}) collective-permute-start(bf16[272,128]{1,0:T(8,128)(2,1)S(1)} %get-tuple-element.14), channel_id=1, source_target_pairs={{0,32},{32,0},{64,96},{96,64},{128,160},{160,128},{192,224},{224,1... | collective-permute-start | bytes 208904 | tf_op jit(solution)/shard_map/ppermute | solution.py:30
